TPU v7x, 32 devices: a whole 2x2x4 slice. The times are simulated.
32 devices in a mesh: gx: 4 (over z), gy: 4 (over y, x), gz: 2 (over core).
Axes of the slice: x: 2, y: 2, z: 4, core: 2. Of those that a mesh axis runs over, the one named last changes fastest.
Arguments:
- body_load: float32 [8, 16, 16, 192], P('gx', 'gy', 'gz'), may hold values from -6 to 6
- probe_load: float32 [8, 16, 16, 192], P('gx', 'gy', 'gz'), may hold values from -6 to 6
- density: float32 [8, 16, 16], P('gx', 'gy', 'gz'), may hold values from 0.3 to 1
- link_types: int32 [8, 16, 16, 7], P('gx', 'gy', 'gz'), may hold values from 0 to 4, as said below
- off_blocks: bfloat16 [4, 192, 192], replicated, may hold values from -0.4375 to 0.4375
- self_blocks: bfloat16 [4, 192, 192], replicated, as said below
- block_owner: int32 [8, 16, 16], P('gx', 'gy', 'gz'), may hold values from 0 to 255, as said below
Outputs:
- state_field: float32 [8, 16, 16, 192], P('gx', 'gy', 'gz')
- adjoint_field: float32 [8, 16, 16, 192], P('gx', 'gy', 'gz')
- coarse_sensitivity: float32 [256], P(('gx', 'gy', 'gz'))
Inputs may be any that keep to these rules, and one draw needn't show every extreme that they name: `link_types`: entries 0, 1, 2 of a group name the kind of its coupling to the next group along the first, second and third dimension (4: no coupling, always so on the grid's last layer); entry 3 + k equals entry k of the group one step lower along dimension k (4 on the first layer); entry 6 names the kind of the group's own block and is below 4. `block_owner`: every design block is named by exactly 8 node groups. `self_blocks`: each own block is symmetric and its diagonal entries exceed 3.8.
All inputs are finite; a program needn't handle non-finite values.
Results may differ from a plain program's by a relative error of at most 0.0012.
Values may be sent and summed in bfloat16 or wider, within the bound.
No kernel may reach another device: no remote copies, remote signals or barrier semaphores. Data moves between devices by JAX's collectives and lax.ppermute only.
A program may use at most 64 MiB of HBM per device.

v0:
```python
import jax
import jax.numpy as jnp
from jax import lax
from jax.sharding import PartitionSpec as P

ITERS = 4
GPB = 8


def with_halo(array, sides, width):
    for axis, dim in sides:
        peers, length = (lax.axis_size(axis), array.shape[dim])
        up = [(i, (i + 1) % peers) for i in range(peers - 1)]
        down = [(j, i) for i, j in up]
        last = lax.slice_in_dim(array, length - width, length, axis=dim)
        initial = lax.slice_in_dim(array, 0, width, axis=dim)
        before = lax.ppermute(last, axis, up)
        after = lax.ppermute(initial, axis, down)
        array = jnp.concatenate([before, array, after], axis=dim)
    return array


def level_masks(type_codes, level_count):
    levels = lax.broadcasted_iota(jnp.int32, type_codes.shape + (level_count,), 3)
    return (type_codes[..., None] == levels).astype(jnp.bfloat16)


def typed_product(window, selector, block_table):
    spread = window[:, :, :, :, None, :] * selector[None, :, :, :, :, None]
    flattened = spread.reshape(-1, block_table.shape[0])
    return jnp.dot(flattened, block_table, preferred_element_type=jnp.float32).reshape(window.shape)


def cut_window(padded, shift):
    span_x = padded.shape[1] - 2
    span_y = padded.shape[2] - 2
    span_z = padded.shape[3] - 2
    return padded[
        :,
        1 + shift[0] : 1 + shift[0] + span_x,
        1 + shift[1] : 1 + shift[1] + span_y,
        1 + shift[2] : 1 + shift[2] + span_z,
        :,
    ]


def local_image(padded, selectors, tables, stiff_scale):
    up_table, low_table, own_table = tables
    accumulated = typed_product(cut_window(padded, (0, 0, 0)), selectors[6], own_table)
    offsets = ((1, 0, 0), (0, 1, 0), (0, 0, 1))
    for k in range(3):
        upper = offsets[k]
        lower = (-upper[0], -upper[1], -upper[2])
        accumulated = accumulated + typed_product(cut_window(padded, upper), selectors[k], up_table)
        accumulated = accumulated + typed_product(
            cut_window(padded, lower), selectors[3 + k], low_table
        )
    return accumulated * stiff_scale[None, :, :, :, None]


def local(body_load, probe_load, density, link_types, off_blocks, self_blocks, block_owner):
    dof_count = body_load.shape[-1]
    type_count = off_blocks.shape[0]
    self_count = self_blocks.shape[0]
    stiff_scale = density**1.5
    selectors = [level_masks(link_types[..., j], type_count) for j in range(6)]
    selectors.append(level_masks(link_types[..., 6], self_count))
    up_table = jnp.swapaxes(off_blocks, 1, 2).reshape(type_count * dof_count, dof_count)
    low_table = off_blocks.reshape(type_count * dof_count, dof_count)
    own_table = self_blocks.reshape(self_count * dof_count, dof_count)
    tables = (up_table, low_table, own_table)
    diagonals = jnp.diagonal(self_blocks, axis1=1, axis2=2).astype(jnp.float32)
    pivots = jnp.zeros(body_load.shape, jnp.float32)
    for level in range(self_count):
        pivots = (
            pivots + selectors[6][..., level : level + 1].astype(jnp.float32) * diagonals[level]
        )
    targets = jnp.stack([body_load, probe_load])
    residual = targets
    solution = jnp.zeros_like(targets)
    for sweep in range(ITERS):
        precond = residual / pivots[None]
        shipped = (precond * stiff_scale[None, :, :, :, None]).astype(jnp.bfloat16)
        padded = with_halo(shipped, (("gx", 1), ("gy", 2), ("gz", 3)), 1)
        image_field = local_image(padded, selectors, tables, stiff_scale)
        projected = jnp.sum(residual * image_field, axis=(1, 2, 3, 4))
        energy = jnp.sum(image_field * image_field, axis=(1, 2, 3, 4))
        projected, energy = lax.psum((projected, energy), ("gx", "gy", "gz"))
        step_size = projected / (energy + 1e-06)
        solution = solution + step_size[:, None, None, None, None] * precond
        residual = residual - step_size[:, None, None, None, None] * image_field
    applied = targets - residual
    bracket = jnp.sum(solution[1] * applied[0] + solution[0] * applied[1], axis=-1)
    sensitivity = -1.5 * bracket / density
    weighted = density * sensitivity
    groups_here = density.shape[0] * density.shape[1] * density.shape[2]
    blocks_here = groups_here // GPB
    size_x = lax.axis_size("gx")
    size_y = lax.axis_size("gy")
    size_z = lax.axis_size("gz")
    block_total = blocks_here * size_x * size_y * size_z
    owners = block_owner.reshape(-1)
    numerator = jnp.zeros((block_total,), jnp.float32).at[owners].add(weighted.reshape(-1))
    denominator = jnp.zeros((block_total,), jnp.float32).at[owners].add(density.reshape(-1))
    numerator, denominator = (
        lax.psum_scatter(numerator, ("gx", "gy", "gz"), scatter_dimension=0, tiled=True),
        lax.psum_scatter(denominator, ("gx", "gy", "gz"), scatter_dimension=0, tiled=True),
    )
    return (solution[0], solution[1], numerator / denominator)


def solution(mesh):
    in_specs = (
        P("gx", "gy", "gz", None),
        P("gx", "gy", "gz", None),
        P("gx", "gy", "gz"),
        P("gx", "gy", "gz", None),
        P(),
        P(),
        P("gx", "gy", "gz"),
    )
    out_specs = (P("gx", "gy", "gz", None), P("gx", "gy", "gz", None), P(("gx", "gy", "gz")))
    return jax.shard_map(local, mesh=mesh, in_specs=in_specs, out_specs=out_specs, check_vma=False)
```

profile of v0, /device:TPU:0, one launch (start us, length us, event | category | flops | bytes accessed | tf_op | source)
XLA Modules:
  0.0 319.7 jit_solution(7538796491172008795)
XLA Ops:
  1.5 7.8 %copy.38 = bf16[4,192,192]{0,2,1:T(8,128)(2,1)} copy(bf16[4,192,192]{2,1,0:T(8,128)(2,1)} %param.12) | data formatting | bytes 589824 | tf_op args[5]
  9.3 5.3 %gather_fusion = bf16[192,4]{1,0:T(8,128)(2,1)S(1)} fusion(bf16[4,192,192]{0,2,1:T(8,128)(2,1)} %copy.38, s32[192]{0:T(256)S(1)} %bitcast.285), kind=kCustom, calls=%fused_computation | custom fusion | bytes 4608 | tf_op jit(solution)/shard_map/jit(diagonal)/gather | solution.py:72
  16.5 5.6 %collective-permute-start.1 = (bf16[2,1,4,8,192]{4,3,2,1,0:T(8,128)(2,1)S(1)}, bf16[2,1,4,8,192]{4,3,2,1,0:T(8,128)(2,1)S(1)}, u32[]{:S(2)}, u32[]{:S(2)}) collective-permute-start(bf16[2,1,4,8,192]{4,3,2,1,0:T(8,128)(2,1)S(1)} %get-tuple-element.82), channel_id=1, source_target_pairs={{0,8},{8,16},{16,24},{1,9},{9,17},{17,25},{2,10},{10,18},{18,26},{... | collective-permute-start | bytes 73736 | tf_op jit(solution)/shard_map/ppermute | solution.py:17
  22.2 1.5 collective-permute-done.1
  25.0 4.5 %collective-permute-start.3 = (bf16[2,4,1,8,192]{4,3,2,1,0:T(8,128)(2,1)S(1)}, bf16[2,4,1,8,192]{4,3,2,1,0:T(8,128)(2,1)S(1)}, u32[]{:S(2)}, u32[]{:S(2)}) collective-permute-start(bf16[2,4,1,8,192]{4,3,2,1,0:T(8,128)(2,1)S(1)} %get-tuple-element.62), channel_id=1, source_target_pairs={{0,2},{2,4},{4,6},{1,3},{3,5},{5,7},{8,10},{10,12},{12,14},{9,11},... | collective-permute-start | bytes 73736 | tf_op jit(solution)/shard_map/ppermute | solution.py:17
  31.2 1.3 collective-permute-start.4
  32.5 3.0 collective-permute-start.5
  37.9 43.2 %all-reduce.6 = (f32[2]{0:T(128)S(1)}, f32[2]{0:T(128)S(1)}) all-reduce(f32[2]{0:T(128)S(1)} %get-tuple-element.10, f32[2]{0:T(128)S(1)} %get-tuple-element.9), channel_id=1, replica_groups=mesh['gx'=4,'gy'=4,'gz'=2] {'gx','gy','gz'}, use_global_device_ids=true, to_apply=%region_1.2 | all-reduce | flops 4 | bytes 32 | tf_op jit(solution)/shard_map/psum | solution.py:88
  81.2 1.3 collective-permute-start.6
  82.5 4.5 %collective-permute-start.7 = (bf16[2,1,4,8,192]{4,3,2,1,0:T(8,128)(2,1)S(1)}, bf16[2,1,4,8,192]{4,3,2,1,0:T(8,128)(2,1)S(1)}, u32[]{:S(2)}, u32[]{:S(2)}) collective-permute-start(bf16[2,1,4,8,192]{4,3,2,1,0:T(8,128)(2,1)S(1)} %get-tuple-element.80), channel_id=1, source_target_pairs={{0,8},{8,16},{16,24},{1,9},{9,17},{17,25},{2,10},{10,18},{18,26},{... | collective-permute-start | bytes 73736 | tf_op jit(solution)/shard_map/ppermute | solution.py:17
  87.0 1.6 collective-permute-done.7
  89.9 4.8 %collective-permute-start.9 = (bf16[2,4,1,8,192]{4,3,2,1,0:T(8,128)(2,1)S(1)}, bf16[2,4,1,8,192]{4,3,2,1,0:T(8,128)(2,1)S(1)}, u32[]{:S(2)}, u32[]{:S(2)}) collective-permute-start(bf16[2,4,1,8,192]{4,3,2,1,0:T(8,128)(2,1)S(1)} %get-tuple-element.60), channel_id=1, source_target_pairs={{0,2},{2,4},{4,6},{1,3},{3,5},{5,7},{8,10},{10,12},{12,14},{9,11},... | collective-permute-start | bytes 73736 | tf_op jit(solution)/shard_map/ppermute | solution.py:17
  97.7 3.0 collective-permute-start.11
  103.0 43.2 %all-reduce.5 = (f32[2]{0:T(128)S(1)}, f32[2]{0:T(128)S(1)}) all-reduce(f32[2]{0:T(128)S(1)} %get-tuple-element.8, f32[2]{0:T(128)S(1)} %get-tuple-element.7), channel_id=1, replica_groups=mesh['gx'=4,'gy'=4,'gz'=2] {'gx','gy','gz'}, use_global_device_ids=true, to_apply=%region_5.6 | all-reduce | flops 4 | bytes 32 | tf_op jit(solution)/shard_map/psum | solution.py:88
  147.7 4.5 %collective-permute-start.13 = (bf16[2,1,4,8,192]{4,3,2,1,0:T(8,128)(2,1)S(1)}, bf16[2,1,4,8,192]{4,3,2,1,0:T(8,128)(2,1)S(1)}, u32[]{:S(2)}, u32[]{:S(2)}) collective-permute-start(bf16[2,1,4,8,192]{4,3,2,1,0:T(8,128)(2,1)S(1)} %get-tuple-element.78), channel_id=1, source_target_pairs={{0,8},{8,16},{16,24},{1,9},{9,17},{17,25},{2,10},{10,18},{18,26},{... | collective-permute-start | bytes 73736 | tf_op jit(solution)/shard_map/ppermute | solution.py:17
  152.3 1.5 collective-permute-done.13
  155.1 4.8 %collective-permute-start.15 = (bf16[2,4,1,8,192]{4,3,2,1,0:T(8,128)(2,1)S(1)}, bf16[2,4,1,8,192]{4,3,2,1,0:T(8,128)(2,1)S(1)}, u32[]{:S(2)}, u32[]{:S(2)}) collective-permute-start(bf16[2,4,1,8,192]{4,3,2,1,0:T(8,128)(2,1)S(1)} %get-tuple-element.58), channel_id=1, source_target_pairs={{0,2},{2,4},{4,6},{1,3},{3,5},{5,7},{8,10},{10,12},{12,14},{9,11},... | collective-permute-start | bytes 73736 | tf_op jit(solution)/shard_map/ppermute | solution.py:17
  162.9 3.0 collective-permute-start.17
  168.2 43.0 %all-reduce.4 = (f32[2]{0:T(128)S(1)}, f32[2]{0:T(128)S(1)}) all-reduce(f32[2]{0:T(128)S(1)} %get-tuple-element.6, f32[2]{0:T(128)S(1)} %get-tuple-element.5), channel_id=1, replica_groups=mesh['gx'=4,'gy'=4,'gz'=2] {'gx','gy','gz'}, use_global_device_ids=true, to_apply=%region_9.10 | all-reduce | flops 4 | bytes 32 | tf_op jit(solution)/shard_map/psum | solution.py:88
  212.6 4.5 %collective-permute-start.19 = (bf16[2,1,4,8,192]{4,3,2,1,0:T(8,128)(2,1)S(1)}, bf16[2,1,4,8,192]{4,3,2,1,0:T(8,128)(2,1)S(1)}, u32[]{:S(2)}, u32[]{:S(2)}) collective-permute-start(bf16[2,1,4,8,192]{4,3,2,1,0:T(8,128)(2,1)S(1)} %get-tuple-element.76), channel_id=1, source_target_pairs={{0,8},{8,16},{16,24},{1,9},{9,17},{17,25},{2,10},{10,18},{18,26},{... | collective-permute-start | bytes 73736 | tf_op jit(solution)/shard_map/ppermute | solution.py:17
  220.1 5.0 %collective-permute-start.21 = (bf16[2,4,1,8,192]{4,3,2,1,0:T(8,128)(2,1)S(1)}, bf16[2,4,1,8,192]{4,3,2,1,0:T(8,128)(2,1)S(1)}, u32[]{:S(2)}, u32[]{:S(2)}) collective-permute-start(bf16[2,4,1,8,192]{4,3,2,1,0:T(8,128)(2,1)S(1)} %get-tuple-element.56), channel_id=1, source_target_pairs={{0,2},{2,4},{4,6},{1,3},{3,5},{5,7},{8,10},{10,12},{12,14},{9,11},... | collective-permute-start | bytes 73736 | tf_op jit(solution)/shard_map/ppermute | solution.py:17
  227.9 3.0 collective-permute-start.23
  233.2 43.0 %all-reduce.3 = (f32[2]{0:T(128)S(1)}, f32[2]{0:T(128)S(1)}) all-reduce(f32[2]{0:T(128)S(1)} %get-tuple-element.4, f32[2]{0:T(128)S(1)} %get-tuple-element.3), channel_id=1, replica_groups=mesh['gx'=4,'gy'=4,'gz'=2] {'gx','gy','gz'}, use_global_device_ids=true, to_apply=%region_13.14 | all-reduce | flops 4 | bytes 32 | tf_op jit(solution)/shard_map/psum | solution.py:88
  278.1 41.0 %all-reduce.2 = (f32[256]{0:T(256)S(1)}, f32[256]{0:T(256)S(1)}) all-reduce(f32[256]{0:T(256)S(1)} %scatter_custom_fusion.1, f32[256]{0:T(256)S(1)} %scatter_custom_fusion), channel_id=3, replica_groups=mesh['gx'=4,'gy'=4,'gz'=2] {'gx','gy','gz'}, use_global_device_ids=true, to_apply=%region_20.21.clone | all-reduce | flops 512 | bytes 4096
  (123 shorter events, 34.2 us)
Async XLA Ops:
  15.2 6.9 %collective-permute-start = (bf16[2,1,4,8,192]{4,3,2,1,0:T(8,128)(2,1)S(1)}, bf16[2,1,4,8,192]{4,3,2,1,0:T(8,128)(2,1)S(1)}, u32[]{:S(2)}, u32[]{:S(2)}) collective-permute-start(bf16[2,1,4,8,192]{4,3,2,1,0:T(8,128)(2,1)S(1)} %get-tuple-element.83), channel_id=1, source_target_pairs={{8,0},{16,8},{24,16},{9,1},{17,9},{25,17},{10,2},{18,10},{26,18},{... | collective-permute-start | bytes 73736 | tf_op jit(solution)/shard_map/ppermute | solution.py:18
  16.5 7.1 %collective-permute-start.1 = (bf16[2,1,4,8,192]{4,3,2,1,0:T(8,128)(2,1)S(1)}, bf16[2,1,4,8,192]{4,3,2,1,0:T(8,128)(2,1)S(1)}, u32[]{:S(2)}, u32[]{:S(2)}) collective-permute-start(bf16[2,1,4,8,192]{4,3,2,1,0:T(8,128)(2,1)S(1)} %get-tuple-element.82), channel_id=1, source_target_pairs={{0,8},{8,16},{16,24},{1,9},{9,17},{17,25},{2,10},{10,18},{18,26},{... | collective-permute-start | bytes 73736 | tf_op jit(solution)/shard_map/ppermute | solution.py:17
  23.7 6.2 %collective-permute-start.2 = (bf16[2,4,1,8,192]{4,3,2,1,0:T(8,128)(2,1)S(1)}, bf16[2,4,1,8,192]{4,3,2,1,0:T(8,128)(2,1)S(1)}, u32[]{:S(2)}, u32[]{:S(2)}) collective-permute-start(bf16[2,4,1,8,192]{4,3,2,1,0:T(8,128)(2,1)S(1)} %get-tuple-element.63), channel_id=1, source_target_pairs={{2,0},{4,2},{6,4},{3,1},{5,3},{7,5},{10,8},{12,10},{14,12},{11,9},... | collective-permute-start | bytes 73736 | tf_op jit(solution)/shard_map/ppermute | solution.py:18
  25.0 6.1 %collective-permute-start.3 = (bf16[2,4,1,8,192]{4,3,2,1,0:T(8,128)(2,1)S(1)}, bf16[2,4,1,8,192]{4,3,2,1,0:T(8,128)(2,1)S(1)}, u32[]{:S(2)}, u32[]{:S(2)}) collective-permute-start(bf16[2,4,1,8,192]{4,3,2,1,0:T(8,128)(2,1)S(1)} %get-tuple-element.62), channel_id=1, source_target_pairs={{0,2},{2,4},{4,6},{1,3},{3,5},{5,7},{8,10},{10,12},{12,14},{9,11},... | collective-permute-start | bytes 73736 | tf_op jit(solution)/shard_map/ppermute | solution.py:17
  31.2 5.1 %collective-permute-start.4 = (bf16[2,4,6,1,192]{4,3,2,1,0:T(2,128)(2,1)S(1)}, bf16[2,4,6,1,192]{4,3,2,1,0:T(2,128)(2,1)S(1)}, u32[]{:S(2)}, u32[]{:S(2)}) collective-permute-start(bf16[2,4,6,1,192]{4,3,2,1,0:T(2,128)(2,1)S(1)} %get-tuple-element.50), channel_id=1, source_target_pairs={{1,0},{3,2},{5,4},{7,6},{9,8},{11,10},{13,12},{15,14},{17,16},{19,... | collective-permute-start | bytes 55304 | tf_op jit(solution)/shard_map/ppermute | solution.py:18
  32.5 3.9 %collective-permute-start.5 = (bf16[2,4,6,1,192]{4,3,2,1,0:T(2,128)(2,1)S(1)}, bf16[2,4,6,1,192]{4,3,2,1,0:T(2,128)(2,1)S(1)}, u32[]{:S(2)}, u32[]{:S(2)}) collective-permute-start(bf16[2,4,6,1,192]{4,3,2,1,0:T(2,128)(2,1)S(1)} %get-tuple-element.51), channel_id=1, source_target_pairs={{0,1},{2,3},{4,5},{6,7},{8,9},{10,11},{12,13},{14,15},{16,17},{18,... | collective-permute-start | bytes 55304 | tf_op jit(solution)/shard_map/ppermute | solution.py:17
  81.2 5.9 %collective-permute-start.6 = (bf16[2,1,4,8,192]{4,3,2,1,0:T(8,128)(2,1)S(1)}, bf16[2,1,4,8,192]{4,3,2,1,0:T(8,128)(2,1)S(1)}, u32[]{:S(2)}, u32[]{:S(2)}) collective-permute-start(bf16[2,1,4,8,192]{4,3,2,1,0:T(8,128)(2,1)S(1)} %get-tuple-element.81), channel_id=1, source_target_pairs={{8,0},{16,8},{24,16},{9,1},{17,9},{25,17},{10,2},{18,10},{26,18},{... | collective-permute-start | bytes 73736 | tf_op jit(solution)/shard_map/ppermute | solution.py:18
  82.5 6.1 %collective-permute-start.7 = (bf16[2,1,4,8,192]{4,3,2,1,0:T(8,128)(2,1)S(1)}, bf16[2,1,4,8,192]{4,3,2,1,0:T(8,128)(2,1)S(1)}, u32[]{:S(2)}, u32[]{:S(2)}) collective-permute-start(bf16[2,1,4,8,192]{4,3,2,1,0:T(8,128)(2,1)S(1)} %get-tuple-element.80), channel_id=1, source_target_pairs={{0,8},{8,16},{16,24},{1,9},{9,17},{17,25},{2,10},{10,18},{18,26},{... | collective-permute-start | bytes 73736 | tf_op jit(solution)/shard_map/ppermute | solution.py:17
  88.6 6.5 %collective-permute-start.8 = (bf16[2,4,1,8,192]{4,3,2,1,0:T(8,128)(2,1)S(1)}, bf16[2,4,1,8,192]{4,3,2,1,0:T(8,128)(2,1)S(1)}, u32[]{:S(2)}, u32[]{:S(2)}) collective-permute-start(bf16[2,4,1,8,192]{4,3,2,1,0:T(8,128)(2,1)S(1)} %get-tuple-element.61), channel_id=1, source_target_pairs={{2,0},{4,2},{6,4},{3,1},{5,3},{7,5},{10,8},{12,10},{14,12},{11,9},... | collective-permute-start | bytes 73736 | tf_op jit(solution)/shard_map/ppermute | solution.py:18
  89.9 6.4 %collective-permute-start.9 = (bf16[2,4,1,8,192]{4,3,2,1,0:T(8,128)(2,1)S(1)}, bf16[2,4,1,8,192]{4,3,2,1,0:T(8,128)(2,1)S(1)}, u32[]{:S(2)}, u32[]{:S(2)}) collective-permute-start(bf16[2,4,1,8,192]{4,3,2,1,0:T(8,128)(2,1)S(1)} %get-tuple-element.60), channel_id=1, source_target_pairs={{0,2},{2,4},{4,6},{1,3},{3,5},{5,7},{8,10},{10,12},{12,14},{9,11},... | collective-permute-start | bytes 73736 | tf_op jit(solution)/shard_map/ppermute | solution.py:17
  96.4 5.1 %collective-permute-start.10 = (bf16[2,4,6,1,192]{4,3,2,1,0:T(2,128)(2,1)S(1)}, bf16[2,4,6,1,192]{4,3,2,1,0:T(2,128)(2,1)S(1)}, u32[]{:S(2)}, u32[]{:S(2)}) collective-permute-start(bf16[2,4,6,1,192]{4,3,2,1,0:T(2,128)(2,1)S(1)} %get-tuple-element.46), channel_id=1, source_target_pairs={{1,0},{3,2},{5,4},{7,6},{9,8},{11,10},{13,12},{15,14},{17,16},{19,... | collective-permute-start | bytes 55304 | tf_op jit(solution)/shard_map/ppermute | solution.py:18
  97.7 3.9 %collective-permute-start.11 = (bf16[2,4,6,1,192]{4,3,2,1,0:T(2,128)(2,1)S(1)}, bf16[2,4,6,1,192]{4,3,2,1,0:T(2,128)(2,1)S(1)}, u32[]{:S(2)}, u32[]{:S(2)}) collective-permute-start(bf16[2,4,6,1,192]{4,3,2,1,0:T(2,128)(2,1)S(1)} %get-tuple-element.47), channel_id=1, source_target_pairs={{0,1},{2,3},{4,5},{6,7},{8,9},{10,11},{12,13},{14,15},{16,17},{18,... | collective-permute-start | bytes 55304 | tf_op jit(solution)/shard_map/ppermute | solution.py:17
  146.4 6.0 %collective-permute-start.12 = (bf16[2,1,4,8,192]{4,3,2,1,0:T(8,128)(2,1)S(1)}, bf16[2,1,4,8,192]{4,3,2,1,0:T(8,128)(2,1)S(1)}, u32[]{:S(2)}, u32[]{:S(2)}) collective-permute-start(bf16[2,1,4,8,192]{4,3,2,1,0:T(8,128)(2,1)S(1)} %get-tuple-element.79), channel_id=1, source_target_pairs={{8,0},{16,8},{24,16},{9,1},{17,9},{25,17},{10,2},{18,10},{26,18},{... | collective-permute-start | bytes 73736 | tf_op jit(solution)/shard_map/ppermute | solution.py:18
  147.7 6.1 %collective-permute-start.13 = (bf16[2,1,4,8,192]{4,3,2,1,0:T(8,128)(2,1)S(1)}, bf16[2,1,4,8,192]{4,3,2,1,0:T(8,128)(2,1)S(1)}, u32[]{:S(2)}, u32[]{:S(2)}) collective-permute-start(bf16[2,1,4,8,192]{4,3,2,1,0:T(8,128)(2,1)S(1)} %get-tuple-element.78), channel_id=1, source_target_pairs={{0,8},{8,16},{16,24},{1,9},{9,17},{17,25},{2,10},{10,18},{18,26},{... | collective-permute-start | bytes 73736 | tf_op jit(solution)/shard_map/ppermute | solution.py:17
  153.8 6.5 %collective-permute-start.14 = (bf16[2,4,1,8,192]{4,3,2,1,0:T(8,128)(2,1)S(1)}, bf16[2,4,1,8,192]{4,3,2,1,0:T(8,128)(2,1)S(1)}, u32[]{:S(2)}, u32[]{:S(2)}) collective-permute-start(bf16[2,4,1,8,192]{4,3,2,1,0:T(8,128)(2,1)S(1)} %get-tuple-element.59), channel_id=1, source_target_pairs={{2,0},{4,2},{6,4},{3,1},{5,3},{7,5},{10,8},{12,10},{14,12},{11,9},... | collective-permute-start | bytes 73736 | tf_op jit(solution)/shard_map/ppermute | solution.py:18
  155.1 6.4 %collective-permute-start.15 = (bf16[2,4,1,8,192]{4,3,2,1,0:T(8,128)(2,1)S(1)}, bf16[2,4,1,8,192]{4,3,2,1,0:T(8,128)(2,1)S(1)}, u32[]{:S(2)}, u32[]{:S(2)}) collective-permute-start(bf16[2,4,1,8,192]{4,3,2,1,0:T(8,128)(2,1)S(1)} %get-tuple-element.58), channel_id=1, source_target_pairs={{0,2},{2,4},{4,6},{1,3},{3,5},{5,7},{8,10},{10,12},{12,14},{9,11},... | collective-permute-start | bytes 73736 | tf_op jit(solution)/shard_map/ppermute | solution.py:17
  161.6 5.0 %collective-permute-start.16 = (bf16[2,4,6,1,192]{4,3,2,1,0:T(2,128)(2,1)S(1)}, bf16[2,4,6,1,192]{4,3,2,1,0:T(2,128)(2,1)S(1)}, u32[]{:S(2)}, u32[]{:S(2)}) collective-permute-start(bf16[2,4,6,1,192]{4,3,2,1,0:T(2,128)(2,1)S(1)} %get-tuple-element.42), channel_id=1, source_target_pairs={{1,0},{3,2},{5,4},{7,6},{9,8},{11,10},{13,12},{15,14},{17,16},{19,... | collective-permute-start | bytes 55304 | tf_op jit(solution)/shard_map/ppermute | solution.py:18
  162.9 3.9 %collective-permute-start.17 = (bf16[2,4,6,1,192]{4,3,2,1,0:T(2,128)(2,1)S(1)}, bf16[2,4,6,1,192]{4,3,2,1,0:T(2,128)(2,1)S(1)}, u32[]{:S(2)}, u32[]{:S(2)}) collective-permute-start(bf16[2,4,6,1,192]{4,3,2,1,0:T(2,128)(2,1)S(1)} %get-tuple-element.43), channel_id=1, source_target_pairs={{0,1},{2,3},{4,5},{6,7},{8,9},{10,11},{12,13},{14,15},{16,17},{18,... | collective-permute-start | bytes 55304 | tf_op jit(solution)/shard_map/ppermute | solution.py:17
  211.3 7.0 %collective-permute-start.18 = (bf16[2,1,4,8,192]{4,3,2,1,0:T(8,128)(2,1)S(1)}, bf16[2,1,4,8,192]{4,3,2,1,0:T(8,128)(2,1)S(1)}, u32[]{:S(2)}, u32[]{:S(2)}) collective-permute-start(bf16[2,1,4,8,192]{4,3,2,1,0:T(8,128)(2,1)S(1)} %get-tuple-element.77), channel_id=1, source_target_pairs={{8,0},{16,8},{24,16},{9,1},{17,9},{25,17},{10,2},{18,10},{26,18},{... | collective-permute-start | bytes 73736 | tf_op jit(solution)/shard_map/ppermute | solution.py:18
  212.6 6.1 %collective-permute-start.19 = (bf16[2,1,4,8,192]{4,3,2,1,0:T(8,128)(2,1)S(1)}, bf16[2,1,4,8,192]{4,3,2,1,0:T(8,128)(2,1)S(1)}, u32[]{:S(2)}, u32[]{:S(2)}) collective-permute-start(bf16[2,1,4,8,192]{4,3,2,1,0:T(8,128)(2,1)S(1)} %get-tuple-element.76), channel_id=1, source_target_pairs={{0,8},{8,16},{16,24},{1,9},{9,17},{17,25},{2,10},{10,18},{18,26},{... | collective-permute-start | bytes 73736 | tf_op jit(solution)/shard_map/ppermute | solution.py:17
  218.8 6.6 %collective-permute-start.20 = (bf16[2,4,1,8,192]{4,3,2,1,0:T(8,128)(2,1)S(1)}, bf16[2,4,1,8,192]{4,3,2,1,0:T(8,128)(2,1)S(1)}, u32[]{:S(2)}, u32[]{:S(2)}) collective-permute-start(bf16[2,4,1,8,192]{4,3,2,1,0:T(8,128)(2,1)S(1)} %get-tuple-element.57), channel_id=1, source_target_pairs={{2,0},{4,2},{6,4},{3,1},{5,3},{7,5},{10,8},{12,10},{14,12},{11,9},... | collective-permute-start | bytes 73736 | tf_op jit(solution)/shard_map/ppermute | solution.py:18
  220.1 6.4 %collective-permute-start.21 = (bf16[2,4,1,8,192]{4,3,2,1,0:T(8,128)(2,1)S(1)}, bf16[2,4,1,8,192]{4,3,2,1,0:T(8,128)(2,1)S(1)}, u32[]{:S(2)}, u32[]{:S(2)}) collective-permute-start(bf16[2,4,1,8,192]{4,3,2,1,0:T(8,128)(2,1)S(1)} %get-tuple-element.56), channel_id=1, source_target_pairs={{0,2},{2,4},{4,6},{1,3},{3,5},{5,7},{8,10},{10,12},{12,14},{9,11},... | collective-permute-start | bytes 73736 | tf_op jit(solution)/shard_map/ppermute | solution.py:17
  226.6 5.0 %collective-permute-start.22 = (bf16[2,4,6,1,192]{4,3,2,1,0:T(2,128)(2,1)S(1)}, bf16[2,4,6,1,192]{4,3,2,1,0:T(2,128)(2,1)S(1)}, u32[]{:S(2)}, u32[]{:S(2)}) collective-permute-start(bf16[2,4,6,1,192]{4,3,2,1,0:T(2,128)(2,1)S(1)} %get-tuple-element.38), channel_id=1, source_target_pairs={{1,0},{3,2},{5,4},{7,6},{9,8},{11,10},{13,12},{15,14},{17,16},{19,... | collective-permute-start | bytes 55304 | tf_op jit(solution)/shard_map/ppermute | solution.py:18
  227.9 3.9 %collective-permute-start.23 = (bf16[2,4,6,1,192]{4,3,2,1,0:T(2,128)(2,1)S(1)}, bf16[2,4,6,1,192]{4,3,2,1,0:T(2,128)(2,1)S(1)}, u32[]{:S(2)}, u32[]{:S(2)}) collective-permute-start(bf16[2,4,6,1,192]{4,3,2,1,0:T(2,128)(2,1)S(1)} %get-tuple-element.39), channel_id=1, source_target_pairs={{0,1},{2,3},{4,5},{6,7},{8,9},{10,11},{12,13},{14,15},{16,17},{18,... | collective-permute-start | bytes 55304 | tf_op jit(solution)/shard_map/ppermute | solution.py:17
  (7 other events, 339.8 us)
where the time goes:
time: 321 us; the launch traced here: 320 us
  blocking collectives  213 us (66%)
  starting transfers between devices  66 us (21%)
  local copies, waits for them, and re-layouts  14.6 us (5%)
  waiting for transfers between devices  10.3 us (3%)
  matrix products  9.28 us (3%)
  other arithmetic  4.76 us (1%)
    psum x4, blocking collectives, local(): projected, energy = lax.psum((projected, energy), ('gx', 'gy', 'gz'))  172 us
    ppermute x12, starting transfers between devices, with_halo(): before = lax.ppermute(last, axis, up)  50.5 us
    unnamed x1, blocking collectives  41 us
    ppermute x12, starting transfers between devices, with_halo(): after = lax.ppermute(initial, axis, down)  15.5 us
    ppermute x12, waiting for transfers between devices, with_halo(): before = lax.ppermute(last, axis, up)  10.3 us
    dot_general x28, matrix products, typed_product(): jnp.dot(flattened, block_table, preferred_element_type=jnp.float32)  9.28 us
    unnamed x15, local copies, waits for them, and re-layouts  7.86 us
  transfers between devices with their start and end apart: 24, of which 12 were waited for; matrix products, arithmetic and copies ran while one was open for 2% of the time, Pallas kernels for 0%

commit v1 on v0

--- a/solution.py
+++ b/solution.py
@@ -1,10 +1,425 @@
+import functools
+
 import jax
 import jax.numpy as jnp
+import numpy as np
 from jax import lax
+from jax.experimental import pallas as pl
+from jax.experimental.pallas import tpu as pltpu
 from jax.sharding import PartitionSpec as P
 
 ITERS = 4
 GPB = 8
+LANES = 256
+F32 = jnp.float32
+BF16 = jnp.bfloat16
+VMEM = pl.BlockSpec(memory_space=pltpu.VMEM)
+SMEM = pl.BlockSpec(memory_space=pltpu.SMEM)
+
+
+def axis_slots(peers, length, depth):
+    reach, following = {}, {}
+    for p in range(-depth, length + depth):
+        key = (p // length) % peers, p % length
+        away = max(0, -p, p - length + 1)
+        reach[key] = min(reach.get(key, away), away)
+        following[key] = ((p + 1) // length) % peers, (p + 1) % length
+    return reach, following
+
+
+class Window:
+    def __init__(self, peers_x, peers_y, len_x, len_y):
+        near_x, next_x = axis_slots(peers_x, len_x, ITERS)
+        near_y, next_y = axis_slots(peers_y, len_y, ITERS)
+        columns = [(near_x[x] + near_y[y], x, y) for x in near_x for y in near_y]
+        columns = sorted(c for c in columns if c[0] <= ITERS)
+        self.depths = [c[0] for c in columns]
+        self.keys = [c[1:] for c in columns]
+        place = {k: i for i, k in enumerate(self.keys)}
+        prev_x = {b: a for a, b in next_x.items()}
+        prev_y = {b: a for a, b in next_y.items()}
+        self.count = [sum(d <= r for d in self.depths) for r in range(ITERS + 1)]
+        self.neighbours = np.array(
+            [
+                (
+                    place[next_x[x], y],
+                    place[x, next_y[y]],
+                    place[prev_x[x], y],
+                    place[x, prev_y[y]],
+                )
+                for x, y in self.keys[: self.count[ITERS - 1]]
+            ],
+            np.int32,
+        )
+        self.x_offsets = sorted({x[0] for x in near_x} - {0})
+        self.y_offsets = sorted({y[0] for y in near_y} - {0})
+        self.y_columns = {o: [k for k in self.keys if k[1][0] == o] for o in self.y_offsets}
+        self.sources = []
+        for x, y in self.keys:
+            if y[0]:
+                at = 1 + len(self.x_offsets) + self.y_offsets.index(y[0])
+                self.sources.append((at, self.y_columns[y[0]].index((x, y))))
+            else:
+                at = 1 + self.x_offsets.index(x[0]) if x[0] else 0
+                self.sources.append((at, x[1] * len_y + y[1]))
+
+
+def lane_iota(shape):
+    return lax.broadcasted_iota(jnp.int32, shape, len(shape) - 1)
+
+
+def pack_kernel(own_ref, got_ref, blocks_ref, hi_ref, lo_ref, diag_ref):
+    dof = blocks_ref.shape[-1]
+    rows = lax.broadcasted_iota(jnp.int32, (dof, dof), 0)
+    eye = (rows == lane_iota((dof, dof))).astype(F32)
+    diag_ref[...] = jnp.ones(diag_ref.shape, F32)
+    for t in range(blocks_ref.shape[0]):
+        diag_ref[t : t + 1, :dof] = jnp.sum(blocks_ref[t].astype(F32) * eye, axis=0, keepdims=True)
+    half = own_ref.shape[1]
+    lane = lane_iota((half, LANES))
+    for i in range(own_ref.shape[0]):
+        his, los = [], []
+        for ref in (own_ref, got_ref):
+            x = ref[i]
+            kind = x[:, dof + 6 : dof + 7]
+            density = x[:, dof + 7 : dof + 8]
+            pivot = jnp.ones((half, LANES), F32)
+            for t in range(blocks_ref.shape[0]):
+                pivot = jnp.where(kind == t, diag_ref[t : t + 1, :], pivot)
+            scale = density * jnp.sqrt(density)
+            ship = jnp.where(lane < dof, (x / pivot) * scale, x)
+            hi = ship.astype(BF16).astype(F32)
+            lo = ship - hi
+            mid = lo.astype(BF16).astype(F32)
+            his.append(jnp.where(lane < dof + 8, hi, jnp.where(lane == dof + 8, mid, lo - mid)))
+            los.append(jnp.where(lane < dof, lo, 0.0))
+        hi_ref[i] = jnp.concatenate(his, axis=0).astype(BF16)
+        lo_ref[i] = jnp.concatenate(los, axis=0).astype(BF16)
+
+
+def divisor(n, cap):
+    return max(d for d in range(1, cap + 1) if n % d == 0)
+
+
+def sweep_kernel(window, refs_in, *rest):
+    pieces = rest[:refs_in]
+    (lo_ref, diag_ref, off_ref, self_ref, near_ref, keep_ref, send_ref) = rest[refs_in : refs_in + 7]
+    (ship_a, ship_b, kinds, gain, scale, up_w, low_w, own_w, up_l, low_l, own_l) = rest[refs_in + 7 :]
+    dof = off_ref.shape[-1]
+    kinds_n = off_ref.shape[0]
+    depth = ship_a.shape[1]
+    half = depth // 2
+    up_w[...] = jnp.zeros(up_w.shape, BF16)
+    low_w[...] = jnp.zeros(low_w.shape, BF16)
+    own_w[...] = jnp.zeros(own_w.shape, BF16)
+    for t in range(kinds_n):
+        up_w[:dof, t * LANES : t * LANES + dof] = off_ref[t]
+        low_w[t * LANES : t * LANES + dof, :dof] = off_ref[t]
+        own_w[t * LANES : t * LANES + dof, :dof] = self_ref[t]
+    for i, (at, j) in enumerate(window.sources):
+        x = pieces[at][j].astype(F32)
+        if window.depths[i] == 0:
+            x = x + lo_ref[j].astype(F32)
+        ship_a[i] = x
+    targets = window.count[ITERS - 1]
+    spread_rows = lax.broadcasted_iota(jnp.int32, (128, 8 * 128), 0) - (dof - 128)
+    spread_cols = lane_iota((128, 8 * 128)) // 128
+    spread = (jnp.minimum(spread_rows, 7) == spread_cols) & (spread_rows >= 0) & (spread_rows < 10)
+    spread = spread.astype(BF16)
+    batch = divisor(targets, 8)
+    for c in range(targets // batch):
+        lines = []
+        for u in range(batch):
+            at, j = window.sources[c * batch + u]
+            lines.append(pieces[at][j, :, 128:])
+        found = jnp.dot(jnp.concatenate(lines, axis=0), spread, preferred_element_type=F32)
+        for u in range(batch):
+            i = c * batch + u
+            part = found[u * depth : (u + 1) * depth]
+            for k in range(7):
+                kinds[i, k] = part[:, k * 128 : (k + 1) * 128]
+            density = part[:, 7 * 128 :]
+            s = density * jnp.sqrt(density)
+            scale[i] = s
+            for side in range(2):
+                lanes = slice(side * 128, side * 128 + 128)
+                pivot = jnp.ones((depth, 128), F32)
+                for t in range(kinds_n):
+                    pivot = jnp.where(part[:, 6 * 128 : 7 * 128] == t, diag_ref[t : t + 1, lanes], pivot)
+                gain[i, :, lanes] = s * s / pivot
+
+    def build(src, i, row, low_row):
+        for side in range(2):
+            lanes = slice(side * 128, side * 128 + 128)
+            mine = src[i, :, lanes]
+            nears = [
+                src[near_ref[i, 0], :, lanes],
+                src[near_ref[i, 1], :, lanes],
+                pltpu.roll(mine, depth - 1, 0),
+                src[near_ref[i, 2], :, lanes],
+                src[near_ref[i, 3], :, lanes],
+                pltpu.roll(mine, 1, 0),
+                mine,
+            ]
+            for t in range(kinds_n):
+                for dest, ks in ((up_l, (0, 1, 2)), (low_l, (3, 4, 5)), (own_l, (6,))):
+                    total = None
+                    for k in ks:
+                        term = jnp.where(kinds[i, k] == t, nears[k], 0.0)
+                        total = term if total is None else total + term
+                    hi = total.astype(BF16)
+                    at = slice(t * LANES + side * 128, t * LANES + side * 128 + 128)
+                    dest[row : row + depth, at] = hi
+                    if low_row is not None:
+                        dest[low_row : low_row + depth, at] = (total - hi.astype(F32)).astype(BF16)
+
+    def product(rows):
+        acc = lax.dot_general(up_l[:rows], up_w[...], (((1,), (1,)), ((), ())), preferred_element_type=F32)
+        acc = acc + jnp.dot(low_l[:rows], low_w[...], preferred_element_type=F32)
+        return acc + jnp.dot(own_l[:rows], own_w[...], preferred_element_type=F32)
+
+    own = window.count[0]
+    for step in range(ITERS):
+        src, dst = (ship_a, ship_b) if step % 2 == 0 else (ship_b, ship_a)
+        for u in range(own):
+            build(src, u, u * depth, (own + u) * depth)
+        acc = product(2 * own * depth)
+        for u in range(own):
+            both = acc[u * depth : (u + 1) * depth] + acc[(own + u) * depth : (own + u + 1) * depth]
+            for side in range(2):
+                lanes = slice(side * 128, side * 128 + 128)
+                value = both[:, lanes] * scale[u]
+                keep_ref[step, u, :, lanes] = value[:half]
+                send_ref[step, u, :, lanes] = value[half:]
+            if step < ITERS - 1:
+                dst[u] = both * gain[u]
+        halo = window.count[ITERS - 1 - step] - own
+        if halo:
+            batch = divisor(halo, 14)
+
+            def one(c, carry):
+                first = own + c * batch
+                for u in range(batch):
+                    build(src, first + u, u * depth, None)
+                acc = product(batch * depth)
+                for u in range(batch):
+                    dst[first + u] = acc[u * depth : (u + 1) * depth] * gain[first + u]
+                return carry
+
+            lax.fori_loop(0, halo // batch, one, 0)
+
+
+def gram_index(i, j):
+    i, j = min(i, j), max(i, j)
+    return i * (ITERS + 1) - i * (i - 1) // 2 + j - i
+
+
+def moments_kernel(place_ref, own_ref, sent_ref, keep_ref, got_ref, diag_ref, message_ref, state_ref, adjoint_ref):
+    dof = 192
+    first = place_ref[0] == 0
+    cols, half = own_ref.shape[0], own_ref.shape[1]
+    lane = lane_iota((half, 128))
+    used = lane < dof - 128
+    sums = [[None] * 15, [None] * 15]
+    terms, dens, dests = [], [], []
+    dest_lane = lane_iota((half, message_ref.shape[0]))
+    for i in range(cols):
+        mine_0, other_0 = own_ref[i], sent_ref[i]
+        kind = mine_0[:, dof + 6 : dof + 7]
+        density = mine_0[:, dof + 7 : dof + 8]
+        owner = mine_0[:, dof + 10 : dof + 11].astype(jnp.int32)
+        inside = lax.rem(owner, GPB)
+        products = [None] * 16
+        for side in range(2):
+            lanes = slice(side * 128, side * 128 + 128)
+            pivot = jnp.ones((half, 128), F32)
+            for t in range(4):
+                pivot = jnp.where(kind == t, diag_ref[t : t + 1, lanes], pivot)
+            state, adjoint = [], []
+            for k in range(ITERS + 1):
+                a = mine_0[:, lanes] if k == 0 else keep_ref[k - 1, i, :, lanes]
+                b = other_0[:, lanes] if k == 0 else got_ref[k - 1, i, :, lanes]
+                if side == 1 and k == 0:
+                    a, b = jnp.where(used, a, 0.0), jnp.where(used, b, 0.0)
+                state.append(jnp.where(first, a, b))
+                adjoint.append(jnp.where(first, b, a))
+            for f, v in enumerate((state, adjoint)):
+                for p in range(ITERS + 1):
+                    for q in range(p, ITERS + 1):
+                        n = gram_index(p, q)
+                        term = v[p] * v[q]
+                        sums[f][n] = term if sums[f][n] is None else sums[f][n] + term
+            pre_s = [v / pivot for v in state[:ITERS]]
+            pre_a = [v / pivot for v in adjoint[:ITERS]]
+            for k in range(ITERS):
+                state_ref[k, i, :, lanes] = pre_s[k]
+                adjoint_ref[k, i, :, lanes] = pre_a[k]
+                for j in range(ITERS):
+                    term = pre_a[k] * state[j + 1] + pre_s[j] * adjoint[k + 1]
+                    n = k * ITERS + j
+                    products[n] = term if products[n] is None else products[n] + term
+        spread = jnp.zeros((half, 128), F32)
+        for n in range(16):
+            spread = jnp.where(lane // GPB == n, jnp.sum(products[n], axis=1, keepdims=True), spread)
+        hit = lane % GPB == inside
+        terms.append(jnp.where(hit, spread, 0.0))
+        dens.append(jnp.where(hit & (lane < GPB), density, 0.0))
+        dests.append((lax.div(owner, GPB) == dest_lane).astype(F32))
+    right = jnp.concatenate([jnp.concatenate(terms, axis=0), jnp.concatenate(dens, axis=0)], axis=1)
+    left = jnp.concatenate(dests, axis=0)
+    message = lax.dot_general(
+        left, right, (((0,), (0,)), ((), ())), preferred_element_type=F32, precision=lax.Precision.HIGHEST
+    )
+    line = lane_iota((1, 128))
+    row = jnp.zeros((1, 128), F32)
+    for f in range(2):
+        for n in range(15):
+            total = jnp.sum(jnp.sum(sums[f][n], axis=0, keepdims=True), axis=1, keepdims=True)
+            row = jnp.where(line == 16 + 32 * f + n, total, row)
+    message_ref[:, :128] = message[:, :128]
+    message_ref[:, 128:] = message[:, 128:] + row
+
+
+def finish_kernel(message_ref, pre_state_ref, pre_adjoint_ref, state_ref, adjoint_ref, coarse_ref):
+    total = jnp.sum(message_ref[...], axis=0, keepdims=True)
+    sums = total[:, 128:]
+    weights = []
+    for f in range(2):
+
+        def inner(c, d):
+            out = None
+            for p, u in enumerate(c):
+                for q, v in enumerate(d):
+                    if u is None or v is None:
+                        continue
+                    n = 16 + 32 * f + gram_index(p, q)
+                    term = (u * v) * sums[:, n : n + 1]
+                    out = term if out is None else out + term
+            return out
+
+        c = [jnp.ones((1, 1), F32)] + [None] * ITERS
+        beta = [None] * ITERS
+        for sweep in range(ITERS):
+            w = [None] + c[:ITERS]
+            step = inner(c, w) / (inner(w, w) + 1e-06)
+            for k in range(ITERS):
+                if c[k] is not None:
+                    beta[k] = step * c[k] if beta[k] is None else beta[k] + step * c[k]
+            moved = []
+            for k in range(ITERS + 1):
+                if w[k] is None:
+                    moved.append(c[k])
+                else:
+                    moved.append(-step * w[k] if c[k] is None else c[k] - step * w[k])
+            c = moved
+        weights.append(beta)
+    dof = state_ref.shape[-1]
+    for beta, pre, out in ((weights[0], pre_state_ref, state_ref), (weights[1], pre_adjoint_ref, adjoint_ref)):
+        value = pre[0] * beta[0]
+        for k in range(1, ITERS):
+            value = value + pre[k] * beta[k]
+        out[...] = value[..., :dof]
+    lane = lane_iota((1, 128))
+    factor = jnp.zeros((1, 128), F32)
+    for k in range(ITERS):
+        for j in range(ITERS):
+            factor = jnp.where(lane // GPB == k * ITERS + j, weights[1][k] * weights[0][j], factor)
+    folded = total[:, :128] * factor
+    for shift in (64, 32, 16, 8):
+        folded = folded + pltpu.roll(folded, shift, 1)
+    coarse_ref[...] = -1.5 * folded / jnp.where(lane < GPB, sums, 1.0)
+
+
+def shifted(array, axis, offset):
+    peers = lax.axis_size(axis)
+    return lax.ppermute(array, axis, [((i + offset) % peers, i) for i in range(peers)])
+
+
+def by_field(body_load, probe_load, density, link_types, off_blocks, self_blocks, block_owner):
+    len_x, len_y, half, dof = body_load.shape
+    cols = len_x * len_y
+    depth = 2 * half
+    window = Window(lax.axis_size("gx"), lax.axis_size("gy"), len_x, len_y)
+    core = lax.axis_index("gz")
+    note = jnp.concatenate(
+        [link_types.astype(F32)] + [density[..., None]] * 3 + [block_owner[..., None].astype(F32)], axis=-1
+    )
+    note = jnp.pad(note, ((0, 0),) * 3 + ((0, LANES - dof - note.shape[-1]),))
+    first = core == 0
+    own = jnp.concatenate([jnp.where(first, body_load, probe_load), note], axis=-1).reshape(cols, half, LANES)
+    sent = jnp.concatenate([jnp.where(first, probe_load, body_load), note], axis=-1).reshape(cols, half, LANES)
+    got = shifted(sent, "gz", 1)
+    hi, lo, diag = pl.pallas_call(
+        pack_kernel,
+        out_shape=(
+            jax.ShapeDtypeStruct((cols, depth, LANES), BF16),
+            jax.ShapeDtypeStruct((cols, depth, LANES), BF16),
+            jax.ShapeDtypeStruct((8, LANES), F32),
+        ),
+        in_specs=[VMEM] * 3,
+        out_specs=(VMEM,) * 3,
+        name="pack",
+    )(own, got, self_blocks)
+    from_x = {0: hi}
+    for o in window.x_offsets:
+        from_x[o] = shifted(hi, "gx", o)
+    pieces = [from_x[o] for o in [0] + window.x_offsets]
+    for o in window.y_offsets:
+        lines = []
+        for x, y in window.y_columns[o]:
+            at = x[1] * len_y + y[1]
+            lines.append(from_x[x[0]][at : at + 1])
+        pieces.append(shifted(jnp.concatenate(lines, axis=0), "gy", o))
+    targets = window.count[ITERS - 1]
+    own_n = window.count[0]
+    rows = depth * max(2 * own_n, 14)
+    keep, send = pl.pallas_call(
+        functools.partial(sweep_kernel, window, len(pieces)),
+        out_shape=(jax.ShapeDtypeStruct((ITERS, cols, half, LANES), F32),) * 2,
+        in_specs=[VMEM] * (len(pieces) + 4) + [SMEM],
+        out_specs=(VMEM,) * 2,
+        scratch_shapes=[
+            pltpu.VMEM((window.count[ITERS], depth, LANES), F32),
+            pltpu.VMEM((targets, depth, LANES), F32),
+            pltpu.VMEM((targets, 7, depth, 128), F32),
+            pltpu.VMEM((targets, depth, LANES), F32),
+            pltpu.VMEM((targets, depth, 128), F32),
+            pltpu.VMEM((LANES, 4 * LANES), BF16),
+            pltpu.VMEM((4 * LANES, LANES), BF16),
+            pltpu.VMEM((4 * LANES, LANES), BF16),
+            pltpu.VMEM((rows, 4 * LANES), BF16),
+            pltpu.VMEM((rows, 4 * LANES), BF16),
+            pltpu.VMEM((rows, 4 * LANES), BF16),
+        ],
+        compiler_params=pltpu.CompilerParams(vmem_limit_bytes=40 * 2**20),
+        name="sweeps",
+    )(*pieces, lo, diag, off_blocks, self_blocks, jnp.asarray(window.neighbours))
+    back = shifted(send, "gz", 1)
+    owners = lax.axis_size("gx") * lax.axis_size("gy") * lax.axis_size("gz")
+    message, pre_state, pre_adjoint = pl.pallas_call(
+        moments_kernel,
+        out_shape=(
+            jax.ShapeDtypeStruct((owners, LANES), F32),
+            jax.ShapeDtypeStruct((ITERS, cols, half, LANES), F32),
+            jax.ShapeDtypeStruct((ITERS, cols, half, LANES), F32),
+        ),
+        in_specs=[SMEM] + [VMEM] * 5,
+        out_specs=(VMEM,) * 3,
+        name="moments",
+    )(core.reshape(1), own, sent, keep, back, diag)
+    message = lax.all_to_all(message, ("gx", "gy", "gz"), 0, 0, tiled=True)
+    state, adjoint, coarse = pl.pallas_call(
+        finish_kernel,
+        out_shape=(
+            jax.ShapeDtypeStruct((cols, half, dof), F32),
+            jax.ShapeDtypeStruct((cols, half, dof), F32),
+            jax.ShapeDtypeStruct((1, 128), F32),
+        ),
+        in_specs=[VMEM] * 3,
+        out_specs=(VMEM,) * 3,
+        name="finish",
+    )(message, pre_state, pre_adjoint)
+    return state.reshape(body_load.shape), adjoint.reshape(body_load.shape), coarse[0, :GPB]
 
 
 def with_halo(array, sides, width):
@@ -58,7 +473,7 @@
     return accumulated * stiff_scale[None, :, :, :, None]
 
 
-def local(body_load, probe_load, density, link_types, off_blocks, self_blocks, block_owner):
+def by_sweep(body_load, probe_load, density, link_types, off_blocks, self_blocks, block_owner):
     dof_count = body_load.shape[-1]
     type_count = off_blocks.shape[0]
     self_count = self_blocks.shape[0]
@@ -120,4 +535,8 @@
         P("gx", "gy", "gz"),
     )
     out_specs = (P("gx", "gy", "gz", None), P("gx", "gy", "gz", None), P(("gx", "gy", "gz")))
+    def local(*arrays):
+        split = lax.axis_size("gz") == 2 and arrays[0].shape[2] % 8 == 0
+        return (by_field if split else by_sweep)(*arrays)
+
     return jax.shard_map(local, mesh=mesh, in_specs=in_specs, out_specs=out_specs, check_vma=False)

time: 321 us -> 64.8 us (0.20)
  blocking collectives: 213 us -> 11.5 us
  starting transfers between devices: 66 us -> 10.3 us
  Pallas kernels: 0 us -> 19.7 us
  matrix products: 9.28 us -> 0 us
  local copies, waits for them, and re-layouts: 14.6 us -> 10.6 us
  other arithmetic: 4.76 us -> 1.52 us
    psum x4 -> x0, blocking collectives: 172 us -> none  [local(): projected, energy = lax.psum((projected, energy), ('gx', 'gy', 'gz'))]
    ppermute x24 -> x7, starting transfers between devices: 66 us -> 10.3 us  [shifted(): lax.ppermute(array, axis, [((i + offset) % peers, i) for i in range(peers)])]
    unnamed x1 -> x0, blocking collectives: 41 us -> none
    pallas_call x0 -> x4, Pallas kernels: none -> 19.7 us  [the longest x1 12.4 us: by_field(): pl.pallas_call(functools.partial(sweep_kernel, window, len(pieces)), out_...]
    all_to_all x0 -> x1, blocking collectives: none -> 11.5 us  [by_field(): message = lax.all_to_all(message, ('gx', 'gy', 'gz'), 0, 0, tiled=True)]
    dot_general x28 -> x0, matrix products: 9.28 us -> none  [typed_product(): jnp.dot(flattened, block_table, preferred_element_type=jnp.float32)]
    gather x1 -> x0, local copies, waits for them, and re-layouts: 5.32 us -> none  [local(): diagonals = jnp.diagonal(self_blocks, axis1=1, axis2=2).astype(jnp.float32)]
    unnamed x15 -> x54, local copies, waits for them, and re-layouts: 7.86 us -> 9.29 us
  transfers between devices with their start and end apart: 24 -> 7, of which waited for: 12 -> 5; matrix products, arithmetic and copies ran while one was open for 2% -> 8% of each run, Pallas kernels for 0% -> 0%
where the time goes in v1:
time: 64.8 us; the launch traced here: 64 us
  Pallas kernels  19.7 us (30%)
  blocking collectives  11.5 us (18%)
  local copies, waits for them, and re-layouts  10.6 us (16%)
  starting transfers between devices  10.3 us (16%)
  waiting for transfers between devices  9.56 us (15%)
  other arithmetic  1.52 us (2%)
  between operations  0.83 us (1%)
    pallas_call x1, Pallas kernels, by_field(): pl.pallas_call(functools.partial(sweep_kernel, window, len(pieces)), out_...  12.4 us
    all_to_all x1, blocking collectives, by_field(): message = lax.all_to_all(message, ('gx', 'gy', 'gz'), 0, 0, tiled=True)  11.5 us
    ppermute x7, starting transfers between devices, shifted(): lax.ppermute(array, axis, [((i + offset) % peers, i) for i in range(peers)])  10.3 us
    ppermute x7, waiting for transfers between devices, shifted(): lax.ppermute(array, axis, [((i + offset) % peers, i) for i in range(peers)])  9.56 us
    unnamed x54, local copies, waits for them, and re-layouts  9.29 us
    pallas_call x1, Pallas kernels, by_field(): pl.pallas_call(finish_kernel, out_shape=(jax.ShapeDtypeStruct((cols, half...  2.66 us
    pallas_call x1, Pallas kernels, by_field(): pl.pallas_call(moments_kernel, out_shape=(jax.ShapeDtypeStruct((owners, L...  2.57 us
    pallas_call x1, Pallas kernels, by_field(): pl.pallas_call(pack_kernel, out_shape=(jax.ShapeDtypeStruct((cols, depth,...  2.02 us
  transfers between devices with their start and end apart: 7, of which 5 were waited for; matrix products, arithmetic and copies ran while one was open for 8% of the time, Pallas kernels for 0%

profile of v1, /device:TPU:0, one launch (start us, length us, event | category | flops | bytes accessed | tf_op | source)
XLA Modules:
  0.0 64.0 jit_solution(8610154227803649230)
XLA Ops:
  0.7 0.8 %constant_dynamic-update-slice_fusion.4 = f32[2,4,8,11]{2,1,3,0:T(4,128)S(1)} fusion(s32[2,4,8,7]{2,1,3,0:T(4,128)} %param.11), kind=kLoop, calls=%fused_computation.4 | loop fusion | flops 447 | bytes 30464
  3.5 0.9 %collective-permute-done.got_ref = f32[8,8,256]{2,1,0:T(8,128)S(1)} collective-permute-done((f32[8,8,256]{2,1,0:T(8,128)S(1)}, f32[8,8,256]{2,1,0:T(8,128)S(1)}, u32[]{:S(2)}, u32[]{:S(2)}) %collective-permute-start) | collective-permute-done | bytes 65568 | tf_op jit(solution)/shard_map/ppermute | solution.py:335
  5.0 2.0 %pack.1 = (bf16[8,16,256]{2,1,0:T(8,128)(2,1)}, bf16[8,16,256]{2,1,0:T(8,128)(2,1)}, f32[8,256]{1,0:T(8,128)}) custom-call(f32[8,8,256]{2,1,0:T(8,128)} %bitcast.21, f32[8,8,256]{2,1,0:T(8,128)} %copy-done.11, bf16[4,192,192]{2,1,0:T(8,128)(2,1)} %rest_9_.1), custom_call_target="tpu_custom_call" | custom-call | tf_op jit(solution)/shard_map/pack/pallas_call | solution.py:352
  7.0 2.9 %collective-permute-start.3 = (bf16[8,16,256]{2,1,0:T(8,128)(2,1)}, bf16[8,16,256]{2,1,0:T(8,128)(2,1)S(1)}, u32[]{:S(2)}, u32[]{:S(2)}) collective-permute-start(bf16[8,16,256]{2,1,0:T(8,128)(2,1)} %get-tuple-element.14.rest_0_), channel_id=1, source_target_pairs={{24,0},{0,8},{8,16},{16,24},{25,1},{1,9},{9,17},{17,25},{26,2},{2,... | collective-permute-start | bytes 196616 | tf_op jit(solution)/shard_map/ppermute | solution.py:335
  10.0 2.6 %collective-permute-start.2 = (bf16[8,16,256]{2,1,0:T(8,128)(2,1)}, bf16[8,16,256]{2,1,0:T(8,128)(2,1)S(1)}, u32[]{:S(2)}, u32[]{:S(2)}) collective-permute-start(bf16[8,16,256]{2,1,0:T(8,128)(2,1)} %get-tuple-element.14.rest_0_), channel_id=1, source_target_pairs={{16,0},{24,8},{0,16},{8,24},{17,1},{25,9},{1,17},{9,25},{18,2},{26... | collective-permute-start | bytes 196616 | tf_op jit(solution)/shard_map/ppermute | solution.py:335
  12.5 1.3 %collective-permute-start.1 = (bf16[8,16,256]{2,1,0:T(8,128)(2,1)}, bf16[8,16,256]{2,1,0:T(8,128)(2,1)S(1)}, u32[]{:S(2)}, u32[]{:S(2)}) collective-permute-start(bf16[8,16,256]{2,1,0:T(8,128)(2,1)} %get-tuple-element.14.rest_0_), channel_id=1, source_target_pairs={{8,0},{16,8},{24,16},{0,24},{9,1},{17,9},{25,17},{1,25},{10,2},{18... | collective-permute-start | bytes 196616 | tf_op jit(solution)/shard_map/ppermute | solution.py:335
  13.9 0.7 %constant_dynamic-update-slice_fusion.44 = (bf16[20,16,256]{2,1,0:T(8,128)(2,1)S(1)}, bf16[20,16,256]{2,1,0:T(8,128)(2,1)S(1)}) fusion(bf16[8,16,256]{2,1,0:T(8,128)(2,1)} %get-tuple-element.14.rest_0_), kind=kLoop, calls=%fused_computation.44 | loop fusion | bytes 32768
  14.6 0.7 %constant_dynamic-update-slice_fusion.43 = (bf16[20,16,256]{2,1,0:T(8,128)(2,1)S(1)}, bf16[20,16,256]{2,1,0:T(8,128)(2,1)S(1)}) fusion(bf16[20,16,256]{2,1,0:T(8,128)(2,1)S(1)} %get-tuple-element.65, bf16[8,16,256]{2,1,0:T(8,128)(2,1)} %get-tuple-element.14.rest_0_, bf16[20,16,256]{2,1,0:T(8,128)(2,1)S(1)} %get-tuple-element.66), kind=kLoop, calls=%fused_computation.43 | loop fusion | bytes 32768
  15.3 0.7 %constant_dynamic-update-slice_fusion.42 = (bf16[20,16,256]{2,1,0:T(8,128)(2,1)S(1)}, bf16[20,16,256]{2,1,0:T(8,128)(2,1)S(1)}) fusion(bf16[20,16,256]{2,1,0:T(8,128)(2,1)S(1)} %get-tuple-element.63, bf16[8,16,256]{2,1,0:T(8,128)(2,1)} %get-tuple-element.14.rest_0_, bf16[20,16,256]{2,1,0:T(8,128)(2,1)S(1)} %get-tuple-element.64), kind=kLoop, calls=%fused_computation.42 | loop fusion | bytes 32768
  16.1 0.7 %constant_dynamic-update-slice_fusion.41 = (bf16[20,16,256]{2,1,0:T(8,128)(2,1)S(1)}, bf16[20,16,256]{2,1,0:T(8,128)(2,1)S(1)}) fusion(bf16[20,16,256]{2,1,0:T(8,128)(2,1)S(1)} %get-tuple-element.61, bf16[8,16,256]{2,1,0:T(8,128)(2,1)} %get-tuple-element.14.rest_0_, bf16[20,16,256]{2,1,0:T(8,128)(2,1)S(1)} %get-tuple-element.62), kind=kLoop, calls=%fused_computation.41 | loop fusion | bytes 32768
  16.8 1.0 %collective-permute-done.1.rest_1_ = bf16[8,16,256]{2,1,0:T(8,128)(2,1)S(1)} collective-permute-done((bf16[8,16,256]{2,1,0:T(8,128)(2,1)}, bf16[8,16,256]{2,1,0:T(8,128)(2,1)S(1)}, u32[]{:S(2)}, u32[]{:S(2)}) %collective-permute-start.1) | collective-permute-done | bytes 65568 | tf_op jit(solution)/shard_map/ppermute | solution.py:335
  17.8 0.7 %constant_dynamic-update-slice_fusion.38 = (bf16[20,16,256]{2,1,0:T(8,128)(2,1)S(1)}, bf16[20,16,256]{2,1,0:T(8,128)(2,1)S(1)}) fusion(bf16[20,16,256]{2,1,0:T(8,128)(2,1)S(1)} %get-tuple-element.55, bf16[8,16,256]{2,1,0:T(8,128)(2,1)} %get-tuple-element.14.rest_0_, bf16[20,16,256]{2,1,0:T(8,128)(2,1)S(1)} %get-tuple-element.56), kind=kLoop, calls=%fused_computation.38 | loop fusion | bytes 32768
  18.5 0.7 %constant_dynamic-update-slice_fusion.37 = (bf16[20,16,256]{2,1,0:T(8,128)(2,1)S(1)}, bf16[20,16,256]{2,1,0:T(8,128)(2,1)S(1)}) fusion(bf16[20,16,256]{2,1,0:T(8,128)(2,1)S(1)} %get-tuple-element.53, bf16[8,16,256]{2,1,0:T(8,128)(2,1)} %get-tuple-element.14.rest_0_, bf16[20,16,256]{2,1,0:T(8,128)(2,1)S(1)} %get-tuple-element.54), kind=kLoop, calls=%fused_computation.37 | loop fusion | bytes 32768
  19.2 0.7 %constant_dynamic-update-slice_fusion.32 = (bf16[20,16,256]{2,1,0:T(8,128)(2,1)S(1)}, bf16[20,16,256]{2,1,0:T(8,128)(2,1)S(1)}) fusion(bf16[20,16,256]{2,1,0:T(8,128)(2,1)S(1)} %get-tuple-element.43, bf16[8,16,256]{2,1,0:T(8,128)(2,1)} %get-tuple-element.14.rest_0_, bf16[20,16,256]{2,1,0:T(8,128)(2,1)S(1)} %get-tuple-element.44), kind=kLoop, calls=%fused_computation.32 | loop fusion | bytes 32768
  20.1 1.5 %collective-permute-start.5 = (bf16[20,16,256]{2,1,0:T(8,128)(2,1)S(1)}, bf16[20,16,256]{2,1,0:T(8,128)(2,1)S(1)}, u32[]{:S(2)}, u32[]{:S(2)}) collective-permute-start(bf16[20,16,256]{2,1,0:T(8,128)(2,1)S(1)} %get-tuple-element.27), channel_id=1, source_target_pairs={{6,0},{0,2},{2,4},{4,6},{7,1},{1,3},{3,5},{5,7},{14,8},{8,10},{10,... | collective-permute-start | bytes 491528 | tf_op jit(solution)/shard_map/ppermute | solution.py:335
  21.7 1.4 %collective-permute-start.4 = (bf16[20,16,256]{2,1,0:T(8,128)(2,1)S(1)}, bf16[20,16,256]{2,1,0:T(8,128)(2,1)S(1)}, u32[]{:S(2)}, u32[]{:S(2)}) collective-permute-start(bf16[20,16,256]{2,1,0:T(8,128)(2,1)S(1)} %get-tuple-element.28), channel_id=1, source_target_pairs={{2,0},{4,2},{6,4},{0,6},{3,1},{5,3},{7,5},{1,7},{10,8},{12,10},{14... | collective-permute-start | bytes 491528 | tf_op jit(solution)/shard_map/ppermute | solution.py:335
  23.1 4.3 %collective-permute-done.5.rest_5_ = bf16[20,16,256]{2,1,0:T(8,128)(2,1)S(1)} collective-permute-done((bf16[20,16,256]{2,1,0:T(8,128)(2,1)S(1)}, bf16[20,16,256]{2,1,0:T(8,128)(2,1)S(1)}, u32[]{:S(2)}, u32[]{:S(2)}) %collective-permute-start.5) | collective-permute-done | bytes 163872 | tf_op jit(solution)/shard_map/ppermute | solution.py:335
  27.4 1.8 %collective-permute-done.4.rest_4_ = bf16[20,16,256]{2,1,0:T(8,128)(2,1)S(1)} collective-permute-done((bf16[20,16,256]{2,1,0:T(8,128)(2,1)S(1)}, bf16[20,16,256]{2,1,0:T(8,128)(2,1)S(1)}, u32[]{:S(2)}, u32[]{:S(2)}) %collective-permute-start.4) | collective-permute-done | bytes 163872 | tf_op jit(solution)/shard_map/ppermute | solution.py:335
  29.3 12.4 %sweeps.1 = (f32[4,8,8,256]{3,2,1,0:T(8,128)S(1)}, f32[4,8,8,256]{3,2,1,0:T(8,128)S(1)}) custom-call(bf16[8,16,256]{2,1,0:T(8,128)(2,1)S(1)} %copy-done.1, bf16[8,16,256]{2,1,0:T(8,128)(2,1)S(1)} %collective-permute-done.1.rest_1_, bf16[8,16,256]{2,1,0:T(8,128)(2,1)S(1)} %collective-permute-done.2.rest_2_, ...), custom_call_target="tpu_custom_call" | custom-call | tf_op jit(solution)/shard_map/sweeps/pallas_call | solution.py:376
  42.4 1.5 %collective-permute-done.6.got_ref = f32[4,8,8,256]{3,2,1,0:T(8,128)S(1)} collective-permute-done((f32[4,8,8,256]{3,2,1,0:T(8,128)S(1)}, f32[4,8,8,256]{3,2,1,0:T(8,128)S(1)}, u32[]{:S(2)}, u32[]{:S(2)}) %collective-permute-start.6) | collective-permute-done | bytes 262176 | tf_op jit(solution)/shard_map/ppermute | solution.py:335
  44.7 2.6 %moments.1 = (f32[32,256]{1,0:T(8,128)}, f32[4,8,8,256]{3,2,1,0:T(8,128)}, f32[4,8,8,256]{3,2,1,0:T(8,128)}) custom-call(s32[1]{0:T(128)} %bitcast.place_ref, f32[8,8,256]{2,1,0:T(8,128)} %bitcast.22, f32[8,8,256]{2,1,0:T(8,128)} %bitcast.24, f32[4,8,8,256]{3,2,1,0:T(8,128)} %copy-done.3, f32[4,8,8,256]{3,2,1,0:T(8,128)} %copy-done.7, ...), custom_call_target="tpu_custom_call" | custom-call | tf_op jit(solution)/shard_map/moments/pallas_call | solution.py:399
  47.2 0.8 %copy.23 = f32[32,1,256]{2,1,0:T(1,128)S(1)} copy(f32[32,1,256]{2,0,1:T(8,128)} %bitcast.26) | data formatting | bytes 65536 | tf_op jit(solution)/shard_map/all_to_all | solution.py:410
  48.0 11.5 %all_to_all.11 = f32[32,1,256]{2,1,0:T(1,128)S(1)} all-to-all(f32[32,1,256]{2,1,0:T(1,128)S(1)} %copy.23), channel_id=1, replica_groups=mesh['gx'=4,'gy'=4,'gz'=2] {'gx','gy','gz'}, dimensions={0} | all-to-all | bytes 65536 | tf_op jit(solution)/shard_map/all_to_all | solution.py:410
  60.1 2.7 %finish.1 = (f32[8,8,192]{2,1,0:T(8,128)}, f32[8,8,192]{2,1,0:T(8,128)}, f32[1,128]{1,0:T(1,128)}) custom-call(f32[32,256]{1,0:T(8,128)} %bitcast.25, f32[4,8,8,256]{3,2,1,0:T(8,128)} %get-tuple-element.20.pre_state_ref, f32[4,8,8,256]{3,2,1,0:T(8,128)} %get-tuple-element.21.pre_adjoint_ref), custom_call_target="tpu_custom_call" | custom-call | tf_op jit(solution)/shard_map/finish/pallas_call | solution.py:411
  (56 shorter events, 5.9 us)
Async XLA Ops:
  0.6 0.8 %copy-start.12 = (f32[2,4,8]{2,1,0:T(4,128)S(1)}, f32[2,4,8]{2,1,0:T(4,128)}, u32[]{:S(2)}) copy-start(f32[2,4,8]{2,1,0:T(4,128)} %param.10) | copy-start | bytes 772
  0.6 0.9 %copy-start.13 = (s32[2,4,8]{2,1,0:T(4,128)S(1)}, s32[2,4,8]{2,1,0:T(4,128)}, u32[]{:S(2)}) copy-start(s32[2,4,8]{2,1,0:T(4,128)} %param.14) | copy-start | bytes 772
  0.7 1.0 %copy-start.10 = (f32[2,4,8,192]{3,2,1,0:T(8,128)S(1)}, f32[2,4,8,192]{3,2,1,0:T(8,128)}, u32[]{:S(2)}) copy-start(f32[2,4,8,192]{3,2,1,0:T(8,128)} %param.8) | copy-start | bytes 147460
  1.5 0.8 %copy-start.9 = (f32[2,4,8,192]{3,2,1,0:T(8,128)S(1)}, f32[2,4,8,192]{3,2,1,0:T(8,128)}, u32[]{:S(2)}) copy-start(f32[2,4,8,192]{3,2,1,0:T(8,128)} %param.9) | copy-start | bytes 147460
  3.0 4.0 %copy-start.8 = (f32[2,4,8,256]{3,2,1,0:T(8,128)}, f32[2,4,8,256]{3,2,1,0:T(8,128)S(1)}, u32[]{:S(2)}) copy-start(f32[2,4,8,256]{3,2,1,0:T(8,128)S(1)} %get-tuple-element.67) | copy-start | bytes 196612
  3.0 1.4 %collective-permute-start = (f32[8,8,256]{2,1,0:T(8,128)S(1)}, f32[8,8,256]{2,1,0:T(8,128)S(1)}, u32[]{:S(2)}, u32[]{:S(2)}) collective-permute-start(f32[8,8,256]{2,1,0:T(8,128)S(1)} %bitcast.23), channel_id=1, source_target_pairs={{1,0},{0,1},{3,2},{2,3},{5,4},{4,5},{7,6},{6,7},{9,8},{8,9},{11,10... | collective-permute-start | bytes 196616 | tf_op jit(solution)/shard_map/ppermute | solution.py:335
  4.4 0.6 copy-start.11
  5.0 24.3 %copy-start.2 = (bf16[4,192,192]{2,1,0:T(8,128)(2,1)S(1)}, bf16[4,192,192]{2,1,0:T(8,128)(2,1)}, u32[]{:S(2)}) copy-start(bf16[4,192,192]{2,1,0:T(8,128)(2,1)} %rest_8_.1) | copy-start | bytes 884740
  7.0 22.2 %copy-start = (bf16[4,192,192]{2,1,0:T(8,128)(2,1)S(1)}, bf16[4,192,192]{2,1,0:T(8,128)(2,1)}, u32[]{:S(2)}) copy-start(bf16[4,192,192]{2,1,0:T(8,128)(2,1)} %rest_9_.1) | copy-start | bytes 884740
  7.0 10.7 %collective-permute-start.3 = (bf16[8,16,256]{2,1,0:T(8,128)(2,1)}, bf16[8,16,256]{2,1,0:T(8,128)(2,1)S(1)}, u32[]{:S(2)}, u32[]{:S(2)}) collective-permute-start(bf16[8,16,256]{2,1,0:T(8,128)(2,1)} %get-tuple-element.14.rest_0_), channel_id=1, source_target_pairs={{24,0},{0,8},{8,16},{16,24},{25,1},{1,9},{9,17},{17,25},{26,2},{2,... | collective-permute-start | bytes 196616 | tf_op jit(solution)/shard_map/ppermute | solution.py:335
  10.0 10.1 %collective-permute-start.2 = (bf16[8,16,256]{2,1,0:T(8,128)(2,1)}, bf16[8,16,256]{2,1,0:T(8,128)(2,1)S(1)}, u32[]{:S(2)}, u32[]{:S(2)}) collective-permute-start(bf16[8,16,256]{2,1,0:T(8,128)(2,1)} %get-tuple-element.14.rest_0_), channel_id=1, source_target_pairs={{16,0},{24,8},{0,16},{8,24},{17,1},{25,9},{1,17},{9,25},{18,2},{26... | collective-permute-start | bytes 196616 | tf_op jit(solution)/shard_map/ppermute | solution.py:335
  12.5 5.2 %collective-permute-start.1 = (bf16[8,16,256]{2,1,0:T(8,128)(2,1)}, bf16[8,16,256]{2,1,0:T(8,128)(2,1)S(1)}, u32[]{:S(2)}, u32[]{:S(2)}) collective-permute-start(bf16[8,16,256]{2,1,0:T(8,128)(2,1)} %get-tuple-element.14.rest_0_), channel_id=1, source_target_pairs={{8,0},{16,8},{24,16},{0,24},{9,1},{17,9},{25,17},{1,25},{10,2},{18... | collective-permute-start | bytes 196616 | tf_op jit(solution)/shard_map/ppermute | solution.py:335
  19.2 0.8 %copy-start.1 = (bf16[8,16,256]{2,1,0:T(8,128)(2,1)S(1)}, bf16[8,16,256]{2,1,0:T(8,128)(2,1)}, u32[]{:S(2)}) copy-start(bf16[8,16,256]{2,1,0:T(8,128)(2,1)} %get-tuple-element.14.rest_0_) | copy-start | bytes 196612
  20.1 9.2 %copy-start.4 = (bf16[8,16,256]{2,1,0:T(8,128)(2,1)S(1)}, bf16[8,16,256]{2,1,0:T(8,128)(2,1)}, u32[]{:S(2)}) copy-start(bf16[8,16,256]{2,1,0:T(8,128)(2,1)} %get-tuple-element.15.rest_6_) | copy-start | bytes 196612
  20.1 9.2 %copy-start.6 = (s32[56,4]{1,0:T(8,128)S(1)}, s32[56,4]{1,0:T(8,128)}, u32[]{:S(2)}) copy-start(s32[56,4]{1,0:T(8,128)} %constant.10.clone.rest_10_) | copy-start | bytes 2692
  20.1 9.2 %copy-start.5 = (f32[8,256]{1,0:T(8,128)S(1)}, f32[8,256]{1,0:T(8,128)}, u32[]{:S(2)}) copy-start(f32[8,256]{1,0:T(8,128)} %get-tuple-element.16.rest_7_.diag_ref) | copy-start | bytes 24580
  20.1 7.3 %collective-permute-start.5 = (bf16[20,16,256]{2,1,0:T(8,128)(2,1)S(1)}, bf16[20,16,256]{2,1,0:T(8,128)(2,1)S(1)}, u32[]{:S(2)}, u32[]{:S(2)}) collective-permute-start(bf16[20,16,256]{2,1,0:T(8,128)(2,1)S(1)} %get-tuple-element.27), channel_id=1, source_target_pairs={{6,0},{0,2},{2,4},{4,6},{7,1},{1,3},{3,5},{5,7},{14,8},{8,10},{10,... | collective-permute-start | bytes 491528 | tf_op jit(solution)/shard_map/ppermute | solution.py:335
  21.7 7.6 %collective-permute-start.4 = (bf16[20,16,256]{2,1,0:T(8,128)(2,1)S(1)}, bf16[20,16,256]{2,1,0:T(8,128)(2,1)S(1)}, u32[]{:S(2)}, u32[]{:S(2)}) collective-permute-start(bf16[20,16,256]{2,1,0:T(8,128)(2,1)S(1)} %get-tuple-element.28), channel_id=1, source_target_pairs={{2,0},{4,2},{6,4},{0,6},{3,1},{5,3},{7,5},{1,7},{10,8},{12,10},{14... | collective-permute-start | bytes 491528 | tf_op jit(solution)/shard_map/ppermute | solution.py:335
  41.7 0.7 %copy-start.3 = (f32[4,8,8,256]{3,2,1,0:T(8,128)}, f32[4,8,8,256]{3,2,1,0:T(8,128)S(1)}, u32[]{:S(2)}) copy-start(f32[4,8,8,256]{3,2,1,0:T(8,128)S(1)} %get-tuple-element.17.keep_ref) | copy-start | bytes 786436
  42.4 1.5 %collective-permute-start.6 = (f32[4,8,8,256]{3,2,1,0:T(8,128)S(1)}, f32[4,8,8,256]{3,2,1,0:T(8,128)S(1)}, u32[]{:S(2)}, u32[]{:S(2)}) collective-permute-start(f32[4,8,8,256]{3,2,1,0:T(8,128)S(1)} %get-tuple-element.18), channel_id=1, source_target_pairs={{1,0},{0,1},{3,2},{2,3},{5,4},{4,5},{7,6},{6,7},{9,8},{8,9},{11,10... | collective-permute-start | bytes 786440 | tf_op jit(solution)/shard_map/ppermute | solution.py:335
  44.0 0.7 %copy-start.7 = (f32[4,8,8,256]{3,2,1,0:T(8,128)}, f32[4,8,8,256]{3,2,1,0:T(8,128)S(1)}, u32[]{:S(2)}) copy-start(f32[4,8,8,256]{3,2,1,0:T(8,128)S(1)} %collective-permute-done.6.got_ref) | copy-start | bytes 786436
  62.8 0.7 %copy-start.14 = (f32[1,128]{1,0:T(1,128)S(1)}, f32[1,128]{1,0:T(1,128)}, u32[]{:S(2)}) copy-start(f32[1,128]{1,0:T(1,128)} %get-tuple-element.24) | copy-start | bytes 1540

commit v2 on v0

--- a/solution.py
+++ b/solution.py
@@ -1,10 +1,535 @@
+import functools
+
 import jax
 import jax.numpy as jnp
+import numpy as np
 from jax import lax
+from jax.experimental import pallas as pl
+from jax.experimental.pallas import tpu as pltpu
 from jax.sharding import PartitionSpec as P
 
 ITERS = 4
 GPB = 8
+LANES = 256
+F32 = jnp.float32
+BF16 = jnp.bfloat16
+VMEM = pl.BlockSpec(memory_space=pltpu.VMEM)
+SMEM = pl.BlockSpec(memory_space=pltpu.SMEM)
+ANY = pl.BlockSpec(memory_space=pl.ANY)
+
+
+def axis_slots(peers, length, depth):
+    reach, following = {}, {}
+    for p in range(-depth, length + depth):
+        key = (p // length) % peers, p % length
+        away = max(0, -p, p - length + 1)
+        reach[key] = min(reach.get(key, away), away)
+        following[key] = ((p + 1) // length) % peers, (p + 1) % length
+    return reach, following
+
+
+class Window:
+    def __init__(self, peers_x, peers_y, len_x, len_y):
+        near_x, next_x = axis_slots(peers_x, len_x, ITERS)
+        near_y, next_y = axis_slots(peers_y, len_y, ITERS)
+        columns = [(near_x[x] + near_y[y], x, y) for x in near_x for y in near_y]
+        columns = sorted(c for c in columns if c[0] <= ITERS)
+        self.depths = [c[0] for c in columns]
+        self.keys = [c[1:] for c in columns]
+        place = {k: i for i, k in enumerate(self.keys)}
+        prev_x = {b: a for a, b in next_x.items()}
+        prev_y = {b: a for a, b in next_y.items()}
+        self.count = [sum(d <= r for d in self.depths) for r in range(ITERS + 1)]
+        self.neighbours = np.array(
+            [
+                (
+                    place[next_x[x], y],
+                    place[x, next_y[y]],
+                    place[prev_x[x], y],
+                    place[x, prev_y[y]],
+                )
+                for x, y in self.keys[: self.count[ITERS - 1]]
+            ],
+            np.int32,
+        )
+        self.x_offsets = sorted({x[0] for x in near_x} - {0})
+        self.y_offsets = sorted({y[0] for y in near_y} - {0})
+        self.y_columns = {o: [k for k in self.keys if k[1][0] == o] for o in self.y_offsets}
+        self.sources = []
+        for x, y in self.keys:
+            if y[0]:
+                at = 1 + len(self.x_offsets) + self.y_offsets.index(y[0])
+                self.sources.append((at, self.y_columns[y[0]].index((x, y))))
+            else:
+                at = 1 + self.x_offsets.index(x[0]) if x[0] else 0
+                self.sources.append((at, x[1] * len_y + y[1]))
+
+
+def lane_iota(shape):
+    return lax.broadcasted_iota(jnp.int32, shape, len(shape) - 1)
+
+
+SIDES = (slice(0, 128), slice(128, 256))
+
+
+def pivot_of(kind, diag_ref, lanes):
+    pivot = jnp.ones((kind.shape[0], 128), F32)
+    for t in range(diag_ref.shape[0]):
+        pivot = jnp.where(kind == t, diag_ref[t : t + 1, lanes], pivot)
+    return pivot
+
+
+def upright(line):
+    n = line.shape[-1]
+    rows = lax.broadcasted_iota(jnp.int32, (n, n), 0)
+    return jnp.sum(jnp.where(rows == lane_iota((n, n)), line, 0.0), axis=1, keepdims=True)
+
+
+def pack_kernel(core_ref, blocks_ref, *refs):
+    own, got = refs[0:4], refs[4:8]
+    hi_ref, lo_ref, diag_ref, wide, notes = refs[8:]
+    dof = blocks_ref.shape[-1]
+    rows = lax.broadcasted_iota(jnp.int32, (dof, dof), 0)
+    eye = (rows == lane_iota((dof, dof))).astype(F32)
+    diag_ref[...] = jnp.ones(diag_ref.shape, F32)
+    for t in range(blocks_ref.shape[0]):
+        diag_ref[t : t + 1, :dof] = jnp.sum(blocks_ref[t].astype(F32) * eye, axis=0, keepdims=True)
+    first = core_ref[0] == 0
+    len_x, len_y, half, kinds_n = own[3].shape
+    lane = lane_iota((half, 128))
+    body_lanes = dof - 128
+    for x in range(len_x):
+        for y in range(len_y):
+            i = x * len_y + y
+            parts = []
+            for h, (body_ref, probe_ref, density_ref, types_ref) in enumerate((own, got)):
+                slot = i * 2 + h
+                wide[slot, :, :dof] = jnp.where(first, body_ref[x, y], probe_ref[x, y])
+                notes[slot, :, :kinds_n] = types_ref[x, y].astype(F32)
+                kinds = notes[slot]
+                kind = kinds[:, kinds_n - 1 : kinds_n]
+                density = upright(density_ref[x, y : y + 1, :])
+                scale = density * jnp.sqrt(density)
+                ship = [(wide[slot, :, lanes] / pivot_of(kind, diag_ref, lanes)) * scale for lanes in SIDES]
+                his = [v.astype(BF16).astype(F32) for v in ship]
+                los = [v - u for v, u in zip(ship, his)]
+                rest = density - density.astype(BF16).astype(F32)
+                note = pltpu.roll(kinds, body_lanes, 1)
+                note = jnp.where(lane == body_lanes + kinds_n, density, note)
+                note = jnp.where(lane == body_lanes + kinds_n + 1, rest, note)
+                note = jnp.where(lane == body_lanes + kinds_n + 2, rest - rest.astype(BF16).astype(F32), note)
+                note = jnp.where(lane < body_lanes + kinds_n + 3, note, 0.0)
+                his[1] = jnp.where(lane < body_lanes, his[1], note)
+                los[1] = jnp.where(lane < body_lanes, los[1], 0.0)
+                parts.append((his, los))
+            for side, lanes in enumerate(SIDES):
+                hi_ref[i, :, lanes] = jnp.concatenate([p[0][side] for p in parts], axis=0).astype(BF16)
+                lo_ref[i, :, lanes] = jnp.concatenate([p[1][side] for p in parts], axis=0).astype(BF16)
+
+
+def assemble_kernel(copies, count_in, *refs):
+    sem = refs[-1]
+    ins, outs = refs[:count_in], refs[count_in:-1]
+    started = []
+    for out, lines in zip(outs, copies):
+        for to, (at, j, n) in lines:
+            copy = pltpu.make_async_copy(ins[at].at[pl.ds(j, n)], out.at[pl.ds(to, n)], sem.at[len(started)])
+            copy.start()
+            started.append(copy)
+    for copy in started:
+        copy.wait()
+
+
+def divisor(n, cap):
+    return max(d for d in range(1, cap + 1) if n % d == 0)
+
+
+def sweep_kernel(window, refs_in, *rest):
+    pieces = rest[:refs_in]
+    (lo_ref, diag_ref, off_ref, self_ref, near_ref, keep_ref, send_ref) = rest[refs_in : refs_in + 7]
+    (ship_a, ship_b, own_a, own_b, kinds, kinds_16, gain, scale, up_w, low_w, lhs, leave, sem) = rest[refs_in + 7 :]
+    dof = off_ref.shape[-1]
+    kinds_n = off_ref.shape[0]
+    depth = ship_a.shape[1]
+    half = depth // 2
+    own = window.count[0]
+    targets = window.count[ITERS - 1]
+    up_w[...] = jnp.zeros(up_w.shape, BF16)
+    low_w[...] = jnp.zeros(low_w.shape, BF16)
+    for t in range(kinds_n):
+        up_w[:dof, t * LANES : t * LANES + dof] = off_ref[t]
+        low_w[t * LANES : t * LANES + dof, :dof] = off_ref[t]
+        low_w[(kinds_n + t) * LANES : (kinds_n + t) * LANES + dof, :dof] = self_ref[t]
+    for i, (at, j) in enumerate(window.sources):
+        ship_a[i] = pieces[at][j]
+        if i < own:
+            own_a[i] = pieces[at][j].astype(F32) + lo_ref[j].astype(F32)
+    spread_rows = lax.broadcasted_iota(jnp.int32, (128, 8 * 128), 0) - (dof - 128)
+    spread_cols = lane_iota((128, 8 * 128)) // 128
+    spread = (jnp.minimum(spread_rows, 7) == spread_cols) & (spread_rows >= 0) & (spread_rows < 10)
+    spread = spread.astype(BF16)
+    batch = divisor(targets, 8)
+    for c in range(targets // batch):
+        lines = [pieces[at][j, :, 128:] for at, j in window.sources[c * batch : (c + 1) * batch]]
+        found = jnp.dot(jnp.concatenate(lines, axis=0), spread, preferred_element_type=F32)
+        for u in range(batch):
+            i = c * batch + u
+            part = found[u * depth : (u + 1) * depth]
+            for k in range(7):
+                if i < own:
+                    kinds[i, k] = part[:, k * 128 : (k + 1) * 128]
+                else:
+                    kinds_16[i, k] = part[:, k * 128 : (k + 1) * 128].astype(BF16)
+            density = part[:, 7 * 128 :]
+            s = density * jnp.sqrt(density)
+            if i < own:
+                scale[i] = s
+            for lanes in SIDES:
+                gain[i, :, lanes] = s * s / pivot_of(part[:, 6 * 128 : 7 * 128], diag_ref, lanes)
+
+    def build(get, kind, i, table, row, low_row):
+        for side, lanes in enumerate(SIDES):
+            mine = get(i, lanes)
+            wide = mine.astype(F32)
+            zero = jnp.zeros((), mine.dtype)
+            nears = [
+                get(table[0], lanes),
+                get(table[1], lanes),
+                pltpu.roll(wide, depth - 1, 0).astype(mine.dtype),
+                get(table[2], lanes),
+                get(table[3], lanes),
+                pltpu.roll(wide, 1, 0).astype(mine.dtype),
+                mine,
+            ]
+            for t in range(kinds_n):
+                for g, ks in enumerate(((0, 1, 2), (3, 4, 5), (6,))):
+                    total = None
+                    for k in ks:
+                        term = jnp.where(kind[i, k] == jnp.asarray(t, mine.dtype), nears[k], zero)
+                        total = term if total is None else total + term
+                    at = (g * kinds_n + t) * LANES + side * 128
+                    hi = total.astype(BF16)
+                    lhs[row : row + depth, at : at + 128] = hi
+                    if low_row is not None:
+                        lhs[low_row : low_row + depth, at : at + 128] = (total - hi.astype(F32)).astype(BF16)
+
+    def product(start, stop):
+        n = kinds_n * LANES
+        acc = lax.dot_general(
+            lhs[start:stop, :n], up_w[...], (((1,), (1,)), ((), ())), preferred_element_type=F32
+        )
+        return acc + jnp.dot(lhs[start:stop, n:], low_w[...], preferred_element_type=F32)
+
+    base = 2 * own * depth
+    copies = []
+    for step in range(ITERS):
+        src, dst = (ship_b, ship_a) if step % 2 else (ship_a, ship_b)
+        src_own, dst_own = (own_b, own_a) if step % 2 else (own_a, own_b)
+
+        def get_own(i, lanes):
+            if i < own:
+                return src_own[i, :, lanes]
+            return src[i, :, lanes].astype(F32)
+
+        for u in range(own):
+            table = [int(n) for n in window.neighbours[u]]
+            build(get_own, kinds, u, table, u * depth, (own + u) * depth)
+        acc = product(0, base)
+        for u in range(own):
+            both = acc[u * depth : (u + 1) * depth] + acc[(own + u) * depth : (own + u + 1) * depth]
+            for lanes in SIDES:
+                value = both[:, lanes] * scale[u]
+                keep_ref[step, u, :, lanes] = value[:half]
+                leave[step, u, :, lanes] = value[half:]
+            if step < ITERS - 1:
+                value = both * gain[u]
+                dst_own[u] = value
+                dst[u] = value.astype(BF16)
+        copy = pltpu.make_async_copy(leave.at[step], send_ref.at[step], sem.at[step])
+        copy.start()
+        copies.append(copy)
+        halo = window.count[ITERS - 1 - step] - own
+        if halo:
+            batch = divisor(halo, 14)
+
+            def one(c, carry):
+                first = own + c * batch
+                for u in range(batch):
+                    table = [near_ref[first + u, k] for k in range(4)]
+                    build(lambda i, lanes: src[i, :, lanes], kinds_16, first + u, table, base + u * depth, None)
+                acc = product(base, base + batch * depth)
+                for u in range(batch):
+                    dst[first + u] = (acc[u * depth : (u + 1) * depth] * gain[first + u]).astype(BF16)
+                return carry
+
+            lax.fori_loop(0, halo // batch, one, 0)
+    for copy in copies:
+        copy.wait()
+
+
+def gram_index(i, j):
+    i, j = min(i, j), max(i, j)
+    return i * (ITERS + 1) - i * (i - 1) // 2 + j - i
+
+
+GRAM = (ITERS + 1) * (ITERS + 2) // 2
+
+
+def moments_kernel(core_ref, body_ref, probe_ref, density_ref, types_ref, owner_ref, keep_ref, diag_ref, back_ref,
+                   message_ref, state_ref, adjoint_ref, got, wide, sem):
+    arrive = pltpu.make_async_copy(back_ref, got, sem)
+    arrive.start()
+    len_x, len_y, half, dof = body_ref.shape
+    kinds_n = diag_ref.shape[0]
+    first = core_ref[0] == 0
+    lane = lane_iota((half, 128))
+    sums = [[None] * GRAM, [None] * GRAM]
+    terms, dens, dests = [], [], []
+    dest_lane = lane_iota((half, message_ref.shape[0]))
+    wide[:, :, 128:] = jnp.zeros(wide.shape[:2] + (128,), F32)
+    for x in range(len_x):
+        for y in range(len_y):
+            i = x * len_y + y
+            wide[2 * i, :, :dof] = body_ref[x, y]
+            wide[2 * i + 1, :, :dof] = probe_ref[x, y]
+    arrive.wait()
+    for x in range(len_x):
+        for y in range(len_y):
+            i = x * len_y + y
+            kind = types_ref[x, y][:, 6:7].astype(F32)
+            density = upright(density_ref[x, y : y + 1, :])
+            owner = upright(owner_ref[x, y : y + 1, :].astype(F32)).astype(jnp.int32)
+            inside = lax.rem(owner, GPB)
+            products = [None] * (ITERS * ITERS)
+            for side, lanes in enumerate(SIDES):
+                inverse = 1.0 / pivot_of(kind, diag_ref, lanes)
+                state, adjoint = [wide[2 * i, :, lanes]], [wide[2 * i + 1, :, lanes]]
+                for k in range(ITERS):
+                    a, b = keep_ref[k, i, :, lanes], got[k, i, :, lanes]
+                    state.append(jnp.where(first, a, b))
+                    adjoint.append(jnp.where(first, b, a))
+                for f, v in enumerate((state, adjoint)):
+                    for p in range(ITERS + 1):
+                        for q in range(p, ITERS + 1):
+                            n = gram_index(p, q)
+                            term = v[p] * v[q]
+                            sums[f][n] = term if sums[f][n] is None else sums[f][n] + term
+                pre_s = [v * inverse for v in state[:ITERS]]
+                pre_a = [v * inverse for v in adjoint[:ITERS]]
+                for k in range(ITERS):
+                    state_ref[k, i, :, lanes] = pre_s[k]
+                    adjoint_ref[k, i, :, lanes] = pre_a[k]
+                    for j in range(ITERS):
+                        term = pre_a[k] * state[j + 1] + pre_s[j] * adjoint[k + 1]
+                        n = k * ITERS + j
+                        products[n] = term if products[n] is None else products[n] + term
+            spread = jnp.zeros((half, 128), F32)
+            for n in range(ITERS * ITERS):
+                spread = jnp.where(lane // GPB == n, jnp.sum(products[n], axis=1, keepdims=True), spread)
+            hit = lane % GPB == inside
+            terms.append(jnp.where(hit, spread, 0.0))
+            dens.append(jnp.where(hit & (lane < GPB), density, 0.0))
+            dests.append((lax.div(owner, GPB) == dest_lane).astype(F32))
+    right = jnp.concatenate([jnp.concatenate(terms, axis=0), jnp.concatenate(dens, axis=0)], axis=1)
+    left = jnp.concatenate(dests, axis=0)
+    message = lax.dot_general(
+        left, right, (((0,), (0,)), ((), ())), preferred_element_type=F32, precision=lax.Precision.HIGHEST
+    )
+    line = lane_iota((1, 128))
+    row = jnp.zeros((1, 128), F32)
+    for f in range(2):
+        for n in range(GRAM):
+            total = jnp.sum(jnp.sum(sums[f][n], axis=0, keepdims=True), axis=1, keepdims=True)
+            row = jnp.where(line == 16 + 32 * f + n, total, row)
+    second = message[:, 128:] + row
+    for d in range(message_ref.shape[0]):
+        message_ref[d, 0:1, :] = message[d : d + 1, :128]
+        message_ref[d, 1:2, :] = second[d : d + 1]
+
+
+def finish_kernel(message_ref, pre_state_ref, pre_adjoint_ref, state_ref, adjoint_ref, coarse_ref, out_s, out_a, out_c,
+                  sem):
+    total = jnp.sum(message_ref[...], axis=0)
+    sums = total[1:2]
+    rows = lax.broadcasted_iota(jnp.int32, (8, 128), 0)
+    both = jnp.broadcast_to(sums, (8, 128))
+    both = jnp.where(rows < 4, both, pltpu.roll(both, 128 - 32, 1))
+    gram = [jnp.broadcast_to(both[:, 16 + n : 17 + n], (8, 128)) for n in range(GRAM)]
+
+    def inner(c, d):
+        out = None
+        for p, u in enumerate(c):
+            part = None
+            for q, v in enumerate(d):
+                if u is not None and v is not None:
+                    term = v * gram[gram_index(p, q)]
+                    part = term if part is None else part + term
+            if part is not None:
+                out = u * part if out is None else out + u * part
+        return out
+
+    c = [jnp.ones((8, 128), F32)] + [None] * ITERS
+    beta = [None] * ITERS
+    for sweep in range(ITERS):
+        w = [None] + c[:ITERS]
+        step = inner(c, w) / (inner(w, w) + 1e-06)
+        for k in range(ITERS):
+            if c[k] is not None:
+                beta[k] = step * c[k] if beta[k] is None else beta[k] + step * c[k]
+        moved = []
+        for k in range(ITERS + 1):
+            if w[k] is None:
+                moved.append(c[k])
+            else:
+                moved.append(-step * w[k] if c[k] is None else c[k] - step * w[k])
+        c = moved
+    dof = out_s.shape[-1]
+    copies = []
+    weights = []
+    for f, (pre, out, to) in enumerate(((pre_state_ref, out_s, state_ref), (pre_adjoint_ref, out_a, adjoint_ref))):
+        weight = [b[4 * f : 4 * f + 1] for b in beta]
+        weights.append(weight)
+        for lanes in (slice(0, 128), slice(128, dof)):
+            width = lanes.stop - lanes.start
+            value = pre[0, :, :, lanes] * weight[0][:, :width]
+            for k in range(1, ITERS):
+                value = value + pre[k, :, :, lanes] * weight[k][:, :width]
+            out[:, :, lanes] = value
+        copy = pltpu.make_async_copy(out, to, sem.at[f])
+        copy.start()
+        copies.append(copy)
+    lane = lane_iota((1, 128))
+    factor = jnp.zeros((1, 128), F32)
+    for k in range(ITERS):
+        for j in range(ITERS):
+            factor = jnp.where(lane // GPB == k * ITERS + j, weights[1][k] * weights[0][j], factor)
+    folded = total[0:1] * factor
+    for shift in (64, 32, 16, 8):
+        folded = folded + pltpu.roll(folded, shift, 1)
+    out_c[...] = (-1.5 * folded / jnp.where(lane < GPB, sums, 1.0))[:, :GPB]
+    copy = pltpu.make_async_copy(out_c, coarse_ref, sem.at[2])
+    copy.start()
+    for copy in copies + [copy]:
+        copy.wait()
+
+
+def shifted(array, axis, offset):
+    peers = lax.axis_size(axis)
+    return lax.ppermute(array, axis, [((i + offset) % peers, i) for i in range(peers)])
+
+
+def runs(lines):
+    out = []
+    for to, (at, j) in enumerate(lines):
+        if out and out[-1][1][0] == at and out[-1][1][1] + out[-1][1][2] == j:
+            out[-1] = (out[-1][0], (at, out[-1][1][1], out[-1][1][2] + 1))
+        else:
+            out.append((to, (at, j, 1)))
+    return out
+
+
+def by_field(body_load, probe_load, density, link_types, off_blocks, self_blocks, block_owner):
+    len_x, len_y, half, dof = body_load.shape
+    cols = len_x * len_y
+    depth = 2 * half
+    kinds_n = off_blocks.shape[0]
+    window = Window(lax.axis_size("gx"), lax.axis_size("gy"), len_x, len_y)
+    core = lax.axis_index("gz").reshape(1)
+    mine = (body_load, probe_load, density, link_types)
+    theirs = tuple(shifted(a, "gz", 1) for a in mine)
+    hi, lo, diag = pl.pallas_call(
+        pack_kernel,
+        out_shape=(
+            jax.ShapeDtypeStruct((cols, depth, LANES), BF16),
+            jax.ShapeDtypeStruct((cols, depth, LANES), BF16),
+            jax.ShapeDtypeStruct((kinds_n, LANES), F32),
+        ),
+        in_specs=[SMEM] + [VMEM] * 9,
+        out_specs=(VMEM,) * 3,
+        scratch_shapes=[pltpu.VMEM((2 * cols, half, LANES), F32), pltpu.VMEM((2 * cols, half, 128), F32)],
+        name="pack",
+    )(core, self_blocks, *mine, *theirs)
+    from_x = [hi] + [shifted(hi, "gx", o) for o in window.x_offsets]
+    copies = []
+    for o in window.y_offsets:
+        lines = []
+        for x, y in window.y_columns[o]:
+            lines.append((1 + window.x_offsets.index(x[0]) if x[0] else 0, x[1] * len_y + y[1]))
+        copies.append(runs(lines))
+    messages = pl.pallas_call(
+        functools.partial(assemble_kernel, copies, len(from_x)),
+        out_shape=tuple(
+            jax.ShapeDtypeStruct((len(window.y_columns[o]), depth, LANES), BF16) for o in window.y_offsets
+        ),
+        in_specs=[ANY] * len(from_x),
+        out_specs=(ANY,) * len(copies),
+        scratch_shapes=[pltpu.SemaphoreType.DMA((sum(len(c) for c in copies),))],
+        name="assemble",
+    )(*from_x)
+    pieces = from_x + [shifted(m, "gy", o) for m, o in zip(messages, window.y_offsets)]
+    own = window.count[0]
+    targets = window.count[ITERS - 1]
+    rows = depth * (2 * own + 14)
+    keep, send = pl.pallas_call(
+        functools.partial(sweep_kernel, window, len(pieces)),
+        out_shape=(jax.ShapeDtypeStruct((ITERS, cols, half, LANES), F32),) * 2,
+        in_specs=[VMEM] * (len(pieces) + 4) + [SMEM],
+        out_specs=(VMEM, ANY),
+        scratch_shapes=[
+            pltpu.VMEM((window.count[ITERS], depth, LANES), BF16),
+            pltpu.VMEM((targets, depth, LANES), BF16),
+            pltpu.VMEM((own, depth, LANES), F32),
+            pltpu.VMEM((own, depth, LANES), F32),
+            pltpu.VMEM((own, 7, depth, 128), F32),
+            pltpu.VMEM((targets, 7, depth, 128), BF16),
+            pltpu.VMEM((targets, depth, LANES), F32),
+            pltpu.VMEM((own, depth, 128), F32),
+            pltpu.VMEM((LANES, kinds_n * LANES), BF16),
+            pltpu.VMEM((2 * kinds_n * LANES, LANES), BF16),
+            pltpu.VMEM((rows, 3 * kinds_n * LANES), BF16),
+            pltpu.VMEM((ITERS, cols, half, LANES), F32),
+            pltpu.SemaphoreType.DMA((ITERS,)),
+        ],
+        compiler_params=pltpu.CompilerParams(vmem_limit_bytes=40 * 2**20),
+        name="sweeps",
+    )(*pieces, lo, diag, off_blocks, self_blocks, jnp.asarray(window.neighbours))
+    back = shifted(send, "gz", 1)
+    owners = lax.axis_size("gx") * lax.axis_size("gy") * lax.axis_size("gz")
+    message, pre_state, pre_adjoint = pl.pallas_call(
+        moments_kernel,
+        out_shape=(
+            jax.ShapeDtypeStruct((owners, 2, 128), F32),
+            jax.ShapeDtypeStruct((ITERS, cols, half, LANES), F32),
+            jax.ShapeDtypeStruct((ITERS, cols, half, LANES), F32),
+        ),
+        in_specs=[SMEM] + [VMEM] * 7 + [ANY],
+        out_specs=(VMEM,) * 3,
+        scratch_shapes=[
+            pltpu.VMEM((ITERS, cols, half, LANES), F32),
+            pltpu.VMEM((2 * cols, half, LANES), F32),
+            pltpu.SemaphoreType.DMA,
+        ],
+        name="moments",
+    )(core, body_load, probe_load, density, link_types, block_owner, keep, diag, back)
+    message = lax.all_to_all(message, ("gx", "gy", "gz"), 0, 0, tiled=True)
+    state, adjoint, coarse = pl.pallas_call(
+        finish_kernel,
+        out_shape=(
+            jax.ShapeDtypeStruct((cols, half, dof), F32),
+            jax.ShapeDtypeStruct((cols, half, dof), F32),
+            jax.ShapeDtypeStruct((1, GPB), F32),
+        ),
+        in_specs=[VMEM] * 3,
+        out_specs=(ANY,) * 3,
+        scratch_shapes=[
+            pltpu.VMEM((cols, half, dof), F32),
+            pltpu.VMEM((cols, half, dof), F32),
+            pltpu.VMEM((1, GPB), F32),
+            pltpu.SemaphoreType.DMA((3,)),
+        ],
+        name="finish",
+    )(message, pre_state, pre_adjoint)
+    return state.reshape(body_load.shape), adjoint.reshape(body_load.shape), coarse.reshape(GPB)
 
 
 def with_halo(array, sides, width):
@@ -58,7 +583,7 @@
     return accumulated * stiff_scale[None, :, :, :, None]
 
 
-def local(body_load, probe_load, density, link_types, off_blocks, self_blocks, block_owner):
+def by_sweep(body_load, probe_load, density, link_types, off_blocks, self_blocks, block_owner):
     dof_count = body_load.shape[-1]
     type_count = off_blocks.shape[0]
     self_count = self_blocks.shape[0]
@@ -120,4 +645,8 @@
         P("gx", "gy", "gz"),
     )
     out_specs = (P("gx", "gy", "gz", None), P("gx", "gy", "gz", None), P(("gx", "gy", "gz")))
+    def local(*arrays):
+        split = lax.axis_size("gz") == 2 and arrays[0].shape[2] % 8 == 0
+        return (by_field if split else by_sweep)(*arrays)
+
     return jax.shard_map(local, mesh=mesh, in_specs=in_specs, out_specs=out_specs, check_vma=False)

time: 321 us -> 75.7 us (0.24)
  blocking collectives: 213 us -> 10.5 us
  starting transfers between devices: 66 us -> 10.4 us
  Pallas kernels: 0 us -> 32.2 us
  matrix products: 9.28 us -> 0 us
  local copies, waits for them, and re-layouts: 14.6 us -> 6.43 us
  other arithmetic: 4.76 us -> 0 us
  waiting for transfers between devices: 10.3 us -> 14.9 us
    psum x4 -> x0, blocking collectives: 172 us -> none  [local(): projected, energy = lax.psum((projected, energy), ('gx', 'gy', 'gz'))]
    ppermute x24 -> x10, starting transfers between devices: 66 us -> 10.4 us  [shifted(): lax.ppermute(array, axis, [((i + offset) % peers, i) for i in range(peers)])]
    unnamed x1 -> x0, blocking collectives: 41 us -> none
    pallas_call x0 -> x5, Pallas kernels: none -> 32.2 us  [the longest x1 13.1 us: by_field(): pl.pallas_call(functools.partial(sweep_kernel, window, len(pieces)), out_...]
    all_to_all x0 -> x1, blocking collectives: none -> 10.5 us  [by_field(): message = lax.all_to_all(message, ('gx', 'gy', 'gz'), 0, 0, tiled=True)]
    dot_general x28 -> x0, matrix products: 9.28 us -> none  [typed_product(): jnp.dot(flattened, block_table, preferred_element_type=jnp.float32)]
    gather x1 -> x0, local copies, waits for them, and re-layouts: 5.32 us -> none  [local(): diagonals = jnp.diagonal(self_blocks, axis1=1, axis2=2).astype(jnp.float32)]
    ppermute x24 -> x10, waiting for transfers between devices: 10.3 us -> 14.9 us  [shifted(): lax.ppermute(array, axis, [((i + offset) % peers, i) for i in range(peers)])]
  transfers between devices with their start and end apart: 24 -> 10, of which waited for: 12 -> 7; matrix products, arithmetic and copies ran while one was open for 2% -> 1% of each run, Pallas kernels for 0% -> 0%
where the time goes in v2:
time: 75.7 us; the launch traced here: 75.3 us
  Pallas kernels  32.2 us (43%)
  waiting for transfers between devices  14.9 us (20%)
  blocking collectives  10.5 us (14%)
  starting transfers between devices  10.4 us (14%)
  local copies, waits for them, and re-layouts  6.43 us (8%)
  between operations  0.78 us (1%)
    ppermute x10, waiting for transfers between devices, shifted(): lax.ppermute(array, axis, [((i + offset) % peers, i) for i in range(peers)])  14.9 us
    pallas_call x1, Pallas kernels, by_field(): pl.pallas_call(functools.partial(sweep_kernel, window, len(pieces)), out_...  13.1 us
    pallas_call x1, Pallas kernels, by_field(): pl.pallas_call(functools.partial(assemble_kernel, copies, len(from_x)), o...  11.4 us
    all_to_all x1, blocking collectives, by_field(): message = lax.all_to_all(message, ('gx', 'gy', 'gz'), 0, 0, tiled=True)  10.5 us
    ppermute x10, starting transfers between devices, shifted(): lax.ppermute(array, axis, [((i + offset) % peers, i) for i in range(peers)])  10.4 us
    unnamed x41, local copies, waits for them, and re-layouts  6.43 us
    pallas_call x1, Pallas kernels, by_field(): pl.pallas_call(moments_kernel, out_shape=(jax.ShapeDtypeStruct((owners, 2...  3.42 us
    pallas_call x1, Pallas kernels, by_field(): pl.pallas_call(pack_kernel, out_shape=(jax.ShapeDtypeStruct((cols, depth,...  2.23 us
  transfers between devices with their start and end apart: 10, of which 7 were waited for; matrix products, arithmetic and copies ran while one was open for 1% of the time, Pallas kernels for 0%

profile of v2, /device:TPU:0, one launch (start us, length us, event | category | flops | bytes accessed | tf_op | source)
XLA Modules:
  0.0 75.3 jit_solution(3343006537412933299)
XLA Ops:
  1.2 0.9 %copy.13.refs_3_.types_ref = s32[2,4,8,7]{3,2,1,0:T(8,128)S(1)} copy(s32[2,4,8,7]{2,1,3,0:T(4,128)} %param.11) | data formatting | bytes 3584 | tf_op args[3]
  2.7 1.1 %collective-permute-done.2.refs_6_ = f32[2,4,8]{2,1,0:T(4,128)S(1)} collective-permute-done((f32[2,4,8]{2,1,0:T(4,128)S(1)}, f32[2,4,8]{2,1,0:T(4,128)S(1)}, u32[]{:S(2)}, u32[]{:S(2)}) %collective-permute-start.2) | collective-permute-done | bytes 288 | tf_op jit(solution)/shard_map/ppermute | solution.py:418
  3.8 0.5 copy-done.19
  4.4 2.2 %pack.1 = (bf16[8,16,256]{2,1,0:T(8,128)(2,1)}, bf16[8,16,256]{2,1,0:T(8,128)(2,1)}, f32[4,256]{1,0:T(4,128)}) custom-call(s32[1]{0:T(128)} %bitcast.core_ref, bf16[4,192,192]{2,1,0:T(8,128)(2,1)} %rest_9_.1, f32[2,4,8,192]{3,2,1,0:T(8,128)} %body_ref.1, f32[2,4,8,192]{3,2,1,0:T(8,128)} %probe_ref.1, f32[2,4,8]{2,1,0:T(4,128)} %density_ref.1, ...), custom_call_target="tpu_custom_call" | custom-call | tf_op jit(solution)/shard_map/pack/pallas_call | solution.py:440
  6.7 2.8 %collective-permute-start.6 = (bf16[8,16,256]{2,1,0:T(8,128)(2,1)}, bf16[8,16,256]{2,1,0:T(8,128)(2,1)S(1)}, u32[]{:S(2)}, u32[]{:S(2)}) collective-permute-start(bf16[8,16,256]{2,1,0:T(8,128)(2,1)} %get-tuple-element.16.refs_0_.rest_0_), channel_id=1, source_target_pairs={{24,0},{0,8},{8,16},{16,24},{25,1},{1,9},{9,17},{17,25},{26,2},{2,... | collective-permute-start | bytes 196616 | tf_op jit(solution)/shard_map/ppermute | solution.py:418
  9.5 2.6 %collective-permute-start.5 = (bf16[8,16,256]{2,1,0:T(8,128)(2,1)}, bf16[8,16,256]{2,1,0:T(8,128)(2,1)S(1)}, u32[]{:S(2)}, u32[]{:S(2)}) collective-permute-start(bf16[8,16,256]{2,1,0:T(8,128)(2,1)} %get-tuple-element.16.refs_0_.rest_0_), channel_id=1, source_target_pairs={{16,0},{24,8},{0,16},{8,24},{17,1},{25,9},{1,17},{9,25},{18,2},{26... | collective-permute-start | bytes 196616 | tf_op jit(solution)/shard_map/ppermute | solution.py:418
  12.0 1.3 %collective-permute-start.4 = (bf16[8,16,256]{2,1,0:T(8,128)(2,1)}, bf16[8,16,256]{2,1,0:T(8,128)(2,1)S(1)}, u32[]{:S(2)}, u32[]{:S(2)}) collective-permute-start(bf16[8,16,256]{2,1,0:T(8,128)(2,1)} %get-tuple-element.16.refs_0_.rest_0_), channel_id=1, source_target_pairs={{8,0},{16,8},{24,16},{0,24},{9,1},{17,9},{25,17},{1,25},{10,2},{18... | collective-permute-start | bytes 196616 | tf_op jit(solution)/shard_map/ppermute | solution.py:418
  13.4 1.1 %collective-permute-done.6.refs_3_.rest_3_ = bf16[8,16,256]{2,1,0:T(8,128)(2,1)S(1)} collective-permute-done((bf16[8,16,256]{2,1,0:T(8,128)(2,1)}, bf16[8,16,256]{2,1,0:T(8,128)(2,1)S(1)}, u32[]{:S(2)}, u32[]{:S(2)}) %collective-permute-start.6) | collective-permute-done | bytes 65568 | tf_op jit(solution)/shard_map/ppermute | solution.py:418
  14.5 2.7 %collective-permute-done.5.refs_2_.rest_2_ = bf16[8,16,256]{2,1,0:T(8,128)(2,1)S(1)} collective-permute-done((bf16[8,16,256]{2,1,0:T(8,128)(2,1)}, bf16[8,16,256]{2,1,0:T(8,128)(2,1)S(1)}, u32[]{:S(2)}, u32[]{:S(2)}) %collective-permute-start.5) | collective-permute-done | bytes 65568 | tf_op jit(solution)/shard_map/ppermute | solution.py:418
  17.8 0.6 copy-done.8
  18.4 11.4 %assemble.1 = (bf16[20,16,256]{2,1,0:T(8,128)(2,1)}, bf16[20,16,256]{2,1,0:T(8,128)(2,1)}) custom-call(bf16[8,16,256]{2,1,0:T(8,128)(2,1)} %get-tuple-element.16.refs_0_.rest_0_, bf16[8,16,256]{2,1,0:T(8,128)(2,1)} %copy-done.8, bf16[8,16,256]{2,1,0:T(8,128)(2,1)} %copy-done.6, bf16[8,16,256]{2,1,0:T(8,128)(2,1)} %copy-done.4), custom_call_target="tpu_custom_call" | custom-call | tf_op jit(solution)/shard_map/assemble/pallas_call | solution.py:459
  29.9 2.5 %collective-permute-start.7 = (bf16[20,16,256]{2,1,0:T(8,128)(2,1)}, bf16[20,16,256]{2,1,0:T(8,128)(2,1)S(1)}, u32[]{:S(2)}, u32[]{:S(2)}) collective-permute-start(bf16[20,16,256]{2,1,0:T(8,128)(2,1)} %get-tuple-element.17), channel_id=1, source_target_pairs={{2,0},{4,2},{6,4},{0,6},{3,1},{5,3},{7,5},{1,7},{10,8},{12,10},{14... | collective-permute-start | bytes 491528 | tf_op jit(solution)/shard_map/ppermute | solution.py:418
  32.4 4.9 %collective-permute-done.7.rest_4_ = bf16[20,16,256]{2,1,0:T(8,128)(2,1)S(1)} collective-permute-done((bf16[20,16,256]{2,1,0:T(8,128)(2,1)}, bf16[20,16,256]{2,1,0:T(8,128)(2,1)S(1)}, u32[]{:S(2)}, u32[]{:S(2)}) %collective-permute-start.7) | collective-permute-done | bytes 163872 | tf_op jit(solution)/shard_map/ppermute | solution.py:418
  37.3 3.4 %collective-permute-done.8.rest_5_ = bf16[20,16,256]{2,1,0:T(8,128)(2,1)S(1)} collective-permute-done((bf16[20,16,256]{2,1,0:T(8,128)(2,1)}, bf16[20,16,256]{2,1,0:T(8,128)(2,1)S(1)}, u32[]{:S(2)}, u32[]{:S(2)}) %collective-permute-start.8) | collective-permute-done | bytes 163872 | tf_op jit(solution)/shard_map/ppermute | solution.py:418
  40.7 0.8 %copy-done.5 = bf16[8,16,256]{2,1,0:T(8,128)(2,1)S(1)} copy-done((bf16[8,16,256]{2,1,0:T(8,128)(2,1)S(1)}, bf16[8,16,256]{2,1,0:T(8,128)(2,1)}, u32[]{:S(2)}) %copy-start.5) | copy-done | bytes 65560
  41.5 0.8 %copy-done.7 = bf16[8,16,256]{2,1,0:T(8,128)(2,1)S(1)} copy-done((bf16[8,16,256]{2,1,0:T(8,128)(2,1)S(1)}, bf16[8,16,256]{2,1,0:T(8,128)(2,1)}, u32[]{:S(2)}) %copy-start.7) | copy-done | bytes 65560
  42.4 0.8 %copy-done.9 = bf16[8,16,256]{2,1,0:T(8,128)(2,1)S(1)} copy-done((bf16[8,16,256]{2,1,0:T(8,128)(2,1)S(1)}, bf16[8,16,256]{2,1,0:T(8,128)(2,1)}, u32[]{:S(2)}) %copy-start.9) | copy-done | bytes 65560
  43.2 13.1 %sweeps.1 = (f32[4,8,8,256]{3,2,1,0:T(8,128)S(1)}, f32[4,8,8,256]{3,2,1,0:T(8,128)S(1)}) custom-call(bf16[8,16,256]{2,1,0:T(8,128)(2,1)S(1)} %copy-done.3, bf16[8,16,256]{2,1,0:T(8,128)(2,1)S(1)} %copy-done.9, bf16[8,16,256]{2,1,0:T(8,128)(2,1)S(1)} %copy-done.7, bf16[8,16,256]{2,1,0:T(8,128)(2,1)S(1)} %copy-done.5, ...), custom_call_target="tpu_custom_call" | custom-call | tf_op jit(solution)/shard_map/sweeps/pallas_call | solution.py:473
  56.3 0.7 copy-done.2
  57.0 1.5 %collective-permute-done.9.back_ref = f32[4,8,8,256]{3,2,1,0:T(8,128)S(1)} collective-permute-done((f32[4,8,8,256]{3,2,1,0:T(8,128)S(1)}, f32[4,8,8,256]{3,2,1,0:T(8,128)S(1)}, u32[]{:S(2)}, u32[]{:S(2)}) %collective-permute-start.9) | collective-permute-done | bytes 262176 | tf_op jit(solution)/shard_map/ppermute | solution.py:418
  58.5 0.7 copy-done.14
  59.2 3.4 %moments.1 = (f32[32,2,128]{2,1,0:T(2,128)}, f32[4,8,8,256]{3,2,1,0:T(8,128)}, f32[4,8,8,256]{3,2,1,0:T(8,128)}) custom-call(s32[1]{0:T(128)} %bitcast.core_ref, f32[2,4,8,192]{3,2,1,0:T(8,128)} %body_ref.1, f32[2,4,8,192]{3,2,1,0:T(8,128)} %probe_ref.1, f32[2,4,8]{2,1,0:T(4,128)} %density_ref.1, s32[2,4,8,7]{3,2,1,0:T(8,128)} %copy-done.13, ...), custom_call_target="tpu_custom_call" | custom-call | tf_op jit(solution)/shard_map/moments/pallas_call | solution.py:498
  62.7 10.5 %all_to_all.5.message_ref = f32[32,2,128]{2,1,0:T(2,128)} all-to-all(f32[32,2,128]{2,1,0:T(2,128)} %get-tuple-element.23), channel_id=1, replica_groups=mesh['gx'=4,'gy'=4,'gz'=2] {'gx','gy','gz'}, dimensions={0} | all-to-all | bytes 65536 | tf_op jit(solution)/shard_map/all_to_all | solution.py:514
  73.2 2.1 %finish.1 = (f32[8,8,192]{2,1,0:T(8,128)}, f32[8,8,192]{2,1,0:T(8,128)}, f32[1,8]{1,0:T(1,128)}) custom-call(f32[32,2,128]{2,1,0:T(2,128)} %all_to_all.5.message_ref, f32[4,8,8,256]{3,2,1,0:T(8,128)} %get-tuple-element.24.pre_state_ref, f32[4,8,8,256]{3,2,1,0:T(8,128)} %get-tuple-element.25.pre_adjoint_ref), custom_call_target="tpu_custom_call" | custom-call | tf_op jit(solution)/shard_map/finish/pallas_call | solution.py:515
  (43 shorter events, 1.9 us)
Async XLA Ops:
  0.6 1.9 %copy-start.18 = (f32[2,4,8]{2,1,0:T(4,128)S(1)}, f32[2,4,8]{2,1,0:T(4,128)}, u32[]{:S(2)}) copy-start(f32[2,4,8]{2,1,0:T(4,128)} %density_ref.1) | copy-start | bytes 772
  0.6 3.1 %collective-permute-start = (f32[2,4,8,192]{3,2,1,0:T(8,128)}, f32[2,4,8,192]{3,2,1,0:T(8,128)S(1)}, u32[]{:S(2)}, u32[]{:S(2)}) collective-permute-start(f32[2,4,8,192]{3,2,1,0:T(8,128)} %body_ref.1), channel_id=1, source_target_pairs={{1,0},{0,1},{3,2},{2,3},{5,4},{4,5},{7,6},{6,7},{9,8},{8,9},{11,10... | collective-permute-start | bytes 147464 | tf_op jit(solution)/shard_map/ppermute | solution.py:418
  1.2 2.6 %collective-permute-start.1 = (f32[2,4,8,192]{3,2,1,0:T(8,128)}, f32[2,4,8,192]{3,2,1,0:T(8,128)S(1)}, u32[]{:S(2)}, u32[]{:S(2)}) collective-permute-start(f32[2,4,8,192]{3,2,1,0:T(8,128)} %probe_ref.1), channel_id=1, source_target_pairs={{1,0},{0,1},{3,2},{2,3},{5,4},{4,5},{7,6},{6,7},{9,8},{8,9},{11,10... | collective-permute-start | bytes 147464 | tf_op jit(solution)/shard_map/ppermute | solution.py:418
  2.1 1.7 %copy-start.13 = (s32[2,4,8,7]{3,2,1,0:T(8,128)}, s32[2,4,8,7]{3,2,1,0:T(8,128)S(1)}, u32[]{:S(2)}) copy-start(s32[2,4,8,7]{3,2,1,0:T(8,128)S(1)} %copy.13.refs_3_.types_ref) | copy-start | bytes 5380
  2.1 1.6 %collective-permute-start.3 = (s32[2,4,8,7]{3,2,1,0:T(8,128)S(1)}, s32[2,4,8,7]{3,2,1,0:T(8,128)S(1)}, u32[]{:S(2)}, u32[]{:S(2)}) collective-permute-start(s32[2,4,8,7]{3,2,1,0:T(8,128)S(1)} %copy.13.refs_3_.types_ref), channel_id=1, source_target_pairs={{1,0},{0,1},{3,2},{2,3},{5,4},{4,5},{7,6},{6,7},{9,8},{8,9},{11,10... | collective-permute-start | bytes 5384 | tf_op jit(solution)/shard_map/ppermute | solution.py:418
  2.6 1.2 %collective-permute-start.2 = (f32[2,4,8]{2,1,0:T(4,128)S(1)}, f32[2,4,8]{2,1,0:T(4,128)S(1)}, u32[]{:S(2)}, u32[]{:S(2)}) collective-permute-start(f32[2,4,8]{2,1,0:T(4,128)S(1)} %copy-done.18), channel_id=1, source_target_pairs={{1,0},{0,1},{3,2},{2,3},{5,4},{4,5},{7,6},{6,7},{9,8},{8,9},{11,10... | collective-permute-start | bytes 776 | tf_op jit(solution)/shard_map/ppermute | solution.py:418
  4.4 36.2 %copy-start = (bf16[4,192,192]{2,1,0:T(8,128)(2,1)S(1)}, bf16[4,192,192]{2,1,0:T(8,128)(2,1)}, u32[]{:S(2)}) copy-start(bf16[4,192,192]{2,1,0:T(8,128)(2,1)} %rest_9_.1) | copy-start | bytes 884740
  4.4 36.2 %copy-start.1 = (bf16[4,192,192]{2,1,0:T(8,128)(2,1)S(1)}, bf16[4,192,192]{2,1,0:T(8,128)(2,1)}, u32[]{:S(2)}) copy-start(bf16[4,192,192]{2,1,0:T(8,128)(2,1)} %rest_8_.1) | copy-start | bytes 884740
  6.7 34.0 %copy-start.3 = (bf16[8,16,256]{2,1,0:T(8,128)(2,1)S(1)}, bf16[8,16,256]{2,1,0:T(8,128)(2,1)}, u32[]{:S(2)}) copy-start(bf16[8,16,256]{2,1,0:T(8,128)(2,1)} %get-tuple-element.16.refs_0_.rest_0_) | copy-start | bytes 196612
  6.7 34.0 %copy-start.10 = (bf16[8,16,256]{2,1,0:T(8,128)(2,1)S(1)}, bf16[8,16,256]{2,1,0:T(8,128)(2,1)}, u32[]{:S(2)}) copy-start(bf16[8,16,256]{2,1,0:T(8,128)(2,1)} %get-tuple-element.19.rest_6_) | copy-start | bytes 196612
  6.7 34.0 %copy-start.11 = (s32[56,4]{1,0:T(8,128)S(1)}, s32[56,4]{1,0:T(8,128)}, u32[]{:S(2)}) copy-start(s32[56,4]{1,0:T(8,128)} %constant.6.clone.rest_10_) | copy-start | bytes 2692
  6.7 7.8 %collective-permute-start.6 = (bf16[8,16,256]{2,1,0:T(8,128)(2,1)}, bf16[8,16,256]{2,1,0:T(8,128)(2,1)S(1)}, u32[]{:S(2)}, u32[]{:S(2)}) collective-permute-start(bf16[8,16,256]{2,1,0:T(8,128)(2,1)} %get-tuple-element.16.refs_0_.rest_0_), channel_id=1, source_target_pairs={{24,0},{0,8},{8,16},{16,24},{25,1},{1,9},{9,17},{17,25},{26,2},{2,... | collective-permute-start | bytes 196616 | tf_op jit(solution)/shard_map/ppermute | solution.py:418
  9.5 7.7 %collective-permute-start.5 = (bf16[8,16,256]{2,1,0:T(8,128)(2,1)}, bf16[8,16,256]{2,1,0:T(8,128)(2,1)S(1)}, u32[]{:S(2)}, u32[]{:S(2)}) collective-permute-start(bf16[8,16,256]{2,1,0:T(8,128)(2,1)} %get-tuple-element.16.refs_0_.rest_0_), channel_id=1, source_target_pairs={{16,0},{24,8},{0,16},{8,24},{17,1},{25,9},{1,17},{9,25},{18,2},{26... | collective-permute-start | bytes 196616 | tf_op jit(solution)/shard_map/ppermute | solution.py:418
  12.0 5.4 %collective-permute-start.4 = (bf16[8,16,256]{2,1,0:T(8,128)(2,1)}, bf16[8,16,256]{2,1,0:T(8,128)(2,1)S(1)}, u32[]{:S(2)}, u32[]{:S(2)}) collective-permute-start(bf16[8,16,256]{2,1,0:T(8,128)(2,1)} %get-tuple-element.16.refs_0_.rest_0_), channel_id=1, source_target_pairs={{8,0},{16,8},{24,16},{0,24},{9,1},{17,9},{25,17},{1,25},{10,2},{18... | collective-permute-start | bytes 196616 | tf_op jit(solution)/shard_map/ppermute | solution.py:418
  14.5 3.0 %copy-start.4 = (bf16[8,16,256]{2,1,0:T(8,128)(2,1)}, bf16[8,16,256]{2,1,0:T(8,128)(2,1)S(1)}, u32[]{:S(2)}) copy-start(bf16[8,16,256]{2,1,0:T(8,128)(2,1)S(1)} %collective-permute-done.6.refs_3_.rest_3_) | copy-start | bytes 196612
  29.9 10.8 %copy-start.12 = (f32[4,256]{1,0:T(4,128)S(1)}, f32[4,256]{1,0:T(4,128)}, u32[]{:S(2)}) copy-start(f32[4,256]{1,0:T(4,128)} %get-tuple-element.20.rest_7_.diag_ref) | copy-start | bytes 12292
  29.9 7.4 %collective-permute-start.7 = (bf16[20,16,256]{2,1,0:T(8,128)(2,1)}, bf16[20,16,256]{2,1,0:T(8,128)(2,1)S(1)}, u32[]{:S(2)}, u32[]{:S(2)}) collective-permute-start(bf16[20,16,256]{2,1,0:T(8,128)(2,1)} %get-tuple-element.17), channel_id=1, source_target_pairs={{2,0},{4,2},{6,4},{0,6},{3,1},{5,3},{7,5},{1,7},{10,8},{12,10},{14... | collective-permute-start | bytes 491528 | tf_op jit(solution)/shard_map/ppermute | solution.py:418
  32.4 8.3 %collective-permute-start.8 = (bf16[20,16,256]{2,1,0:T(8,128)(2,1)}, bf16[20,16,256]{2,1,0:T(8,128)(2,1)S(1)}, u32[]{:S(2)}, u32[]{:S(2)}) collective-permute-start(bf16[20,16,256]{2,1,0:T(8,128)(2,1)} %get-tuple-element.18), channel_id=1, source_target_pairs={{6,0},{0,2},{2,4},{4,6},{7,1},{1,3},{3,5},{5,7},{14,8},{8,10},{10,... | collective-permute-start | bytes 491528 | tf_op jit(solution)/shard_map/ppermute | solution.py:418
  40.7 0.8 %copy-start.5 = (bf16[8,16,256]{2,1,0:T(8,128)(2,1)S(1)}, bf16[8,16,256]{2,1,0:T(8,128)(2,1)}, u32[]{:S(2)}) copy-start(bf16[8,16,256]{2,1,0:T(8,128)(2,1)} %copy-done.4) | copy-start | bytes 196612
  41.5 0.8 %copy-start.7 = (bf16[8,16,256]{2,1,0:T(8,128)(2,1)S(1)}, bf16[8,16,256]{2,1,0:T(8,128)(2,1)}, u32[]{:S(2)}) copy-start(bf16[8,16,256]{2,1,0:T(8,128)(2,1)} %copy-done.6) | copy-start | bytes 196612
  42.4 0.8 %copy-start.9 = (bf16[8,16,256]{2,1,0:T(8,128)(2,1)S(1)}, bf16[8,16,256]{2,1,0:T(8,128)(2,1)}, u32[]{:S(2)}) copy-start(bf16[8,16,256]{2,1,0:T(8,128)(2,1)} %copy-done.8) | copy-start | bytes 196612
  56.3 0.7 copy-start.2
  57.0 1.5 %collective-permute-start.9 = (f32[4,8,8,256]{3,2,1,0:T(8,128)S(1)}, f32[4,8,8,256]{3,2,1,0:T(8,128)S(1)}, u32[]{:S(2)}, u32[]{:S(2)}) collective-permute-start(f32[4,8,8,256]{3,2,1,0:T(8,128)S(1)} %get-tuple-element.22), channel_id=1, source_target_pairs={{1,0},{0,1},{3,2},{2,3},{5,4},{4,5},{7,6},{6,7},{9,8},{8,9},{11,10... | collective-permute-start | bytes 786440 | tf_op jit(solution)/shard_map/ppermute | solution.py:418
  58.5 0.7 copy-start.14
  (6 other events, 3.7 us)

commit v3 on v2

--- a/solution.py
+++ b/solution.py
@@ -87,7 +87,7 @@
 
 def pack_kernel(core_ref, blocks_ref, *refs):
     own, got = refs[0:4], refs[4:8]
-    hi_ref, lo_ref, diag_ref, wide, notes = refs[8:]
+    hi_ref, lo_ref, diag_ref, wide, flat = refs[8:]
     dof = blocks_ref.shape[-1]
     rows = lax.broadcasted_iota(jnp.int32, (dof, dof), 0)
     eye = (rows == lane_iota((dof, dof))).astype(F32)
@@ -95,9 +95,22 @@
     for t in range(blocks_ref.shape[0]):
         diag_ref[t : t + 1, :dof] = jnp.sum(blocks_ref[t].astype(F32) * eye, axis=0, keepdims=True)
     first = core_ref[0] == 0
-    len_x, len_y, half, kinds_n = own[3].shape
+    len_x, links_n, len_y, half = own[3].shape
     lane = lane_iota((half, 128))
     body_lanes = dof - 128
+    flat[...] = jnp.zeros(flat.shape, F32)
+    turned, notes = {}, {}
+    for x in range(len_x):
+        for h, (_, _, density_ref, types_ref) in enumerate((own, got)):
+            for k in range(links_n):
+                flat[k * len_y : (k + 1) * len_y, :half] = types_ref[x, k].astype(F32)
+            density = density_ref[x]
+            rest = density - density.astype(BF16).astype(F32)
+            last = rest - rest.astype(BF16).astype(F32)
+            for k, v in enumerate((density, rest, last)):
+                flat[(links_n + k) * len_y : (links_n + k + 1) * len_y, :half] = v
+            turned[x, h] = jnp.transpose(flat[...])[:half]
+            notes[x, h] = pltpu.roll(turned[x, h], body_lanes, 1)
     for x in range(len_x):
         for y in range(len_y):
             i = x * len_y + y
@@ -105,20 +118,13 @@
             for h, (body_ref, probe_ref, density_ref, types_ref) in enumerate((own, got)):
                 slot = i * 2 + h
                 wide[slot, :, :dof] = jnp.where(first, body_ref[x, y], probe_ref[x, y])
-                notes[slot, :, :kinds_n] = types_ref[x, y].astype(F32)
-                kinds = notes[slot]
-                kind = kinds[:, kinds_n - 1 : kinds_n]
-                density = upright(density_ref[x, y : y + 1, :])
+                kind = turned[x, h][:, (links_n - 1) * len_y + y : (links_n - 1) * len_y + y + 1]
+                density = turned[x, h][:, links_n * len_y + y : links_n * len_y + y + 1]
                 scale = density * jnp.sqrt(density)
                 ship = [(wide[slot, :, lanes] / pivot_of(kind, diag_ref, lanes)) * scale for lanes in SIDES]
                 his = [v.astype(BF16).astype(F32) for v in ship]
                 los = [v - u for v, u in zip(ship, his)]
-                rest = density - density.astype(BF16).astype(F32)
-                note = pltpu.roll(kinds, body_lanes, 1)
-                note = jnp.where(lane == body_lanes + kinds_n, density, note)
-                note = jnp.where(lane == body_lanes + kinds_n + 1, rest, note)
-                note = jnp.where(lane == body_lanes + kinds_n + 2, rest - rest.astype(BF16).astype(F32), note)
-                note = jnp.where(lane < body_lanes + kinds_n + 3, note, 0.0)
+                note = jnp.where(lane % len_y == y, notes[x, h], 0.0)
                 his[1] = jnp.where(lane < body_lanes, his[1], note)
                 los[1] = jnp.where(lane < body_lanes, los[1], 0.0)
                 parts.append((his, los))
@@ -127,27 +133,21 @@
                 lo_ref[i, :, lanes] = jnp.concatenate([p[1][side] for p in parts], axis=0).astype(BF16)
 
 
-def assemble_kernel(copies, count_in, *refs):
-    sem = refs[-1]
-    ins, outs = refs[:count_in], refs[count_in:-1]
-    started = []
-    for out, lines in zip(outs, copies):
-        for to, (at, j, n) in lines:
-            copy = pltpu.make_async_copy(ins[at].at[pl.ds(j, n)], out.at[pl.ds(to, n)], sem.at[len(started)])
-            copy.start()
-            started.append(copy)
-    for copy in started:
-        copy.wait()
+def assemble_kernel(lines, count_in, *refs):
+    ins, outs = refs[:count_in], refs[count_in:]
+    for out, line in zip(outs, lines):
+        for to, (at, j) in enumerate(line):
+            out[to] = ins[at][j]
 
 
 def divisor(n, cap):
     return max(d for d in range(1, cap + 1) if n % d == 0)
 
 
-def sweep_kernel(window, refs_in, *rest):
+def sweep_kernel(window, refs_in, len_y, *rest):
     pieces = rest[:refs_in]
     (lo_ref, diag_ref, off_ref, self_ref, near_ref, keep_ref, send_ref) = rest[refs_in : refs_in + 7]
-    (ship_a, ship_b, own_a, own_b, kinds, kinds_16, gain, scale, up_w, low_w, lhs, leave, sem) = rest[refs_in + 7 :]
+    (ship_a, ship_b, own_a, own_b, kinds, kinds_16, gain, scale, up_w, low_w, lhs) = rest[refs_in + 7 :]
     dof = off_ref.shape[-1]
     kinds_n = off_ref.shape[0]
     depth = ship_a.shape[1]
@@ -164,7 +164,7 @@
         ship_a[i] = pieces[at][j]
         if i < own:
             own_a[i] = pieces[at][j].astype(F32) + lo_ref[j].astype(F32)
-    spread_rows = lax.broadcasted_iota(jnp.int32, (128, 8 * 128), 0) - (dof - 128)
+    spread_rows = (lax.broadcasted_iota(jnp.int32, (128, 8 * 128), 0) - (dof - 128)) // len_y
     spread_cols = lane_iota((128, 8 * 128)) // 128
     spread = (jnp.minimum(spread_rows, 7) == spread_cols) & (spread_rows >= 0) & (spread_rows < 10)
     spread = spread.astype(BF16)
@@ -221,7 +221,6 @@
         return acc + jnp.dot(lhs[start:stop, n:], low_w[...], preferred_element_type=F32)
 
     base = 2 * own * depth
-    copies = []
     for step in range(ITERS):
         src, dst = (ship_b, ship_a) if step % 2 else (ship_a, ship_b)
         src_own, dst_own = (own_b, own_a) if step % 2 else (own_a, own_b)
@@ -240,14 +239,11 @@
             for lanes in SIDES:
                 value = both[:, lanes] * scale[u]
                 keep_ref[step, u, :, lanes] = value[:half]
-                leave[step, u, :, lanes] = value[half:]
+                send_ref[step, u, :, lanes] = value[half:]
             if step < ITERS - 1:
                 value = both * gain[u]
                 dst_own[u] = value
                 dst[u] = value.astype(BF16)
-        copy = pltpu.make_async_copy(leave.at[step], send_ref.at[step], sem.at[step])
-        copy.start()
-        copies.append(copy)
         halo = window.count[ITERS - 1 - step] - own
         if halo:
             batch = divisor(halo, 14)
@@ -263,8 +259,6 @@
                 return carry
 
             lax.fori_loop(0, halo // batch, one, 0)
-    for copy in copies:
-        copy.wait()
 
 
 def gram_index(i, j):
@@ -275,10 +269,8 @@
 GRAM = (ITERS + 1) * (ITERS + 2) // 2
 
 
-def moments_kernel(core_ref, body_ref, probe_ref, density_ref, types_ref, owner_ref, keep_ref, diag_ref, back_ref,
-                   message_ref, state_ref, adjoint_ref, got, wide, sem):
-    arrive = pltpu.make_async_copy(back_ref, got, sem)
-    arrive.start()
+def moments_kernel(core_ref, body_ref, probe_ref, density_ref, types_ref, owner_ref, keep_ref, diag_ref, got,
+                   message_ref, state_ref, adjoint_ref, wide):
     len_x, len_y, half, dof = body_ref.shape
     kinds_n = diag_ref.shape[0]
     first = core_ref[0] == 0
@@ -292,11 +284,10 @@
             i = x * len_y + y
             wide[2 * i, :, :dof] = body_ref[x, y]
             wide[2 * i + 1, :, :dof] = probe_ref[x, y]
-    arrive.wait()
     for x in range(len_x):
         for y in range(len_y):
             i = x * len_y + y
-            kind = types_ref[x, y][:, 6:7].astype(F32)
+            kind = upright(types_ref[x, 6, y : y + 1, :].astype(F32))
             density = upright(density_ref[x, y : y + 1, :])
             owner = upright(owner_ref[x, y : y + 1, :].astype(F32)).astype(jnp.int32)
             inside = lax.rem(owner, GPB)
@@ -413,19 +404,18 @@
         copy.wait()
 
 
+def small(mebibytes):
+    return pltpu.CompilerParams(vmem_limit_bytes=mebibytes * 2**20)
+
+
 def shifted(array, axis, offset):
     peers = lax.axis_size(axis)
     return lax.ppermute(array, axis, [((i + offset) % peers, i) for i in range(peers)])
 
 
-def runs(lines):
-    out = []
-    for to, (at, j) in enumerate(lines):
-        if out and out[-1][1][0] == at and out[-1][1][1] + out[-1][1][2] == j:
-            out[-1] = (out[-1][0], (at, out[-1][1][1], out[-1][1][2] + 1))
-        else:
-            out.append((to, (at, j, 1)))
-    return out
+def fits(shape):
+    _, len_y, half, dof = shape
+    return half % 8 == 0 and 128 < dof and dof + 10 * len_y <= LANES
 
 
 def by_field(body_load, probe_load, density, link_types, off_blocks, self_blocks, block_owner):
@@ -435,7 +425,8 @@
     kinds_n = off_blocks.shape[0]
     window = Window(lax.axis_size("gx"), lax.axis_size("gy"), len_x, len_y)
     core = lax.axis_index("gz").reshape(1)
-    mine = (body_load, probe_load, density, link_types)
+    kinds = jnp.transpose(link_types, (0, 3, 1, 2))
+    mine = (body_load, probe_load, density, kinds)
     theirs = tuple(shifted(a, "gz", 1) for a in mine)
     hi, lo, diag = pl.pallas_call(
         pack_kernel,
@@ -446,7 +437,8 @@
         ),
         in_specs=[SMEM] + [VMEM] * 9,
         out_specs=(VMEM,) * 3,
-        scratch_shapes=[pltpu.VMEM((2 * cols, half, LANES), F32), pltpu.VMEM((2 * cols, half, 128), F32)],
+        scratch_shapes=[pltpu.VMEM((2 * cols, half, LANES), F32), pltpu.VMEM((128, 128), F32)],
+        compiler_params=small(8),
         name="pack",
     )(core, self_blocks, *mine, *theirs)
     from_x = [hi] + [shifted(hi, "gx", o) for o in window.x_offsets]
@@ -455,15 +447,15 @@
         lines = []
         for x, y in window.y_columns[o]:
             lines.append((1 + window.x_offsets.index(x[0]) if x[0] else 0, x[1] * len_y + y[1]))
-        copies.append(runs(lines))
+        copies.append(lines)
     messages = pl.pallas_call(
         functools.partial(assemble_kernel, copies, len(from_x)),
         out_shape=tuple(
             jax.ShapeDtypeStruct((len(window.y_columns[o]), depth, LANES), BF16) for o in window.y_offsets
         ),
-        in_specs=[ANY] * len(from_x),
-        out_specs=(ANY,) * len(copies),
-        scratch_shapes=[pltpu.SemaphoreType.DMA((sum(len(c) for c in copies),))],
+        in_specs=[VMEM] * len(from_x),
+        out_specs=(VMEM,) * len(copies),
+        compiler_params=small(8),
         name="assemble",
     )(*from_x)
     pieces = from_x + [shifted(m, "gy", o) for m, o in zip(messages, window.y_offsets)]
@@ -471,10 +463,10 @@
     targets = window.count[ITERS - 1]
     rows = depth * (2 * own + 14)
     keep, send = pl.pallas_call(
-        functools.partial(sweep_kernel, window, len(pieces)),
+        functools.partial(sweep_kernel, window, len(pieces), len_y),
         out_shape=(jax.ShapeDtypeStruct((ITERS, cols, half, LANES), F32),) * 2,
         in_specs=[VMEM] * (len(pieces) + 4) + [SMEM],
-        out_specs=(VMEM, ANY),
+        out_specs=(VMEM,) * 2,
         scratch_shapes=[
             pltpu.VMEM((window.count[ITERS], depth, LANES), BF16),
             pltpu.VMEM((targets, depth, LANES), BF16),
@@ -487,10 +479,8 @@
             pltpu.VMEM((LANES, kinds_n * LANES), BF16),
             pltpu.VMEM((2 * kinds_n * LANES, LANES), BF16),
             pltpu.VMEM((rows, 3 * kinds_n * LANES), BF16),
-            pltpu.VMEM((ITERS, cols, half, LANES), F32),
-            pltpu.SemaphoreType.DMA((ITERS,)),
         ],
-        compiler_params=pltpu.CompilerParams(vmem_limit_bytes=40 * 2**20),
+        compiler_params=small(20),
         name="sweeps",
     )(*pieces, lo, diag, off_blocks, self_blocks, jnp.asarray(window.neighbours))
     back = shifted(send, "gz", 1)
@@ -502,15 +492,12 @@
             jax.ShapeDtypeStruct((ITERS, cols, half, LANES), F32),
             jax.ShapeDtypeStruct((ITERS, cols, half, LANES), F32),
         ),
-        in_specs=[SMEM] + [VMEM] * 7 + [ANY],
+        in_specs=[SMEM] + [VMEM] * 8,
         out_specs=(VMEM,) * 3,
-        scratch_shapes=[
-            pltpu.VMEM((ITERS, cols, half, LANES), F32),
-            pltpu.VMEM((2 * cols, half, LANES), F32),
-            pltpu.SemaphoreType.DMA,
-        ],
+        scratch_shapes=[pltpu.VMEM((2 * cols, half, LANES), F32)],
+        compiler_params=small(12),
         name="moments",
-    )(core, body_load, probe_load, density, link_types, block_owner, keep, diag, back)
+    )(core, body_load, probe_load, density, kinds, block_owner, keep, diag, back)
     message = lax.all_to_all(message, ("gx", "gy", "gz"), 0, 0, tiled=True)
     state, adjoint, coarse = pl.pallas_call(
         finish_kernel,
@@ -527,6 +514,7 @@
             pltpu.VMEM((1, GPB), F32),
             pltpu.SemaphoreType.DMA((3,)),
         ],
+        compiler_params=small(8),
         name="finish",
     )(message, pre_state, pre_adjoint)
     return state.reshape(body_load.shape), adjoint.reshape(body_load.shape), coarse.reshape(GPB)
@@ -646,7 +634,7 @@
     )
     out_specs = (P("gx", "gy", "gz", None), P("gx", "gy", "gz", None), P(("gx", "gy", "gz")))
     def local(*arrays):
-        split = lax.axis_size("gz") == 2 and arrays[0].shape[2] % 8 == 0
+        split = lax.axis_size("gz") == 2 and fits(arrays[0].shape)
         return (by_field if split else by_sweep)(*arrays)
 
     return jax.shard_map(local, mesh=mesh, in_specs=in_specs, out_specs=out_specs, check_vma=False)

time: 75.7 us -> 54.4 us (0.72)
  Pallas kernels: 32.2 us -> 14.6 us
  local copies, waits for them, and re-layouts: 6.43 us -> 3.46 us
    pallas_call x1, Pallas kernels: 11.4 us -> 0.02 us  [by_field(): pl.pallas_call(functools.partial(assemble_kernel, copies, len(from_x)), o...]
    unnamed x41 -> x24, local copies, waits for them, and re-layouts: 6.43 us -> 3.46 us
    pallas_call x1, Pallas kernels: 3.42 us -> 0.6 us  [by_field(): pl.pallas_call(moments_kernel, out_shape=(jax.ShapeDtypeStruct((owners, 2...]
    pallas_call x1, Pallas kernels: 2.23 us -> 0.31 us  [by_field(): pl.pallas_call(pack_kernel, out_shape=(jax.ShapeDtypeStruct((cols, depth,...]
    pallas_call x1, Pallas kernels: 2.1 us -> 1.05 us  [by_field(): pl.pallas_call(finish_kernel, out_shape=(jax.ShapeDtypeStruct((cols, half...]
  transfers between devices with their start and end apart: 10 -> 10, of which waited for: 7 -> 7; matrix products, arithmetic and copies ran while one was open for 1% -> 0% of each run, Pallas kernels for 0% -> 0%
where the time goes in v3:
time: 54.4 us; the launch traced here: 54.1 us
  Pallas kernels  14.6 us (27%)
  waiting for transfers between devices  14.5 us (27%)
  starting transfers between devices  10.4 us (19%)
  blocking collectives  10.4 us (19%)
  local copies, waits for them, and re-layouts  3.46 us (6%)
  between operations  0.76 us (1%)
    ppermute x10, waiting for transfers between devices, shifted(): lax.ppermute(array, axis, [((i + offset) % peers, i) for i in range(peers)])  14.5 us
    pallas_call x1, Pallas kernels, by_field(): pl.pallas_call(functools.partial(sweep_kernel, window, len(pieces), len_y...  12.6 us
    ppermute x10, starting transfers between devices, shifted(): lax.ppermute(array, axis, [((i + offset) % peers, i) for i in range(peers)])  10.4 us
    all_to_all x1, blocking collectives, by_field(): message = lax.all_to_all(message, ('gx', 'gy', 'gz'), 0, 0, tiled=True)  10.4 us
    unnamed x24, local copies, waits for them, and re-layouts  3.46 us
  transfers between devices with their start and end apart: 10, of which 7 were waited for; matrix products, arithmetic and copies ran while one was open for 0% of the time, Pallas kernels for 0%

profile of v3, /device:TPU:0, one launch (start us, length us, event | category | flops | bytes accessed | tf_op | source)
XLA Modules:
  0.0 54.1 jit_solution(13907034691757183044)
XLA Ops:
  0.6 0.5 collective-permute-start
  1.1 0.1 collective-permute-start.1
  1.2 0.4 collective-permute-start.3
  1.7 0.1 collective-permute-start.2
  1.7 1.3 %collective-permute-done.2.refs_6_ = f32[2,4,8]{2,1,0:T(4,128)S(1)} collective-permute-done((f32[2,4,8]{2,1,0:T(4,128)}, f32[2,4,8]{2,1,0:T(4,128)S(1)}, u32[]{:S(2)}, u32[]{:S(2)}) %collective-permute-start.2) | collective-permute-done | bytes 288 | tf_op jit(solution)/shard_map/ppermute | solution.py:413
  3.1 1.0 %copy-done = bf16[4,192,192]{2,1,0:T(8,128)(2,1)S(1)} copy-done((bf16[4,192,192]{2,1,0:T(8,128)(2,1)S(1)}, bf16[4,192,192]{2,1,0:T(8,128)(2,1)}, u32[]{:S(2)}) %copy-start) | copy-done | bytes 294936
  4.1 0.8 %copy-done.3 = f32[2,4,8,192]{3,2,1,0:T(8,128)S(1)} copy-done((f32[2,4,8,192]{3,2,1,0:T(8,128)S(1)}, f32[2,4,8,192]{3,2,1,0:T(8,128)}, u32[]{:S(2)}) %copy-start.3) | copy-done | bytes 49176
  4.9 0.8 %copy-done.5 = f32[2,4,8,192]{3,2,1,0:T(8,128)S(1)} copy-done((f32[2,4,8,192]{3,2,1,0:T(8,128)S(1)}, f32[2,4,8,192]{3,2,1,0:T(8,128)}, u32[]{:S(2)}) %copy-start.5) | copy-done | bytes 49176
  5.7 0.7 %copy-done.7 = s32[2,4,8,7]{2,1,3,0:T(4,128)S(1)} copy-done((s32[2,4,8,7]{2,1,3,0:T(4,128)S(1)}, s32[2,4,8,7]{2,1,3,0:T(4,128)}, u32[]{:S(2)}) %copy-start.7) | copy-done | bytes 1816
  6.5 0.3 pack.1
  6.8 2.8 %collective-permute-start.6 = (bf16[8,16,256]{2,1,0:T(8,128)(2,1)S(1)}, bf16[8,16,256]{2,1,0:T(8,128)(2,1)S(1)}, u32[]{:S(2)}, u32[]{:S(2)}) collective-permute-start(bf16[8,16,256]{2,1,0:T(8,128)(2,1)S(1)} %get-tuple-element.16.refs_0_.rest_0_), channel_id=1, source_target_pairs={{24,0},{0,8},{8,16},{16,24},{25,1},{1,9},{9,17},{17,25},{26,2},{2,... | collective-permute-start | bytes 196616 | tf_op jit(solution)/shard_map/ppermute | solution.py:413
  9.6 2.6 %collective-permute-start.5 = (bf16[8,16,256]{2,1,0:T(8,128)(2,1)S(1)}, bf16[8,16,256]{2,1,0:T(8,128)(2,1)S(1)}, u32[]{:S(2)}, u32[]{:S(2)}) collective-permute-start(bf16[8,16,256]{2,1,0:T(8,128)(2,1)S(1)} %get-tuple-element.16.refs_0_.rest_0_), channel_id=1, source_target_pairs={{16,0},{24,8},{0,16},{8,24},{17,1},{25,9},{1,17},{9,25},{18,2},{26... | collective-permute-start | bytes 196616 | tf_op jit(solution)/shard_map/ppermute | solution.py:413
  12.2 1.3 %collective-permute-start.4 = (bf16[8,16,256]{2,1,0:T(8,128)(2,1)S(1)}, bf16[8,16,256]{2,1,0:T(8,128)(2,1)S(1)}, u32[]{:S(2)}, u32[]{:S(2)}) collective-permute-start(bf16[8,16,256]{2,1,0:T(8,128)(2,1)S(1)} %get-tuple-element.16.refs_0_.rest_0_), channel_id=1, source_target_pairs={{8,0},{16,8},{24,16},{0,24},{9,1},{17,9},{25,17},{1,25},{10,2},{18... | collective-permute-start | bytes 196616 | tf_op jit(solution)/shard_map/ppermute | solution.py:413
  13.6 0.8 %collective-permute-done.6.refs_3_.rest_3_ = bf16[8,16,256]{2,1,0:T(8,128)(2,1)S(1)} collective-permute-done((bf16[8,16,256]{2,1,0:T(8,128)(2,1)S(1)}, bf16[8,16,256]{2,1,0:T(8,128)(2,1)S(1)}, u32[]{:S(2)}, u32[]{:S(2)}) %collective-permute-start.6) | collective-permute-done | bytes 65568 | tf_op jit(solution)/shard_map/ppermute | solution.py:413
  14.4 2.7 %collective-permute-done.5.refs_2_.rest_2_ = bf16[8,16,256]{2,1,0:T(8,128)(2,1)S(1)} collective-permute-done((bf16[8,16,256]{2,1,0:T(8,128)(2,1)S(1)}, bf16[8,16,256]{2,1,0:T(8,128)(2,1)S(1)}, u32[]{:S(2)}, u32[]{:S(2)}) %collective-permute-start.5) | collective-permute-done | bytes 65568 | tf_op jit(solution)/shard_map/ppermute | solution.py:413
  17.1 0.3 collective-permute-done.4.refs_1_.rest_1_
  17.4 2.5 %collective-permute-start.7 = (bf16[20,16,256]{2,1,0:T(8,128)(2,1)S(1)}, bf16[20,16,256]{2,1,0:T(8,128)(2,1)S(1)}, u32[]{:S(2)}, u32[]{:S(2)}) collective-permute-start(bf16[20,16,256]{2,1,0:T(8,128)(2,1)S(1)} %get-tuple-element.17), channel_id=1, source_target_pairs={{2,0},{4,2},{6,4},{0,6},{3,1},{5,3},{7,5},{1,7},{10,8},{12,10},{14... | collective-permute-start | bytes 491528 | tf_op jit(solution)/shard_map/ppermute | solution.py:413
  19.9 4.7 %collective-permute-done.7.rest_4_ = bf16[20,16,256]{2,1,0:T(8,128)(2,1)S(1)} collective-permute-done((bf16[20,16,256]{2,1,0:T(8,128)(2,1)S(1)}, bf16[20,16,256]{2,1,0:T(8,128)(2,1)S(1)}, u32[]{:S(2)}, u32[]{:S(2)}) %collective-permute-start.7) | collective-permute-done | bytes 163872 | tf_op jit(solution)/shard_map/ppermute | solution.py:413
  24.6 3.1 %collective-permute-done.8.rest_5_ = bf16[20,16,256]{2,1,0:T(8,128)(2,1)S(1)} collective-permute-done((bf16[20,16,256]{2,1,0:T(8,128)(2,1)S(1)}, bf16[20,16,256]{2,1,0:T(8,128)(2,1)S(1)}, u32[]{:S(2)}, u32[]{:S(2)}) %collective-permute-start.8) | collective-permute-done | bytes 163872 | tf_op jit(solution)/shard_map/ppermute | solution.py:413
  27.8 12.6 %sweeps.1 = (f32[4,8,8,256]{3,2,1,0:T(8,128)S(1)}, f32[4,8,8,256]{3,2,1,0:T(8,128)S(1)}) custom-call(bf16[8,16,256]{2,1,0:T(8,128)(2,1)S(1)} %get-tuple-element.16.refs_0_.rest_0_, bf16[8,16,256]{2,1,0:T(8,128)(2,1)S(1)} %collective-permute-done.4.refs_1_.rest_1_, bf16[8,16,256]{2,1,0:T(8,128)(2,1)S(1)} %collective-permute-done.5.refs_2_.rest_2_, ...), custom_call_target="tpu_custom_call" | custom-call | tf_op jit(solution)/shard_map/sweeps/pallas_call | solution.py:465
  40.5 1.5 %collective-permute-done.9.got = f32[4,8,8,256]{3,2,1,0:T(8,128)S(1)} collective-permute-done((f32[4,8,8,256]{3,2,1,0:T(8,128)S(1)}, f32[4,8,8,256]{3,2,1,0:T(8,128)S(1)}, u32[]{:S(2)}, u32[]{:S(2)}) %collective-permute-start.9) | collective-permute-done | bytes 262176 | tf_op jit(solution)/shard_map/ppermute | solution.py:413
  42.0 0.6 %moments.1 = (f32[32,2,128]{2,1,0:T(2,128)S(1)}, f32[4,8,8,256]{3,2,1,0:T(8,128)S(1)}, f32[4,8,8,256]{3,2,1,0:T(8,128)S(1)}) custom-call(s32[1]{0:T(128)} %bitcast.core_ref, f32[2,4,8,192]{3,2,1,0:T(8,128)S(1)} %copy-done.4, f32[2,4,8,192]{3,2,1,0:T(8,128)S(1)} %copy-done.6, f32[2,4,8]{2,1,0:T(4,128)S(1)} %copy-done.10, s32[2,7,4,8]{3,2,1,0:T(4,128)S(1)} %bitcast.7, ...), custom_call_target="tpu_custom_call" | custom-call | tf_op jit(solution)/shard_map/moments/pallas_call | solution.py:488
  42.6 10.4 %all_to_all.5.message_ref = f32[32,2,128]{2,1,0:T(2,128)S(1)} all-to-all(f32[32,2,128]{2,1,0:T(2,128)S(1)} %get-tuple-element.23), channel_id=1, replica_groups=mesh['gx'=4,'gy'=4,'gz'=2] {'gx','gy','gz'}, dimensions={0} | all-to-all | bytes 65536 | tf_op jit(solution)/shard_map/all_to_all | solution.py:501
  53.0 1.1 %finish.1 = (f32[8,8,192]{2,1,0:T(8,128)}, f32[8,8,192]{2,1,0:T(8,128)}, f32[1,8]{1,0:T(1,128)}) custom-call(f32[32,2,128]{2,1,0:T(2,128)S(1)} %all_to_all.5.message_ref, f32[4,8,8,256]{3,2,1,0:T(8,128)S(1)} %get-tuple-element.24.pre_state_ref, f32[4,8,8,256]{3,2,1,0:T(8,128)S(1)} %get-tuple-element.25.pre_adjoint_ref), custom_call_target="tpu_custom_call" | custom-call | tf_op jit(solution)/shard_map/finish/pallas_call | solution.py:502
  (26 shorter events, 0.2 us)
Async XLA Ops:
  0.6 2.4 %collective-permute-start = (f32[2,4,8,192]{3,2,1,0:T(8,128)}, f32[2,4,8,192]{3,2,1,0:T(8,128)S(1)}, u32[]{:S(2)}, u32[]{:S(2)}) collective-permute-start(f32[2,4,8,192]{3,2,1,0:T(8,128)} %body_ref.1), channel_id=1, source_target_pairs={{1,0},{0,1},{3,2},{2,3},{5,4},{4,5},{7,6},{6,7},{9,8},{8,9},{11,10... | collective-permute-start | bytes 147464 | tf_op jit(solution)/shard_map/ppermute | solution.py:413
  1.1 1.9 %collective-permute-start.1 = (f32[2,4,8,192]{3,2,1,0:T(8,128)}, f32[2,4,8,192]{3,2,1,0:T(8,128)S(1)}, u32[]{:S(2)}, u32[]{:S(2)}) collective-permute-start(f32[2,4,8,192]{3,2,1,0:T(8,128)} %probe_ref.1), channel_id=1, source_target_pairs={{1,0},{0,1},{3,2},{2,3},{5,4},{4,5},{7,6},{6,7},{9,8},{8,9},{11,10... | collective-permute-start | bytes 147464 | tf_op jit(solution)/shard_map/ppermute | solution.py:413
  1.2 1.8 %copy-start.10 = (f32[2,4,8]{2,1,0:T(4,128)S(1)}, f32[2,4,8]{2,1,0:T(4,128)}, u32[]{:S(2)}) copy-start(f32[2,4,8]{2,1,0:T(4,128)} %density_ref.1) | copy-start | bytes 772
  1.2 1.8 %collective-permute-start.3 = (s32[2,7,4,8]{3,2,1,0:T(4,128)}, s32[2,7,4,8]{3,2,1,0:T(4,128)S(1)}, u32[]{:S(2)}, u32[]{:S(2)}) collective-permute-start(s32[2,7,4,8]{3,2,1,0:T(4,128)} %bitcast.5), channel_id=1, source_target_pairs={{1,0},{0,1},{3,2},{2,3},{5,4},{4,5},{7,6},{6,7},{9,8},{8,9},{11,10... | collective-permute-start | bytes 5384 | tf_op jit(solution)/shard_map/ppermute | solution.py:413
  1.7 1.4 %collective-permute-start.2 = (f32[2,4,8]{2,1,0:T(4,128)}, f32[2,4,8]{2,1,0:T(4,128)S(1)}, u32[]{:S(2)}, u32[]{:S(2)}) collective-permute-start(f32[2,4,8]{2,1,0:T(4,128)} %density_ref.1), channel_id=1, source_target_pairs={{1,0},{0,1},{3,2},{2,3},{5,4},{4,5},{7,6},{6,7},{9,8},{8,9},{11,10... | collective-permute-start | bytes 776 | tf_op jit(solution)/shard_map/ppermute | solution.py:413
  3.1 1.0 %copy-start = (bf16[4,192,192]{2,1,0:T(8,128)(2,1)S(1)}, bf16[4,192,192]{2,1,0:T(8,128)(2,1)}, u32[]{:S(2)}) copy-start(bf16[4,192,192]{2,1,0:T(8,128)(2,1)} %rest_9_.1) | copy-start | bytes 884740
  4.1 0.8 %copy-start.3 = (f32[2,4,8,192]{3,2,1,0:T(8,128)S(1)}, f32[2,4,8,192]{3,2,1,0:T(8,128)}, u32[]{:S(2)}) copy-start(f32[2,4,8,192]{3,2,1,0:T(8,128)} %body_ref.1) | copy-start | bytes 147460
  4.9 0.8 %copy-start.5 = (f32[2,4,8,192]{3,2,1,0:T(8,128)S(1)}, f32[2,4,8,192]{3,2,1,0:T(8,128)}, u32[]{:S(2)}) copy-start(f32[2,4,8,192]{3,2,1,0:T(8,128)} %probe_ref.1) | copy-start | bytes 147460
  5.7 0.7 %copy-start.7 = (s32[2,4,8,7]{2,1,3,0:T(4,128)S(1)}, s32[2,4,8,7]{2,1,3,0:T(4,128)}, u32[]{:S(2)}) copy-start(s32[2,4,8,7]{2,1,3,0:T(4,128)} %param.11) | copy-start | bytes 5380
  6.5 21.2 %copy-start.1 = (bf16[4,192,192]{2,1,0:T(8,128)(2,1)S(1)}, bf16[4,192,192]{2,1,0:T(8,128)(2,1)}, u32[]{:S(2)}) copy-start(bf16[4,192,192]{2,1,0:T(8,128)(2,1)} %rest_9_.1) | copy-start | bytes 884740
  6.5 21.3 %copy-start.2 = (bf16[4,192,192]{2,1,0:T(8,128)(2,1)S(1)}, bf16[4,192,192]{2,1,0:T(8,128)(2,1)}, u32[]{:S(2)}) copy-start(bf16[4,192,192]{2,1,0:T(8,128)(2,1)} %rest_8_.1) | copy-start | bytes 884740
  6.8 20.9 %copy-start.9 = (s32[56,4]{1,0:T(8,128)S(1)}, s32[56,4]{1,0:T(8,128)}, u32[]{:S(2)}) copy-start(s32[56,4]{1,0:T(8,128)} %constant.6.clone.rest_10_) | copy-start | bytes 2692
  6.8 7.6 %collective-permute-start.6 = (bf16[8,16,256]{2,1,0:T(8,128)(2,1)S(1)}, bf16[8,16,256]{2,1,0:T(8,128)(2,1)S(1)}, u32[]{:S(2)}, u32[]{:S(2)}) collective-permute-start(bf16[8,16,256]{2,1,0:T(8,128)(2,1)S(1)} %get-tuple-element.16.refs_0_.rest_0_), channel_id=1, source_target_pairs={{24,0},{0,8},{8,16},{16,24},{25,1},{1,9},{9,17},{17,25},{26,2},{2,... | collective-permute-start | bytes 196616 | tf_op jit(solution)/shard_map/ppermute | solution.py:413
  9.6 7.5 %collective-permute-start.5 = (bf16[8,16,256]{2,1,0:T(8,128)(2,1)S(1)}, bf16[8,16,256]{2,1,0:T(8,128)(2,1)S(1)}, u32[]{:S(2)}, u32[]{:S(2)}) collective-permute-start(bf16[8,16,256]{2,1,0:T(8,128)(2,1)S(1)} %get-tuple-element.16.refs_0_.rest_0_), channel_id=1, source_target_pairs={{16,0},{24,8},{0,16},{8,24},{17,1},{25,9},{1,17},{9,25},{18,2},{26... | collective-permute-start | bytes 196616 | tf_op jit(solution)/shard_map/ppermute | solution.py:413
  12.2 5.2 %collective-permute-start.4 = (bf16[8,16,256]{2,1,0:T(8,128)(2,1)S(1)}, bf16[8,16,256]{2,1,0:T(8,128)(2,1)S(1)}, u32[]{:S(2)}, u32[]{:S(2)}) collective-permute-start(bf16[8,16,256]{2,1,0:T(8,128)(2,1)S(1)} %get-tuple-element.16.refs_0_.rest_0_), channel_id=1, source_target_pairs={{8,0},{16,8},{24,16},{0,24},{9,1},{17,9},{25,17},{1,25},{10,2},{18... | collective-permute-start | bytes 196616 | tf_op jit(solution)/shard_map/ppermute | solution.py:413
  17.4 7.2 %collective-permute-start.7 = (bf16[20,16,256]{2,1,0:T(8,128)(2,1)S(1)}, bf16[20,16,256]{2,1,0:T(8,128)(2,1)S(1)}, u32[]{:S(2)}, u32[]{:S(2)}) collective-permute-start(bf16[20,16,256]{2,1,0:T(8,128)(2,1)S(1)} %get-tuple-element.17), channel_id=1, source_target_pairs={{2,0},{4,2},{6,4},{0,6},{3,1},{5,3},{7,5},{1,7},{10,8},{12,10},{14... | collective-permute-start | bytes 491528 | tf_op jit(solution)/shard_map/ppermute | solution.py:413
  19.9 7.8 %collective-permute-start.8 = (bf16[20,16,256]{2,1,0:T(8,128)(2,1)S(1)}, bf16[20,16,256]{2,1,0:T(8,128)(2,1)S(1)}, u32[]{:S(2)}, u32[]{:S(2)}) collective-permute-start(bf16[20,16,256]{2,1,0:T(8,128)(2,1)S(1)} %get-tuple-element.18), channel_id=1, source_target_pairs={{6,0},{0,2},{2,4},{4,6},{7,1},{1,3},{3,5},{5,7},{14,8},{8,10},{10,... | collective-permute-start | bytes 491528 | tf_op jit(solution)/shard_map/ppermute | solution.py:413
  27.7 14.3 %copy-start.4 = (f32[2,4,8,192]{3,2,1,0:T(8,128)S(1)}, f32[2,4,8,192]{3,2,1,0:T(8,128)}, u32[]{:S(2)}) copy-start(f32[2,4,8,192]{3,2,1,0:T(8,128)} %body_ref.1) | copy-start | bytes 147460
  27.8 14.3 %copy-start.6 = (f32[2,4,8,192]{3,2,1,0:T(8,128)S(1)}, f32[2,4,8,192]{3,2,1,0:T(8,128)}, u32[]{:S(2)}) copy-start(f32[2,4,8,192]{3,2,1,0:T(8,128)} %probe_ref.1) | copy-start | bytes 147460
  27.8 14.2 %copy-start.8 = (s32[2,4,8,7]{2,1,3,0:T(4,128)S(1)}, s32[2,4,8,7]{2,1,3,0:T(4,128)}, u32[]{:S(2)}) copy-start(s32[2,4,8,7]{2,1,3,0:T(4,128)} %param.11) | copy-start | bytes 5380
  27.8 14.2 %copy-start.11 = (s32[2,4,8]{2,1,0:T(4,128)S(1)}, s32[2,4,8]{2,1,0:T(4,128)}, u32[]{:S(2)}) copy-start(s32[2,4,8]{2,1,0:T(4,128)} %owner_ref.1) | copy-start | bytes 772
  40.4 1.6 %collective-permute-start.9 = (f32[4,8,8,256]{3,2,1,0:T(8,128)S(1)}, f32[4,8,8,256]{3,2,1,0:T(8,128)S(1)}, u32[]{:S(2)}, u32[]{:S(2)}) collective-permute-start(f32[4,8,8,256]{3,2,1,0:T(8,128)S(1)} %get-tuple-element.22), channel_id=1, source_target_pairs={{1,0},{0,1},{3,2},{2,3},{5,4},{4,5},{7,6},{6,7},{9,8},{8,9},{11,10... | collective-permute-start | bytes 786440 | tf_op jit(solution)/shard_map/ppermute | solution.py:413

commit v4 on v3

--- a/solution.py
+++ b/solution.py
@@ -16,6 +16,7 @@
 VMEM = pl.BlockSpec(memory_space=pltpu.VMEM)
 SMEM = pl.BlockSpec(memory_space=pltpu.SMEM)
 ANY = pl.BlockSpec(memory_space=pl.ANY)
+HBM = pl.BlockSpec(memory_space=pltpu.HBM)
 
 
 def axis_slots(peers, length, depth):
@@ -63,6 +64,8 @@
             else:
                 at = 1 + self.x_offsets.index(x[0]) if x[0] else 0
                 self.sources.append((at, x[1] * len_y + y[1]))
+        self.first_late = 1 + len(self.x_offsets)
+        self.early = [i for i, (at, _) in enumerate(self.sources) if at < self.first_late]
 
 
 def lane_iota(shape):
@@ -85,15 +88,60 @@
     return jnp.sum(jnp.where(rows == lane_iota((n, n)), line, 0.0), axis=1, keepdims=True)
 
 
-def pack_kernel(core_ref, blocks_ref, *refs):
+def doubled(block, wide):
+    body = block.shape[-1] - 128
+    wide[...] = jnp.zeros(wide.shape, F32)
+    wide[:, :body] = block[:, 128:].astype(F32)
+    rest = wide[...]
+    return block[:, :128], (rest + pltpu.roll(rest, body, 1)).astype(BF16)
+
+
+def tables_kernel(*refs):
+    count = (len(refs) - 9) // 2
+    blocks, plain, (off_out, self_out) = refs[:2], refs[2 : 2 + count], refs[-2:]
+    (diag_ref, up_w, low_w), copies_out = refs[2 + count : 5 + count], refs[5 + count : 5 + 2 * count]
+    wide, sem = refs[5 + 2 * count : 7 + 2 * count]
+    copies = [
+        pltpu.make_async_copy(a, b, sem.at[n])
+        for n, (a, b) in enumerate(zip(blocks + plain, (off_out, self_out) + copies_out))
+    ]
+    for copy in copies:
+        copy.start()
+    copies[0].wait()
+    copies[1].wait()
+    kinds_n, dof, _ = off_out.shape
+    body = dof - 128
+    span = 2 * dof
+    diag_ref[...] = jnp.ones(diag_ref.shape, F32)
+    rows = lax.broadcasted_iota(jnp.int32, (dof, 128), 0)
+    lane = lane_iota((dof, 128))
+    eyes = (rows == lane).astype(F32), (rows == 128 + lane % body).astype(F32)
+    first = lane < body
+    for p in range(kinds_n // 2):
+        pair = [doubled(off_out[2 * p + u], wide) for u in range(2)]
+        at = p * span
+        mixed = jnp.where(first, pair[0][1].astype(F32), pair[1][1].astype(F32)).astype(BF16)
+        for q, tile in enumerate((pair[0][0], mixed, pair[1][0])):
+            up_w[:dof, at + q * 128 : at + q * 128 + 128] = tile
+            up_w[dof:, at + q * 128 : at + q * 128 + 128] = tile[128:]
+        owns = [doubled(self_out[2 * p + u], wide) for u in range(2)]
+        for base, halves in ((0, pair), (kinds_n // 2 * span, owns)):
+            for side, lanes in enumerate(SIDES):
+                low_w[base + at : base + at + dof, lanes] = halves[0][side]
+                low_w[base + at + dof : base + at + dof + body, lanes] = halves[1][side][128:]
+                low_w[base + at + dof + body : base + at + span, lanes] = halves[1][side][:128]
+        for u in range(2):
+            for side, lanes in enumerate(SIDES):
+                found = jnp.sum(owns[u][side].astype(F32) * eyes[side], axis=0, keepdims=True)
+                diag_ref[2 * p + u : 2 * p + u + 1, lanes] = found
+    for copy in copies[2:]:
+        copy.wait()
+
+
+def pack_kernel(core_ref, diag_ref, *refs):
     own, got = refs[0:4], refs[4:8]
-    hi_ref, lo_ref, diag_ref, wide, flat = refs[8:]
-    dof = blocks_ref.shape[-1]
-    rows = lax.broadcasted_iota(jnp.int32, (dof, dof), 0)
-    eye = (rows == lane_iota((dof, dof))).astype(F32)
-    diag_ref[...] = jnp.ones(diag_ref.shape, F32)
-    for t in range(blocks_ref.shape[0]):
-        diag_ref[t : t + 1, :dof] = jnp.sum(blocks_ref[t].astype(F32) * eye, axis=0, keepdims=True)
+    hi_ref, lo_ref, wide, flat = refs[8:]
+    dof = own[0].shape[-1]
     first = core_ref[0] == 0
     len_x, links_n, len_y, half = own[3].shape
     lane = lane_iota((half, 128))
@@ -144,77 +192,123 @@
     return max(d for d in range(1, cap + 1) if n % d == 0)
 
 
-def sweep_kernel(window, refs_in, len_y, *rest):
+def read_notes(lines, len_y, body, diag_ref):
+    depth = lines[0].shape[0]
+    spread_rows = (lax.broadcasted_iota(jnp.int32, (128, 8 * 128), 0) - body) // len_y
+    spread_cols = lane_iota((128, 8 * 128)) // 128
+    spread = (jnp.minimum(spread_rows, 7) == spread_cols) & (spread_rows >= 0) & (spread_rows < 10)
+    found = jnp.dot(jnp.concatenate(lines, axis=0), spread.astype(BF16), preferred_element_type=F32)
+    for u in range(len(lines)):
+        part = found[u * depth : (u + 1) * depth]
+        kinds = [part[:, k * 128 : (k + 1) * 128] for k in range(7)]
+        density = part[:, 7 * 128 :]
+        scale = density * jnp.sqrt(density)
+        yield kinds, scale, [scale * scale / pivot_of(kinds[6], diag_ref, lanes) for lanes in SIDES]
+
+
+def batches(items, cap):
+    size = divisor(len(items), cap)
+    return [items[i : i + size] for i in range(0, len(items), size)]
+
+
+def ready_kernel(window, refs_in, len_y, body, *rest):
     pieces = rest[:refs_in]
-    (lo_ref, diag_ref, off_ref, self_ref, near_ref, keep_ref, send_ref) = rest[refs_in : refs_in + 7]
-    (ship_a, ship_b, own_a, own_b, kinds, kinds_16, gain, scale, up_w, low_w, lhs) = rest[refs_in + 7 :]
-    dof = off_ref.shape[-1]
-    kinds_n = off_ref.shape[0]
+    lo_ref, diag_ref, ship, ship_own, kinds, kinds_16, gain, scale = rest[refs_in:]
+    own = window.count[0]
+    lane = lane_iota((ship.shape[1], 128))
+    for n, i in enumerate(window.early):
+        at, j = window.sources[i]
+        unpack(pieces[at][j], lo_ref[j] if i < own else None, n, lane < body, body, ship, ship_own)
+    for group in batches([(n, i) for n, i in enumerate(window.early) if i < window.count[ITERS - 1]], 8):
+        lines = [pieces[window.sources[i][0]][window.sources[i][1], :, 128:] for _, i in group]
+        for (n, i), (kind, s, gains) in zip(group, read_notes(lines, len_y, body, diag_ref)):
+            for k in range(7):
+                if i < own:
+                    kinds[n, k] = kind[k]
+                else:
+                    kinds_16[n, k] = kind[k].astype(BF16)
+            if i < own:
+                scale[n] = s
+            for lanes, g in zip(SIDES, gains):
+                gain[n, :, lanes] = g
+
+
+def unpack(piece, low, n, first, body, ship, ship_own):
+    for side, lanes in enumerate(SIDES):
+        x = piece[:, lanes].astype(F32)
+        if side:
+            x = jnp.where(first, x, pltpu.roll(x, body, 1))
+        ship[n, :, lanes] = x.astype(BF16)
+        if low is not None:
+            y = low[:, lanes].astype(F32)
+            if side:
+                y = jnp.where(first, y, pltpu.roll(y, body, 1))
+            ship_own[n, :, lanes] = x + y
+
+
+def sweep_kernel(window, refs_in, len_y, body, *rest):
+    pieces = rest[:refs_in]
+    (ship_in, own_a, kinds, kinds_in, gain_in, scale, diag_ref, up_w, low_w, near_ref) = rest[refs_in : refs_in + 10]
+    (keep_ref, send_ref, ship_a, ship_b, own_b, own_c, kinds_16, gain, lhs) = rest[refs_in + 10 :]
+    kinds_n = diag_ref.shape[0]
     depth = ship_a.shape[1]
     half = depth // 2
     own = window.count[0]
     targets = window.count[ITERS - 1]
-    up_w[...] = jnp.zeros(up_w.shape, BF16)
-    low_w[...] = jnp.zeros(low_w.shape, BF16)
-    for t in range(kinds_n):
-        up_w[:dof, t * LANES : t * LANES + dof] = off_ref[t]
-        low_w[t * LANES : t * LANES + dof, :dof] = off_ref[t]
-        low_w[(kinds_n + t) * LANES : (kinds_n + t) * LANES + dof, :dof] = self_ref[t]
-    for i, (at, j) in enumerate(window.sources):
-        ship_a[i] = pieces[at][j]
-        if i < own:
-            own_a[i] = pieces[at][j].astype(F32) + lo_ref[j].astype(F32)
-    spread_rows = (lax.broadcasted_iota(jnp.int32, (128, 8 * 128), 0) - (dof - 128)) // len_y
-    spread_cols = lane_iota((128, 8 * 128)) // 128
-    spread = (jnp.minimum(spread_rows, 7) == spread_cols) & (spread_rows >= 0) & (spread_rows < 10)
-    spread = spread.astype(BF16)
-    batch = divisor(targets, 8)
-    for c in range(targets // batch):
-        lines = [pieces[at][j, :, 128:] for at, j in window.sources[c * batch : (c + 1) * batch]]
-        found = jnp.dot(jnp.concatenate(lines, axis=0), spread, preferred_element_type=F32)
-        for u in range(batch):
-            i = c * batch + u
-            part = found[u * depth : (u + 1) * depth]
+    first = lane_iota((depth, 128)) < body
+    late = [i for i in range(len(window.keys)) if i not in window.early]
+    for n, i in enumerate(window.early):
+        ship_a[i] = ship_in[n]
+        if i < targets:
+            gain[i] = gain_in[n]
+            if i >= own:
+                kinds_16[i] = kinds_in[n]
+    for i in late:
+        at, j = window.sources[i]
+        unpack(pieces[at - window.first_late][j], None, i, first, body, ship_a, None)
+    for group in batches([i for i in late if i < targets], 8):
+        lines = [pieces[window.sources[i][0] - window.first_late][window.sources[i][1], :, 128:] for i in group]
+        for i, (kind, _, gains) in zip(group, read_notes(lines, len_y, body, diag_ref)):
             for k in range(7):
-                if i < own:
-                    kinds[i, k] = part[:, k * 128 : (k + 1) * 128]
-                else:
-                    kinds_16[i, k] = part[:, k * 128 : (k + 1) * 128].astype(BF16)
-            density = part[:, 7 * 128 :]
-            s = density * jnp.sqrt(density)
-            if i < own:
-                scale[i] = s
-            for lanes in SIDES:
-                gain[i, :, lanes] = s * s / pivot_of(part[:, 6 * 128 : 7 * 128], diag_ref, lanes)
+                kinds_16[i, k] = kind[k].astype(BF16)
+            for lanes, g in zip(SIDES, gains):
+                gain[i, :, lanes] = g
 
     def build(get, kind, i, table, row, low_row):
-        for side, lanes in enumerate(SIDES):
+        nears = []
+        for lanes in SIDES:
             mine = get(i, lanes)
             wide = mine.astype(F32)
-            zero = jnp.zeros((), mine.dtype)
-            nears = [
-                get(table[0], lanes),
-                get(table[1], lanes),
-                pltpu.roll(wide, depth - 1, 0).astype(mine.dtype),
-                get(table[2], lanes),
-                get(table[3], lanes),
-                pltpu.roll(wide, 1, 0).astype(mine.dtype),
-                mine,
-            ]
-            for t in range(kinds_n):
-                for g, ks in enumerate(((0, 1, 2), (3, 4, 5), (6,))):
+            nears.append(
+                [
+                    get(table[0], lanes),
+                    get(table[1], lanes),
+                    pltpu.roll(wide, depth - 1, 0).astype(mine.dtype),
+                    get(table[2], lanes),
+                    get(table[3], lanes),
+                    pltpu.roll(wide, 1, 0).astype(mine.dtype),
+                    mine,
+                ]
+            )
+        dtype = nears[0][0].dtype
+        zero = jnp.zeros((), dtype)
+        at = 0
+        for ks in ((0, 1, 2), (3, 4, 5), (6,)):
+            for t in range(0, kinds_n, 2):
+                mixed = jnp.where(first, float(t), float(t + 1)).astype(dtype)
+                for side, wanted in ((0, jnp.asarray(t, dtype)), (1, mixed), (0, jnp.asarray(t + 1, dtype))):
                     total = None
                     for k in ks:
-                        term = jnp.where(kind[i, k] == jnp.asarray(t, mine.dtype), nears[k], zero)
+                        term = jnp.where(kind[i, k] == wanted, nears[side][k], zero)
                         total = term if total is None else total + term
-                    at = (g * kinds_n + t) * LANES + side * 128
                     hi = total.astype(BF16)
                     lhs[row : row + depth, at : at + 128] = hi
                     if low_row is not None:
                         lhs[low_row : low_row + depth, at : at + 128] = (total - hi.astype(F32)).astype(BF16)
+                    at += 128
 
     def product(start, stop):
-        n = kinds_n * LANES
+        n = up_w.shape[1]
         acc = lax.dot_general(
             lhs[start:stop, :n], up_w[...], (((1,), (1,)), ((), ())), preferred_element_type=F32
         )
@@ -223,7 +317,7 @@
     base = 2 * own * depth
     for step in range(ITERS):
         src, dst = (ship_b, ship_a) if step % 2 else (ship_a, ship_b)
-        src_own, dst_own = (own_b, own_a) if step % 2 else (own_a, own_b)
+        src_own, dst_own = ((own_a, own_b), (own_b, own_c), (own_c, own_b), (own_b, own_c))[step]
 
         def get_own(i, lanes):
             if i < own:
@@ -236,8 +330,10 @@
         acc = product(0, base)
         for u in range(own):
             both = acc[u * depth : (u + 1) * depth] + acc[(own + u) * depth : (own + u + 1) * depth]
-            for lanes in SIDES:
+            for side, lanes in enumerate(SIDES):
                 value = both[:, lanes] * scale[u]
+                if side:
+                    value = jnp.where(first, value, 0.0)
                 keep_ref[step, u, :, lanes] = value[:half]
                 send_ref[step, u, :, lanes] = value[half:]
             if step < ITERS - 1:
@@ -249,13 +345,13 @@
             batch = divisor(halo, 14)
 
             def one(c, carry):
-                first = own + c * batch
+                start = own + c * batch
                 for u in range(batch):
-                    table = [near_ref[first + u, k] for k in range(4)]
-                    build(lambda i, lanes: src[i, :, lanes], kinds_16, first + u, table, base + u * depth, None)
+                    table = [near_ref[start + u, k] for k in range(4)]
+                    build(lambda i, lanes: src[i, :, lanes], kinds_16, start + u, table, base + u * depth, None)
                 acc = product(base, base + batch * depth)
                 for u in range(batch):
-                    dst[first + u] = (acc[u * depth : (u + 1) * depth] * gain[first + u]).astype(BF16)
+                    dst[start + u] = (acc[u * depth : (u + 1) * depth] * gain[start + u]).astype(BF16)
                 return carry
 
             lax.fori_loop(0, halo // batch, one, 0)
@@ -415,7 +511,7 @@
 
 def fits(shape):
     _, len_y, half, dof = shape
-    return half % 8 == 0 and 128 < dof and dof + 10 * len_y <= LANES
+    return half % 8 == 0 and dof == 192 and 10 * len_y <= LANES - dof
 
 
 def by_field(body_load, probe_load, density, link_types, off_blocks, self_blocks, block_owner):
@@ -426,21 +522,40 @@
     window = Window(lax.axis_size("gx"), lax.axis_size("gy"), len_x, len_y)
     core = lax.axis_index("gz").reshape(1)
     kinds = jnp.transpose(link_types, (0, 3, 1, 2))
-    mine = (body_load, probe_load, density, kinds)
-    theirs = tuple(shifted(a, "gz", 1) for a in mine)
-    hi, lo, diag = pl.pallas_call(
+    given = (body_load, probe_load, density, kinds)
+    theirs = tuple(shifted(a, "gz", 1) for a in given)
+    plain = given + (block_owner,)
+    span = kinds_n * dof
+    diag, up_w, low_w, *plain = pl.pallas_call(
+        tables_kernel,
+        out_shape=(
+            jax.ShapeDtypeStruct((kinds_n, LANES), F32),
+            jax.ShapeDtypeStruct((LANES, span), BF16),
+            jax.ShapeDtypeStruct((2 * span, LANES), BF16),
+            *(jax.ShapeDtypeStruct(a.shape, a.dtype) for a in plain),
+        ),
+        in_specs=[HBM] * (2 + len(plain)),
+        out_specs=(VMEM,) * (3 + len(plain)),
+        scratch_shapes=[
+            pltpu.VMEM((dof, 128), F32),
+            pltpu.SemaphoreType.DMA((2 + len(plain),)),
+            pltpu.VMEM(off_blocks.shape, BF16),
+            pltpu.VMEM(self_blocks.shape, BF16),
+        ],
+        compiler_params=small(8),
+        cost_estimate=pl.CostEstimate(flops=10**6, bytes_accessed=8 * 10**6, transcendentals=0),
+        name="tables",
+    )(*(pltpu.with_memory_space_constraint(a, pltpu.HBM) for a in (off_blocks, self_blocks, *plain)))
+    body_load, probe_load, density, kinds, block_owner = plain
+    hi, lo = pl.pallas_call(
         pack_kernel,
-        out_shape=(
-            jax.ShapeDtypeStruct((cols, depth, LANES), BF16),
-            jax.ShapeDtypeStruct((cols, depth, LANES), BF16),
-            jax.ShapeDtypeStruct((kinds_n, LANES), F32),
-        ),
+        out_shape=(jax.ShapeDtypeStruct((cols, depth, LANES), BF16),) * 2,
         in_specs=[SMEM] + [VMEM] * 9,
-        out_specs=(VMEM,) * 3,
+        out_specs=(VMEM,) * 2,
         scratch_shapes=[pltpu.VMEM((2 * cols, half, LANES), F32), pltpu.VMEM((128, 128), F32)],
         compiler_params=small(8),
         name="pack",
-    )(core, self_blocks, *mine, *theirs)
+    )(core, diag, *plain[:4], *theirs)
     from_x = [hi] + [shifted(hi, "gx", o) for o in window.x_offsets]
     copies = []
     for o in window.y_offsets:
@@ -458,31 +573,45 @@
         compiler_params=small(8),
         name="assemble",
     )(*from_x)
-    pieces = from_x + [shifted(m, "gy", o) for m, o in zip(messages, window.y_offsets)]
+    late = [shifted(m, "gy", o) for m, o in zip(messages, window.y_offsets)]
     own = window.count[0]
     targets = window.count[ITERS - 1]
-    rows = depth * (2 * own + 14)
+    early = len(window.early)
+    batch = 14
+    ready = pl.pallas_call(
+        functools.partial(ready_kernel, window, len(from_x), len_y, dof - 128),
+        out_shape=(
+            jax.ShapeDtypeStruct((early, depth, LANES), BF16),
+            jax.ShapeDtypeStruct((own, depth, LANES), F32),
+            jax.ShapeDtypeStruct((own, 7, depth, 128), F32),
+            jax.ShapeDtypeStruct((early, 7, depth, 128), BF16),
+            jax.ShapeDtypeStruct((early, depth, LANES), F32),
+            jax.ShapeDtypeStruct((own, depth, 128), F32),
+        ),
+        in_specs=[VMEM] * (len(from_x) + 2),
+        out_specs=(VMEM,) * 6,
+        compiler_params=small(8),
+        cost_estimate=pl.CostEstimate(flops=10**8, bytes_accessed=4 * 10**6, transcendentals=0),
+        name="ready",
+    )(*from_x, lo, diag)
+    rows = depth * (2 * own + batch)
     keep, send = pl.pallas_call(
-        functools.partial(sweep_kernel, window, len(pieces), len_y),
+        functools.partial(sweep_kernel, window, len(late), len_y, dof - 128),
         out_shape=(jax.ShapeDtypeStruct((ITERS, cols, half, LANES), F32),) * 2,
-        in_specs=[VMEM] * (len(pieces) + 4) + [SMEM],
+        in_specs=[VMEM] * (len(late) + 9) + [SMEM],
         out_specs=(VMEM,) * 2,
         scratch_shapes=[
             pltpu.VMEM((window.count[ITERS], depth, LANES), BF16),
             pltpu.VMEM((targets, depth, LANES), BF16),
             pltpu.VMEM((own, depth, LANES), F32),
             pltpu.VMEM((own, depth, LANES), F32),
-            pltpu.VMEM((own, 7, depth, 128), F32),
             pltpu.VMEM((targets, 7, depth, 128), BF16),
             pltpu.VMEM((targets, depth, LANES), F32),
-            pltpu.VMEM((own, depth, 128), F32),
-            pltpu.VMEM((LANES, kinds_n * LANES), BF16),
-            pltpu.VMEM((2 * kinds_n * LANES, LANES), BF16),
-            pltpu.VMEM((rows, 3 * kinds_n * LANES), BF16),
+            pltpu.VMEM((rows, 3 * span), BF16),
         ],
-        compiler_params=small(20),
+        compiler_params=small(16),
         name="sweeps",
-    )(*pieces, lo, diag, off_blocks, self_blocks, jnp.asarray(window.neighbours))
+    )(*late, *ready, diag, up_w, low_w, jnp.asarray(window.neighbours))
     back = shifted(send, "gz", 1)
     owners = lax.axis_size("gx") * lax.axis_size("gy") * lax.axis_size("gz")
     message, pre_state, pre_adjoint = pl.pallas_call(

time: 54.4 us -> 48.7 us (0.90)
  local copies, waits for them, and re-layouts: 3.46 us -> 0.01 us
  waiting for transfers between devices: 14.5 us -> 12.4 us
    unnamed x24 -> x2, local copies, waits for them, and re-layouts: 3.46 us -> 0.01 us
    ppermute x10, waiting for transfers between devices: 14.5 us -> 12.4 us  [shifted(): lax.ppermute(array, axis, [((i + offset) % peers, i) for i in range(peers)])]
    pallas_call x1 -> x3, Pallas kernels: 12.6 us -> 12.5 us  [the longest x1 10.4 us: by_field(): pl.pallas_call(functools.partial(sweep_kernel, window, len(late), len_y,...]
  transfers between devices with their start and end apart: 10 -> 10, of which waited for: 7 -> 6; matrix products, arithmetic and copies ran while one was open for 0% -> 0% of each run, Pallas kernels for 0% -> 4%
where the time goes in v4:
time: 48.7 us; the launch traced here: 48.6 us
  Pallas kernels  14.5 us (30%)
  waiting for transfers between devices  12.4 us (25%)
  starting transfers between devices  10.6 us (22%)
  blocking collectives  10.3 us (21%)
  between operations  0.72 us (1%)
    ppermute x10, waiting for transfers between devices, shifted(): lax.ppermute(array, axis, [((i + offset) % peers, i) for i in range(peers)])  12.4 us
    ppermute x10, starting transfers between devices, shifted(): lax.ppermute(array, axis, [((i + offset) % peers, i) for i in range(peers)])  10.6 us
    pallas_call x1, Pallas kernels, by_field(): pl.pallas_call(functools.partial(sweep_kernel, window, len(late), len_y,...  10.4 us
    all_to_all x1, blocking collectives, by_field(): message = lax.all_to_all(message, ('gx', 'gy', 'gz'), 0, 0, tiled=True)  10.3 us
    pallas_call x1, Pallas kernels, by_field(): pl.pallas_call(tables_kernel, out_shape=(jax.ShapeDtypeStruct((kinds_n, L...  1.64 us
    pallas_call x1, Pallas kernels, by_field(): pl.pallas_call(finish_kernel, out_shape=(jax.ShapeDtypeStruct((cols, half...  1.05 us
  transfers between devices with their start and end apart: 10, of which 6 were waited for; matrix products, arithmetic and copies ran while one was open for 0% of the time, Pallas kernels for 4%

profile of v4, /device:TPU:0, one launch (start us, length us, event | category | flops | bytes accessed | tf_op | source)
XLA Modules:
  0.0 48.6 jit_solution(18120827985229628029)
XLA Ops:
  0.6 0.5 %collective-permute-start = (f32[2,4,8,192]{3,2,1,0:T(8,128)}, f32[2,4,8,192]{3,2,1,0:T(8,128)S(1)}, u32[]{:S(2)}, u32[]{:S(2)}) collective-permute-start(f32[2,4,8,192]{3,2,1,0:T(8,128)} %refs_2_.1), channel_id=1, source_target_pairs={{1,0},{0,1},{3,2},{2,3},{5,4},{4,5},{7,6},{6,7},{9,8},{8,9},{11,10... | collective-permute-start | bytes 147464 | tf_op jit(solution)/shard_map/ppermute | solution.py:509
  1.2 0.1 collective-permute-start.1
  1.2 0.4 collective-permute-start.3
  1.7 0.1 collective-permute-start.2
  1.7 1.6 %tables.1 = (f32[4,256]{1,0:T(4,128)S(1)}, bf16[256,768]{1,0:T(8,128)(2,1)S(1)}, bf16[1536,256]{1,0:T(8,128)(2,1)S(1)}, f32[2,4,8,192]{3,2,1,0:T(8,128)S(1)}, f3...) custom-call(bf16[4,192,192]{2,1,0:T(8,128)(2,1)} %refs_0_.1, ...), custom_call_target="tpu_custom_call" | custom-call | flops 1000000 | bytes 8000000 | tf_op jit(solution)/shard_map/tables/pallas_call | solution.py:529
  3.4 0.0 collective-permute-done.refs_4_
  3.4 0.0 collective-permute-done.1.refs_5_
  3.4 0.3 pack.1
  3.7 3.1 %collective-permute-start.6 = (bf16[8,16,256]{2,1,0:T(8,128)(2,1)S(1)}, bf16[8,16,256]{2,1,0:T(8,128)(2,1)S(1)}, u32[]{:S(2)}, u32[]{:S(2)}) collective-permute-start(bf16[8,16,256]{2,1,0:T(8,128)(2,1)S(1)} %get-tuple-element.35.refs_0_.rest_0_), channel_id=1, source_target_pairs={{24,0},{0,8},{8,16},{16,24},{25,1},{1,9},{9,17},{17,25},{26,2},{2,... | collective-permute-start | bytes 196616 | tf_op jit(solution)/shard_map/ppermute | solution.py:509
  6.8 2.6 %collective-permute-start.5 = (bf16[8,16,256]{2,1,0:T(8,128)(2,1)S(1)}, bf16[8,16,256]{2,1,0:T(8,128)(2,1)S(1)}, u32[]{:S(2)}, u32[]{:S(2)}) collective-permute-start(bf16[8,16,256]{2,1,0:T(8,128)(2,1)S(1)} %get-tuple-element.35.refs_0_.rest_0_), channel_id=1, source_target_pairs={{16,0},{24,8},{0,16},{8,24},{17,1},{25,9},{1,17},{9,25},{18,2},{26... | collective-permute-start | bytes 196616 | tf_op jit(solution)/shard_map/ppermute | solution.py:509
  9.4 1.3 %collective-permute-start.4 = (bf16[8,16,256]{2,1,0:T(8,128)(2,1)S(1)}, bf16[8,16,256]{2,1,0:T(8,128)(2,1)S(1)}, u32[]{:S(2)}, u32[]{:S(2)}) collective-permute-start(bf16[8,16,256]{2,1,0:T(8,128)(2,1)S(1)} %get-tuple-element.35.refs_0_.rest_0_), channel_id=1, source_target_pairs={{8,0},{16,8},{24,16},{0,24},{9,1},{17,9},{25,17},{1,25},{10,2},{18... | collective-permute-start | bytes 196616 | tf_op jit(solution)/shard_map/ppermute | solution.py:509
  10.7 0.6 %collective-permute-done.6.refs_3_.rest_3_ = bf16[8,16,256]{2,1,0:T(8,128)(2,1)S(1)} collective-permute-done((bf16[8,16,256]{2,1,0:T(8,128)(2,1)S(1)}, bf16[8,16,256]{2,1,0:T(8,128)(2,1)S(1)}, u32[]{:S(2)}, u32[]{:S(2)}) %collective-permute-start.6) | collective-permute-done | bytes 65568 | tf_op jit(solution)/shard_map/ppermute | solution.py:509
  11.4 2.7 %collective-permute-done.5.refs_2_.rest_2_ = bf16[8,16,256]{2,1,0:T(8,128)(2,1)S(1)} collective-permute-done((bf16[8,16,256]{2,1,0:T(8,128)(2,1)S(1)}, bf16[8,16,256]{2,1,0:T(8,128)(2,1)S(1)}, u32[]{:S(2)}, u32[]{:S(2)}) %collective-permute-start.5) | collective-permute-done | bytes 65568 | tf_op jit(solution)/shard_map/ppermute | solution.py:509
  14.1 0.3 collective-permute-done.4.refs_1_.rest_1_
  14.4 2.5 %collective-permute-start.7 = (bf16[20,16,256]{2,1,0:T(8,128)(2,1)S(1)}, bf16[20,16,256]{2,1,0:T(8,128)(2,1)S(1)}, u32[]{:S(2)}, u32[]{:S(2)}) collective-permute-start(bf16[20,16,256]{2,1,0:T(8,128)(2,1)S(1)} %get-tuple-element.36), channel_id=1, source_target_pairs={{2,0},{4,2},{6,4},{0,6},{3,1},{5,3},{7,5},{1,7},{10,8},{12,10},{14... | collective-permute-start | bytes 491528 | tf_op jit(solution)/shard_map/ppermute | solution.py:509
  16.8 0.5 %ready.1 = (bf16[32,16,256]{2,1,0:T(8,128)(2,1)S(1)}, f32[8,16,256]{2,1,0:T(8,128)S(1)}, f32[8,7,16,128]{3,2,1,0:T(8,128)S(1)}, bf16[32,7,16,128]{3,2,1,0:T(8,12...) custom-call(bf16[8,16,256]{2,1,0:T(8,128)(2,1)S(1)} %get-tuple-element.35.refs_0_.rest_0_, ...), custom_call_target="tpu_custom_call" | custom-call | flops 100000000 | bytes 4000000 | tf_op jit(solution)/shard_map/ready/pallas_call | solution.py:581
  17.4 4.1 %collective-permute-done.7.rest_0_ = bf16[20,16,256]{2,1,0:T(8,128)(2,1)S(1)} collective-permute-done((bf16[20,16,256]{2,1,0:T(8,128)(2,1)S(1)}, bf16[20,16,256]{2,1,0:T(8,128)(2,1)S(1)}, u32[]{:S(2)}, u32[]{:S(2)}) %collective-permute-start.7) | collective-permute-done | bytes 163872 | tf_op jit(solution)/shard_map/ppermute | solution.py:509
  21.5 3.1 %collective-permute-done.8.rest_1_ = bf16[20,16,256]{2,1,0:T(8,128)(2,1)S(1)} collective-permute-done((bf16[20,16,256]{2,1,0:T(8,128)(2,1)S(1)}, bf16[20,16,256]{2,1,0:T(8,128)(2,1)S(1)}, u32[]{:S(2)}, u32[]{:S(2)}) %collective-permute-start.8) | collective-permute-done | bytes 163872 | tf_op jit(solution)/shard_map/ppermute | solution.py:509
  24.6 10.4 %sweeps.1 = (f32[4,8,8,256]{3,2,1,0:T(8,128)S(1)}, f32[4,8,8,256]{3,2,1,0:T(8,128)S(1)}) custom-call(bf16[20,16,256]{2,1,0:T(8,128)(2,1)S(1)} %collective-permute-done.7.rest_0_, bf16[20,16,256]{2,1,0:T(8,128)(2,1)S(1)} %collective-permute-done.8.rest_1_, bf16[32,16,256]{2,1,0:T(8,128)(2,1)S(1)} %get-tuple-element.39.rest_2_, ...), custom_call_target="tpu_custom_call" | custom-call | tf_op jit(solution)/shard_map/sweeps/pallas_call | solution.py:598
  35.0 0.1 collective-permute-start.9
  35.1 1.5 %collective-permute-done.9.got = f32[4,8,8,256]{3,2,1,0:T(8,128)S(1)} collective-permute-done((f32[4,8,8,256]{3,2,1,0:T(8,128)S(1)}, f32[4,8,8,256]{3,2,1,0:T(8,128)S(1)}, u32[]{:S(2)}, u32[]{:S(2)}) %collective-permute-start.9) | collective-permute-done | bytes 262176 | tf_op jit(solution)/shard_map/ppermute | solution.py:509
  36.6 0.6 %moments.1 = (f32[32,2,128]{2,1,0:T(2,128)S(1)}, f32[4,8,8,256]{3,2,1,0:T(8,128)S(1)}, f32[4,8,8,256]{3,2,1,0:T(8,128)S(1)}) custom-call(s32[1]{0:T(128)} %bitcast.core_ref, f32[2,4,8,192]{3,2,1,0:T(8,128)S(1)} %get-tuple-element.29.refs_0_.body_ref, f32[2,4,8,192]{3,2,1,0:T(8,128)S(1)} %get-tuple-element.30.refs_1_.probe_ref, ...), custom_call_target="tpu_custom_call" | custom-call | tf_op jit(solution)/shard_map/moments/pallas_call | solution.py:617
  37.2 10.3 %all_to_all.5.message_ref = f32[32,2,128]{2,1,0:T(2,128)S(1)} all-to-all(f32[32,2,128]{2,1,0:T(2,128)S(1)} %get-tuple-element.49), channel_id=1, replica_groups=mesh['gx'=4,'gy'=4,'gz'=2] {'gx','gy','gz'}, dimensions={0} | all-to-all | bytes 65536 | tf_op jit(solution)/shard_map/all_to_all | solution.py:630
  47.5 1.1 %finish.1 = (f32[8,8,192]{2,1,0:T(8,128)}, f32[8,8,192]{2,1,0:T(8,128)}, f32[1,8]{1,0:T(1,128)}) custom-call(f32[32,2,128]{2,1,0:T(2,128)S(1)} %all_to_all.5.message_ref, f32[4,8,8,256]{3,2,1,0:T(8,128)S(1)} %get-tuple-element.50.pre_state_ref, f32[4,8,8,256]{3,2,1,0:T(8,128)S(1)} %get-tuple-element.51.pre_adjoint_ref), custom_call_target="tpu_custom_call" | custom-call | tf_op jit(solution)/shard_map/finish/pallas_call | solution.py:631
  (6 shorter events, 0.0 us)
Async XLA Ops:
  0.6 2.8 %collective-permute-start = (f32[2,4,8,192]{3,2,1,0:T(8,128)}, f32[2,4,8,192]{3,2,1,0:T(8,128)S(1)}, u32[]{:S(2)}, u32[]{:S(2)}) collective-permute-start(f32[2,4,8,192]{3,2,1,0:T(8,128)} %refs_2_.1), channel_id=1, source_target_pairs={{1,0},{0,1},{3,2},{2,3},{5,4},{4,5},{7,6},{6,7},{9,8},{8,9},{11,10... | collective-permute-start | bytes 147464 | tf_op jit(solution)/shard_map/ppermute | solution.py:509
  1.2 2.3 %collective-permute-start.1 = (f32[2,4,8,192]{3,2,1,0:T(8,128)}, f32[2,4,8,192]{3,2,1,0:T(8,128)S(1)}, u32[]{:S(2)}, u32[]{:S(2)}) collective-permute-start(f32[2,4,8,192]{3,2,1,0:T(8,128)} %refs_3_.1), channel_id=1, source_target_pairs={{1,0},{0,1},{3,2},{2,3},{5,4},{4,5},{7,6},{6,7},{9,8},{8,9},{11,10... | collective-permute-start | bytes 147464 | tf_op jit(solution)/shard_map/ppermute | solution.py:509
  1.2 2.2 %collective-permute-start.3 = (s32[2,7,4,8]{3,2,1,0:T(4,128)}, s32[2,7,4,8]{3,2,1,0:T(4,128)S(1)}, u32[]{:S(2)}, u32[]{:S(2)}) collective-permute-start(s32[2,7,4,8]{3,2,1,0:T(4,128)} %bitcast.5), channel_id=1, source_target_pairs={{1,0},{0,1},{3,2},{2,3},{5,4},{4,5},{7,6},{6,7},{9,8},{8,9},{11,10... | collective-permute-start | bytes 5384 | tf_op jit(solution)/shard_map/ppermute | solution.py:509
  1.7 1.7 %collective-permute-start.2 = (f32[2,4,8]{2,1,0:T(4,128)}, f32[2,4,8]{2,1,0:T(4,128)S(1)}, u32[]{:S(2)}, u32[]{:S(2)}) collective-permute-start(f32[2,4,8]{2,1,0:T(4,128)} %refs_4_.1), channel_id=1, source_target_pairs={{1,0},{0,1},{3,2},{2,3},{5,4},{4,5},{7,6},{6,7},{9,8},{8,9},{11,10... | collective-permute-start | bytes 776 | tf_op jit(solution)/shard_map/ppermute | solution.py:509
  3.7 7.6 %collective-permute-start.6 = (bf16[8,16,256]{2,1,0:T(8,128)(2,1)S(1)}, bf16[8,16,256]{2,1,0:T(8,128)(2,1)S(1)}, u32[]{:S(2)}, u32[]{:S(2)}) collective-permute-start(bf16[8,16,256]{2,1,0:T(8,128)(2,1)S(1)} %get-tuple-element.35.refs_0_.rest_0_), channel_id=1, source_target_pairs={{24,0},{0,8},{8,16},{16,24},{25,1},{1,9},{9,17},{17,25},{26,2},{2,... | collective-permute-start | bytes 196616 | tf_op jit(solution)/shard_map/ppermute | solution.py:509
  6.8 7.3 %collective-permute-start.5 = (bf16[8,16,256]{2,1,0:T(8,128)(2,1)S(1)}, bf16[8,16,256]{2,1,0:T(8,128)(2,1)S(1)}, u32[]{:S(2)}, u32[]{:S(2)}) collective-permute-start(bf16[8,16,256]{2,1,0:T(8,128)(2,1)S(1)} %get-tuple-element.35.refs_0_.rest_0_), channel_id=1, source_target_pairs={{16,0},{24,8},{0,16},{8,24},{17,1},{25,9},{1,17},{9,25},{18,2},{26... | collective-permute-start | bytes 196616 | tf_op jit(solution)/shard_map/ppermute | solution.py:509
  9.4 4.9 %collective-permute-start.4 = (bf16[8,16,256]{2,1,0:T(8,128)(2,1)S(1)}, bf16[8,16,256]{2,1,0:T(8,128)(2,1)S(1)}, u32[]{:S(2)}, u32[]{:S(2)}) collective-permute-start(bf16[8,16,256]{2,1,0:T(8,128)(2,1)S(1)} %get-tuple-element.35.refs_0_.rest_0_), channel_id=1, source_target_pairs={{8,0},{16,8},{24,16},{0,24},{9,1},{17,9},{25,17},{1,25},{10,2},{18... | collective-permute-start | bytes 196616 | tf_op jit(solution)/shard_map/ppermute | solution.py:509
  14.4 7.2 %collective-permute-start.7 = (bf16[20,16,256]{2,1,0:T(8,128)(2,1)S(1)}, bf16[20,16,256]{2,1,0:T(8,128)(2,1)S(1)}, u32[]{:S(2)}, u32[]{:S(2)}) collective-permute-start(bf16[20,16,256]{2,1,0:T(8,128)(2,1)S(1)} %get-tuple-element.36), channel_id=1, source_target_pairs={{2,0},{4,2},{6,4},{0,6},{3,1},{5,3},{7,5},{1,7},{10,8},{12,10},{14... | collective-permute-start | bytes 491528 | tf_op jit(solution)/shard_map/ppermute | solution.py:509
  16.8 7.8 %collective-permute-start.8 = (bf16[20,16,256]{2,1,0:T(8,128)(2,1)S(1)}, bf16[20,16,256]{2,1,0:T(8,128)(2,1)S(1)}, u32[]{:S(2)}, u32[]{:S(2)}) collective-permute-start(bf16[20,16,256]{2,1,0:T(8,128)(2,1)S(1)} %get-tuple-element.37), channel_id=1, source_target_pairs={{6,0},{0,2},{2,4},{4,6},{7,1},{1,3},{3,5},{5,7},{14,8},{8,10},{10,... | collective-permute-start | bytes 491528 | tf_op jit(solution)/shard_map/ppermute | solution.py:509
  16.8 7.8 %copy-start = (s32[56,4]{1,0:T(8,128)S(1)}, s32[56,4]{1,0:T(8,128)}, u32[]{:S(2)}) copy-start(s32[56,4]{1,0:T(8,128)} %constant.6.clone.rest_11_) | copy-start | bytes 2692
  35.0 1.6 %collective-permute-start.9 = (f32[4,8,8,256]{3,2,1,0:T(8,128)S(1)}, f32[4,8,8,256]{3,2,1,0:T(8,128)S(1)}, u32[]{:S(2)}, u32[]{:S(2)}) collective-permute-start(f32[4,8,8,256]{3,2,1,0:T(8,128)S(1)} %get-tuple-element.48), channel_id=1, source_target_pairs={{1,0},{0,1},{3,2},{2,3},{5,4},{4,5},{7,6},{6,7},{9,8},{8,9},{11,10... | collective-permute-start | bytes 786440 | tf_op jit(solution)/shard_map/ppermute | solution.py:509

commit v5 on v4

--- a/solution.py
+++ b/solution.py
@@ -65,7 +65,28 @@
                 at = 1 + self.x_offsets.index(x[0]) if x[0] else 0
                 self.sources.append((at, x[1] * len_y + y[1]))
         self.first_late = 1 + len(self.x_offsets)
+        cols = len_x * len_y
+        self.tiles = 3 * ((cols + 1) // 2) + (len_x + 1) // 2
+        wanted = self.keys[: self.count[ITERS - 1]]
+        self.y_notes = {
+            o: sorted({(x[0], x[1] // 2) for x, y in wanted if y[0] == o}) for o in self.y_offsets
+        }
+        self.notes = []
+        for x, y in wanted:
+            if y[0]:
+                at = 1 + len(self.x_offsets) + self.y_offsets.index(y[0])
+                before = 3 * ((len(self.y_columns[y[0]]) + 1) // 2)
+                j = before + self.y_notes[y[0]].index((x[0], x[1] // 2))
+            else:
+                at = 1 + self.x_offsets.index(x[0]) if x[0] else 0
+                j = 3 * ((cols + 1) // 2) + x[1] // 2
+            self.notes.append((at, j, x[1], y[1]))
         self.early = [i for i, (at, _) in enumerate(self.sources) if at < self.first_late]
+        self.late = [i for i, (at, _) in enumerate(self.sources) if at >= self.first_late]
+        self.ready = [i for i in self.early if self.count[0] <= i < self.count[ITERS - 1]]
+        self.inside = [
+            i for i, table in enumerate(self.neighbours) if i in self.early and all(n in self.early for n in table)
+        ]
 
 
 def lane_iota(shape):
@@ -147,7 +168,8 @@
     lane = lane_iota((half, 128))
     body_lanes = dof - 128
     flat[...] = jnp.zeros(flat.shape, F32)
-    turned, notes = {}, {}
+    turned = {}
+    cols = len_x * len_y
     for x in range(len_x):
         for h, (_, _, density_ref, types_ref) in enumerate((own, got)):
             for k in range(links_n):
@@ -158,34 +180,50 @@
             for k, v in enumerate((density, rest, last)):
                 flat[(links_n + k) * len_y : (links_n + k + 1) * len_y, :half] = v
             turned[x, h] = jnp.transpose(flat[...])[:half]
-            notes[x, h] = pltpu.roll(turned[x, h], body_lanes, 1)
     for x in range(len_x):
         for y in range(len_y):
             i = x * len_y + y
             parts = []
-            for h, (body_ref, probe_ref, density_ref, types_ref) in enumerate((own, got)):
+            for h, (body_ref, probe_ref, _, _) in enumerate((own, got)):
                 slot = i * 2 + h
                 wide[slot, :, :dof] = jnp.where(first, body_ref[x, y], probe_ref[x, y])
                 kind = turned[x, h][:, (links_n - 1) * len_y + y : (links_n - 1) * len_y + y + 1]
                 density = turned[x, h][:, links_n * len_y + y : links_n * len_y + y + 1]
                 scale = density * jnp.sqrt(density)
                 ship = [(wide[slot, :, lanes] / pivot_of(kind, diag_ref, lanes)) * scale for lanes in SIDES]
+                ship[1] = jnp.where(lane < body_lanes, ship[1], 0.0)
                 his = [v.astype(BF16).astype(F32) for v in ship]
-                los = [v - u for v, u in zip(ship, his)]
-                note = jnp.where(lane % len_y == y, notes[x, h], 0.0)
-                his[1] = jnp.where(lane < body_lanes, his[1], note)
-                los[1] = jnp.where(lane < body_lanes, los[1], 0.0)
-                parts.append((his, los))
+                parts.append((his, [v - u for v, u in zip(ship, his)]))
             for side, lanes in enumerate(SIDES):
-                hi_ref[i, :, lanes] = jnp.concatenate([p[0][side] for p in parts], axis=0).astype(BF16)
                 lo_ref[i, :, lanes] = jnp.concatenate([p[1][side] for p in parts], axis=0).astype(BF16)
-
-
-def assemble_kernel(lines, count_in, *refs):
+            main, rest = (jnp.concatenate([p[0][side] for p in parts], axis=0) for side in range(2))
+            hi_ref[3 * (i // 2) + i % 2] = main.astype(BF16)
+            if i % 2 == 0:
+                before = rest
+            if i % 2 or i == cols - 1:
+                pair = before + pltpu.roll(rest, body_lanes, 1) if i % 2 else rest
+                hi_ref[3 * (i // 2) + 2] = pair.astype(BF16)
+    for x in range(0, len_x, 2):
+        tile = jnp.concatenate([turned[x, h] for h in range(2)], axis=0)
+        if x + 1 < len_x:
+            tile = tile + pltpu.roll(jnp.concatenate([turned[x + 1, h] for h in range(2)], axis=0), body_lanes, 1)
+        hi_ref[3 * ((cols + 1) // 2) + x // 2] = tile.astype(BF16)
+
+
+def assemble_kernel(lines, count_in, body, *refs):
     ins, outs = refs[:count_in], refs[count_in:]
-    for out, line in zip(outs, lines):
-        for to, (at, j) in enumerate(line):
-            out[to] = ins[at][j]
+    for out, (columns, notes) in zip(outs, lines):
+        for to in range(0, len(columns), 2):
+            pair = None
+            for u, (at, j) in enumerate(columns[to : to + 2]):
+                out[3 * (to // 2) + u] = ins[at][3 * (j // 2) + j % 2]
+                rest = ins[at][3 * (j // 2) + 2].astype(F32)
+                if u != j % 2:
+                    rest = pltpu.roll(rest, body, 1)
+                pair = rest if pair is None else jnp.where(lane_iota(rest.shape) < body, pair, rest)
+            out[3 * (to // 2) + 2] = pair.astype(BF16)
+        for n, (at, j) in enumerate(notes):
+            out[3 * ((len(columns) + 1) // 2) + n] = ins[at][j]
 
 
 def divisor(n, cap):
@@ -194,9 +232,9 @@
 
 def read_notes(lines, len_y, body, diag_ref):
     depth = lines[0].shape[0]
-    spread_rows = (lax.broadcasted_iota(jnp.int32, (128, 8 * 128), 0) - body) // len_y
+    spread_rows = lax.broadcasted_iota(jnp.int32, (128, 8 * 128), 0) % body // len_y
     spread_cols = lane_iota((128, 8 * 128)) // 128
-    spread = (jnp.minimum(spread_rows, 7) == spread_cols) & (spread_rows >= 0) & (spread_rows < 10)
+    spread = (jnp.minimum(spread_rows, 7) == spread_cols) & (spread_rows < 10)
     found = jnp.dot(jnp.concatenate(lines, axis=0), spread.astype(BF16), preferred_element_type=F32)
     for u in range(len(lines)):
         part = found[u * depth : (u + 1) * depth]
@@ -207,37 +245,17 @@
 
 
 def batches(items, cap):
-    size = divisor(len(items), cap)
+    size = divisor(len(items), cap) if items else 1
     return [items[i : i + size] for i in range(0, len(items), size)]
 
 
-def ready_kernel(window, refs_in, len_y, body, *rest):
-    pieces = rest[:refs_in]
-    lo_ref, diag_ref, ship, ship_own, kinds, kinds_16, gain, scale = rest[refs_in:]
-    own = window.count[0]
-    lane = lane_iota((ship.shape[1], 128))
-    for n, i in enumerate(window.early):
-        at, j = window.sources[i]
-        unpack(pieces[at][j], lo_ref[j] if i < own else None, n, lane < body, body, ship, ship_own)
-    for group in batches([(n, i) for n, i in enumerate(window.early) if i < window.count[ITERS - 1]], 8):
-        lines = [pieces[window.sources[i][0]][window.sources[i][1], :, 128:] for _, i in group]
-        for (n, i), (kind, s, gains) in zip(group, read_notes(lines, len_y, body, diag_ref)):
-            for k in range(7):
-                if i < own:
-                    kinds[n, k] = kind[k]
-                else:
-                    kinds_16[n, k] = kind[k].astype(BF16)
-            if i < own:
-                scale[n] = s
-            for lanes, g in zip(SIDES, gains):
-                gain[n, :, lanes] = g
-
-
-def unpack(piece, low, n, first, body, ship, ship_own):
+def unpack(piece, j, low, n, first, body, ship, ship_own):
+    main = piece[3 * (j // 2) + j % 2].astype(F32)
+    rest = piece[3 * (j // 2) + 2].astype(F32)
+    turned = pltpu.roll(rest, body, 1)
+    rest = jnp.where(first, turned, rest) if j % 2 else jnp.where(first, rest, turned)
     for side, lanes in enumerate(SIDES):
-        x = piece[:, lanes].astype(F32)
-        if side:
-            x = jnp.where(first, x, pltpu.roll(x, body, 1))
+        x = rest if side else main
         ship[n, :, lanes] = x.astype(BF16)
         if low is not None:
             y = low[:, lanes].astype(F32)
@@ -246,115 +264,216 @@
             ship_own[n, :, lanes] = x + y
 
 
-def sweep_kernel(window, refs_in, len_y, body, *rest):
-    pieces = rest[:refs_in]
-    (ship_in, own_a, kinds, kinds_in, gain_in, scale, diag_ref, up_w, low_w, near_ref) = rest[refs_in : refs_in + 10]
-    (keep_ref, send_ref, ship_a, ship_b, own_b, own_c, kinds_16, gain, lhs) = rest[refs_in + 10 :]
-    kinds_n = diag_ref.shape[0]
-    depth = ship_a.shape[1]
-    half = depth // 2
-    own = window.count[0]
-    targets = window.count[ITERS - 1]
-    first = lane_iota((depth, 128)) < body
-    late = [i for i in range(len(window.keys)) if i not in window.early]
-    for n, i in enumerate(window.early):
-        ship_a[i] = ship_in[n]
-        if i < targets:
-            gain[i] = gain_in[n]
-            if i >= own:
-                kinds_16[i] = kinds_in[n]
-    for i in late:
-        at, j = window.sources[i]
-        unpack(pieces[at - window.first_late][j], None, i, first, body, ship_a, None)
-    for group in batches([i for i in late if i < targets], 8):
-        lines = [pieces[window.sources[i][0] - window.first_late][window.sources[i][1], :, 128:] for i in group]
-        for i, (kind, _, gains) in zip(group, read_notes(lines, len_y, body, diag_ref)):
-            for k in range(7):
-                kinds_16[i, k] = kind[k].astype(BF16)
-            for lanes, g in zip(SIDES, gains):
-                gain[i, :, lanes] = g
-
-    def build(get, kind, i, table, row, low_row):
-        nears = []
+def note_lines(window, pieces, skip, group, len_y, body, depth):
+    lane = lane_iota((depth, 128))
+    lines = []
+    for i in group:
+        at, j, layer, y = window.notes[i]
+        mine = (lane // body == layer % 2) & (lane % len_y == y)
+        lines.append(pieces[at - skip][j] * jnp.where(mine, 1.0, 0.0).astype(BF16))
+    return lines
+
+
+class Columns:
+    def __init__(self, *places):
+        self.at = {i: (ref, n) for ref, columns in places for n, i in enumerate(columns)}
+
+    def __call__(self, i, *rest):
+        ref, n = self.at[i]
+        return ref[(n, *rest)]
+
+
+def tiles_of(kinds_n):
+    for t in range(0, kinds_n, 2):
+        yield from ((t, t), (t, t + 1), (t + 1, t + 1))
+
+
+def build(near, kind, mask, lhs, row, low_row, first, kinds_n):
+    depth = near[0][0].shape[0]
+    dtype = near[0][0].dtype
+    zero = jnp.zeros((), dtype)
+    at = 0
+    for ks in ((0, 1, 2), (3, 4, 5), (6,)):
+        for t in range(0, kinds_n, 2):
+            mixed = jnp.where(first, float(t), float(t + 1)).astype(dtype)
+            for side, wanted in ((0, jnp.asarray(t, dtype)), (1, mixed), (0, jnp.asarray(t + 1, dtype))):
+                total = None
+                for k in ks:
+                    if mask is None:
+                        term = jnp.where(kind(k) == wanted, near[side][k], zero)
+                    else:
+                        term = near[side][k] * mask(k * 3 * kinds_n // 2 + at // 128 % (3 * kinds_n // 2))
+                    total = term if total is None else total + term
+                hi = total.astype(BF16)
+                lhs[row : row + depth, at : at + 128] = hi
+                if low_row is not None:
+                    lhs[low_row : low_row + depth, at : at + 128] = (total - hi.astype(F32)).astype(BF16)
+                at += 128
+
+
+def advance(window, own, halo, get_own, get, kinds, kinds_16, masks, up_w, low_w, lhs, first):
+    kinds_n = up_w.shape[1] // 192
+    depth = first.shape[0]
+
+    def around(fetch, i):
+        table = window.neighbours[i]
+        sides = []
         for lanes in SIDES:
-            mine = get(i, lanes)
+            mine = fetch(i, lanes)
             wide = mine.astype(F32)
-            nears.append(
-                [
-                    get(table[0], lanes),
-                    get(table[1], lanes),
-                    pltpu.roll(wide, depth - 1, 0).astype(mine.dtype),
-                    get(table[2], lanes),
-                    get(table[3], lanes),
-                    pltpu.roll(wide, 1, 0).astype(mine.dtype),
-                    mine,
-                ]
-            )
-        dtype = nears[0][0].dtype
-        zero = jnp.zeros((), dtype)
-        at = 0
-        for ks in ((0, 1, 2), (3, 4, 5), (6,)):
-            for t in range(0, kinds_n, 2):
-                mixed = jnp.where(first, float(t), float(t + 1)).astype(dtype)
-                for side, wanted in ((0, jnp.asarray(t, dtype)), (1, mixed), (0, jnp.asarray(t + 1, dtype))):
-                    total = None
-                    for k in ks:
-                        term = jnp.where(kind[i, k] == wanted, nears[side][k], zero)
-                        total = term if total is None else total + term
-                    hi = total.astype(BF16)
-                    lhs[row : row + depth, at : at + 128] = hi
-                    if low_row is not None:
-                        lhs[low_row : low_row + depth, at : at + 128] = (total - hi.astype(F32)).astype(BF16)
-                    at += 128
+            above, below = (pltpu.roll(wide, by, 0).astype(mine.dtype) for by in (depth - 1, 1))
+            x0, y0, x1, y1 = (fetch(int(n), lanes) for n in table)
+            sides.append([x0, y0, above, x1, y1, below, mine])
+        return sides
+
+    n = up_w.shape[1]
 
     def product(start, stop):
-        n = up_w.shape[1]
         acc = lax.dot_general(
             lhs[start:stop, :n], up_w[...], (((1,), (1,)), ((), ())), preferred_element_type=F32
         )
         return acc + jnp.dot(lhs[start:stop, n:], low_w[...], preferred_element_type=F32)
 
-    base = 2 * own * depth
+    base = 2 * len(own) * depth
+    for u, i in enumerate(own):
+        build(around(get_own, i), lambda k: kinds(i, k), None, lhs, u * depth, (len(own) + u) * depth, first, kinds_n)
+    accs = []
+    if own:
+        accs.append((own, True, product(0, base)))
+    for group in batches(halo, 14):
+        for u, i in enumerate(group):
+            mask = (lambda n: masks(i, n)) if i in masks.at else None
+            build(around(get, i), lambda k: kinds_16(i, k), mask, lhs, base + u * depth, None, first, kinds_n)
+        accs.append((group, False, product(base, base + len(group) * depth)))
+        base += len(group) * depth
+    for group, paired, acc in accs:
+        for u, i in enumerate(group):
+            if paired:
+                n = len(group)
+                yield i, acc[u * depth : (u + 1) * depth] + acc[(n + u) * depth : (n + u + 1) * depth]
+            else:
+                yield i, acc[u * depth : (u + 1) * depth]
+
+
+def deliver(image, scale, first, keep_ref, send_ref, step, u):
+    half = keep_ref.shape[2]
+    for side, lanes in enumerate(SIDES):
+        value = image[:, lanes] * scale
+        if side:
+            value = jnp.where(first, value, 0.0)
+        keep_ref[step, u, :, lanes] = value[:half]
+        send_ref[step, u, :, lanes] = value[half:]
+
+
+def ready_kernel(window, refs_in, len_y, body, *rest):
+    pieces = rest[:refs_in]
+    lo_ref, diag_ref, up_w, low_w = rest[refs_in : refs_in + 4]
+    ship, ship_own, kinds, masks, gain, scale, done, done_own, image, lhs = rest[refs_in + 4 :]
+    own = window.count[0]
+    depth = ship.shape[1]
+    first = lane_iota((depth, 128)) < body
+    kinds_n = diag_ref.shape[0]
+    for n, i in enumerate(window.early):
+        at, j = window.sources[i]
+        unpack(pieces[at], j, lo_ref[j] if i < own else None, n, first, body, ship, ship_own)
+    for group in batches([(n, i) for n, i in enumerate(window.early) if i < window.count[ITERS - 1]], 8):
+        lines = note_lines(window, pieces, 0, [i for _, i in group], len_y, body, depth)
+        for (n, i), (kind, s, gains) in zip(group, read_notes(lines, len_y, body, diag_ref)):
+            for k in range(7):
+                if i < own:
+                    kinds[n, k] = kind[k]
+                    continue
+                for q, (low, high) in enumerate(tiles_of(kinds_n)):
+                    wanted = jnp.where(first, float(low), float(high)) if low != high else float(low)
+                    at = k * 3 * kinds_n // 2 + q
+                    masks[n - own, at] = jnp.where(kind[k] == wanted, 1.0, 0.0).astype(BF16)
+            if i < own:
+                scale[n] = s
+            for lanes, g in zip(SIDES, gains):
+                gain[n, :, lanes] = g
+    get = Columns((ship, window.early))
+
+    def get_own(i, lanes):
+        if i < own:
+            return ship_own[i, :, lanes]
+        return get(i, slice(None), lanes).astype(F32)
+
+    for i, value in advance(
+        window, [i for i in window.inside if i < own], [i for i in window.inside if i >= own], get_own,
+        lambda i, lanes: get(i, slice(None), lanes), lambda i, k: kinds[i, k], None,
+        Columns((masks, window.ready)), up_w, low_w, lhs, first,
+    ):
+        n = window.inside.index(i)
+        moved = value * gain[window.early.index(i)]
+        done[n] = moved.astype(BF16)
+        if i < own:
+            done_own[n] = moved
+            image[n] = value
+
+
+def sweep_kernel(window, refs_in, len_y, body, *rest):
+    pieces = rest[:refs_in]
+    (ship_in, own_a, kinds, masks_in, gain_in, scale, done, done_own, image, diag_ref, up_w, low_w) = rest[
+        refs_in : refs_in + 12
+    ]
+    (keep_ref, send_ref, ship_late, ship_a, ship_b, own_b, own_c, kinds_late, gain_late, lhs) = rest[refs_in + 12 :]
+    depth = ship_a.shape[1]
+    own = window.count[0]
+    targets = window.count[ITERS - 1]
+    first = lane_iota((depth, 128)) < body
+    for n, i in enumerate(window.late):
+        at, j = window.sources[i]
+        unpack(pieces[at - window.first_late], j, None, n, first, body, ship_late, None)
+    for group in batches([(n, i) for n, i in enumerate(window.late) if i < targets], 8):
+        lines = note_lines(window, pieces, window.first_late, [i for _, i in group], len_y, body, depth)
+        for (n, i), (kind, _, gains) in zip(group, read_notes(lines, len_y, body, diag_ref)):
+            for k in range(7):
+                kinds_late[n, k] = kind[k].astype(BF16)
+            for lanes, g in zip(SIDES, gains):
+                gain_late[n, :, lanes] = g
+    kinds_16 = Columns((kinds_late, window.late))
+    masks = Columns((masks_in, window.ready))
+    gain = Columns((gain_in, window.early), (gain_late, window.late))
+    everything = list(range(targets))
+    ships = [
+        Columns((ship_in, window.early), (ship_late, window.late)),
+        Columns((ship_a, everything), (done, window.inside)),
+        Columns((ship_b, everything)),
+        Columns((ship_a, everything)),
+    ]
+    owns = [
+        Columns((own_a, everything[:own])),
+        Columns((own_b, everything[:own]), (done_own, [i for i in window.inside if i < own])),
+        Columns((own_c, everything[:own])),
+        Columns((own_b, everything[:own])),
+    ]
+    into = ((ship_a, own_b), (ship_b, own_c), (ship_a, own_b), None)
     for step in range(ITERS):
-        src, dst = (ship_b, ship_a) if step % 2 else (ship_a, ship_b)
-        src_own, dst_own = ((own_a, own_b), (own_b, own_c), (own_c, own_b), (own_b, own_c))[step]
+        wanted = [i for i in range(window.count[ITERS - 1 - step]) if step or i not in window.inside]
+
+        def get(i, lanes):
+            return ships[step](i, slice(None), lanes)
 
         def get_own(i, lanes):
             if i < own:
-                return src_own[i, :, lanes]
-            return src[i, :, lanes].astype(F32)
-
-        for u in range(own):
-            table = [int(n) for n in window.neighbours[u]]
-            build(get_own, kinds, u, table, u * depth, (own + u) * depth)
-        acc = product(0, base)
-        for u in range(own):
-            both = acc[u * depth : (u + 1) * depth] + acc[(own + u) * depth : (own + u + 1) * depth]
-            for side, lanes in enumerate(SIDES):
-                value = both[:, lanes] * scale[u]
-                if side:
-                    value = jnp.where(first, value, 0.0)
-                keep_ref[step, u, :, lanes] = value[:half]
-                send_ref[step, u, :, lanes] = value[half:]
-            if step < ITERS - 1:
-                value = both * gain[u]
-                dst_own[u] = value
-                dst[u] = value.astype(BF16)
-        halo = window.count[ITERS - 1 - step] - own
-        if halo:
-            batch = divisor(halo, 14)
-
-            def one(c, carry):
-                start = own + c * batch
-                for u in range(batch):
-                    table = [near_ref[start + u, k] for k in range(4)]
-                    build(lambda i, lanes: src[i, :, lanes], kinds_16, start + u, table, base + u * depth, None)
-                acc = product(base, base + batch * depth)
-                for u in range(batch):
-                    dst[start + u] = (acc[u * depth : (u + 1) * depth] * gain[start + u]).astype(BF16)
-                return carry
-
-            lax.fori_loop(0, halo // batch, one, 0)
+                return owns[step](i, slice(None), lanes)
+            return get(i, lanes).astype(F32)
+
+        if step == 0:
+            for n, i in enumerate(window.inside):
+                if i < own:
+                    deliver(image[n], scale[i], first, keep_ref, send_ref, step, i)
+        for i, value in advance(
+            window, [i for i in wanted if i < own], [i for i in wanted if i >= own], get_own, get,
+            lambda i, k: kinds[i, k], kinds_16, masks, up_w, low_w, lhs, first,
+        ):
+            if i < own:
+                deliver(value, scale[i], first, keep_ref, send_ref, step, i)
+            if into[step] is not None:
+                moved = value * gain(i)
+                into[step][0][i] = moved.astype(BF16)
+                if i < own:
+                    into[step][1][i] = moved
 
 
 def gram_index(i, j):
@@ -549,7 +668,10 @@
     body_load, probe_load, density, kinds, block_owner = plain
     hi, lo = pl.pallas_call(
         pack_kernel,
-        out_shape=(jax.ShapeDtypeStruct((cols, depth, LANES), BF16),) * 2,
+        out_shape=(
+            jax.ShapeDtypeStruct((window.tiles, depth, 128), BF16),
+            jax.ShapeDtypeStruct((cols, depth, LANES), BF16),
+        ),
         in_specs=[SMEM] + [VMEM] * 9,
         out_specs=(VMEM,) * 2,
         scratch_shapes=[pltpu.VMEM((2 * cols, half, LANES), F32), pltpu.VMEM((128, 128), F32)],
@@ -559,14 +681,18 @@
     from_x = [hi] + [shifted(hi, "gx", o) for o in window.x_offsets]
     copies = []
     for o in window.y_offsets:
-        lines = []
-        for x, y in window.y_columns[o]:
-            lines.append((1 + window.x_offsets.index(x[0]) if x[0] else 0, x[1] * len_y + y[1]))
-        copies.append(lines)
+        columns = [
+            (1 + window.x_offsets.index(x[0]) if x[0] else 0, x[1] * len_y + y[1]) for x, y in window.y_columns[o]
+        ]
+        notes = [
+            (1 + window.x_offsets.index(dev) if dev else 0, 3 * ((cols + 1) // 2) + n) for dev, n in window.y_notes[o]
+        ]
+        copies.append((columns, notes))
     messages = pl.pallas_call(
-        functools.partial(assemble_kernel, copies, len(from_x)),
+        functools.partial(assemble_kernel, copies, len(from_x), dof - 128),
         out_shape=tuple(
-            jax.ShapeDtypeStruct((len(window.y_columns[o]), depth, LANES), BF16) for o in window.y_offsets
+            jax.ShapeDtypeStruct((3 * ((len(columns) + 1) // 2) + len(notes), depth, 128), BF16)
+            for columns, notes in copies
         ),
         in_specs=[VMEM] * len(from_x),
         out_specs=(VMEM,) * len(copies),
@@ -577,41 +703,47 @@
     own = window.count[0]
     targets = window.count[ITERS - 1]
     early = len(window.early)
-    batch = 14
+    inside = len(window.inside)
+    inside_own = sum(i < own for i in window.inside)
     ready = pl.pallas_call(
         functools.partial(ready_kernel, window, len(from_x), len_y, dof - 128),
         out_shape=(
             jax.ShapeDtypeStruct((early, depth, LANES), BF16),
             jax.ShapeDtypeStruct((own, depth, LANES), F32),
             jax.ShapeDtypeStruct((own, 7, depth, 128), F32),
-            jax.ShapeDtypeStruct((early, 7, depth, 128), BF16),
+            jax.ShapeDtypeStruct((len(window.ready), 21 * kinds_n // 2, depth, 128), BF16),
             jax.ShapeDtypeStruct((early, depth, LANES), F32),
             jax.ShapeDtypeStruct((own, depth, 128), F32),
+            jax.ShapeDtypeStruct((inside, depth, LANES), BF16),
+            jax.ShapeDtypeStruct((inside_own, depth, LANES), F32),
+            jax.ShapeDtypeStruct((inside_own, depth, LANES), F32),
         ),
-        in_specs=[VMEM] * (len(from_x) + 2),
-        out_specs=(VMEM,) * 6,
-        compiler_params=small(8),
+        in_specs=[VMEM] * (len(from_x) + 4),
+        out_specs=(VMEM,) * 9,
+        scratch_shapes=[pltpu.VMEM((depth * (inside + inside_own), 3 * span), BF16)],
+        compiler_params=small(16),
         cost_estimate=pl.CostEstimate(flops=10**8, bytes_accessed=4 * 10**6, transcendentals=0),
         name="ready",
-    )(*from_x, lo, diag)
-    rows = depth * (2 * own + batch)
+    )(*from_x, lo, diag, up_w, low_w)
+    rows = depth * (targets + own)
     keep, send = pl.pallas_call(
         functools.partial(sweep_kernel, window, len(late), len_y, dof - 128),
         out_shape=(jax.ShapeDtypeStruct((ITERS, cols, half, LANES), F32),) * 2,
-        in_specs=[VMEM] * (len(late) + 9) + [SMEM],
+        in_specs=[VMEM] * (len(late) + 12),
         out_specs=(VMEM,) * 2,
         scratch_shapes=[
-            pltpu.VMEM((window.count[ITERS], depth, LANES), BF16),
+            pltpu.VMEM((len(window.late), depth, LANES), BF16),
+            pltpu.VMEM((targets, depth, LANES), BF16),
             pltpu.VMEM((targets, depth, LANES), BF16),
             pltpu.VMEM((own, depth, LANES), F32),
             pltpu.VMEM((own, depth, LANES), F32),
-            pltpu.VMEM((targets, 7, depth, 128), BF16),
-            pltpu.VMEM((targets, depth, LANES), F32),
+            pltpu.VMEM((len(window.late), 7, depth, 128), BF16),
+            pltpu.VMEM((len(window.late), depth, LANES), F32),
             pltpu.VMEM((rows, 3 * span), BF16),
         ],
-        compiler_params=small(16),
+        compiler_params=small(24),
         name="sweeps",
-    )(*late, *ready, diag, up_w, low_w, jnp.asarray(window.neighbours))
+    )(*late, *ready, diag, up_w, low_w)
     back = shifted(send, "gz", 1)
     owners = lax.axis_size("gx") * lax.axis_size("gy") * lax.axis_size("gz")
     message, pre_state, pre_adjoint = pl.pallas_call(

time: 48.7 us -> 44.3 us (0.910)
  waiting for transfers between devices: 12.4 us -> 8.88 us
  Pallas kernels: 14.5 us -> 13.3 us
    ppermute x10, waiting for transfers between devices: 12.4 us -> 8.88 us  [shifted(): lax.ppermute(array, axis, [((i + offset) % peers, i) for i in range(peers)])]
    pallas_call x1, Pallas kernels: 10.4 us -> 7.39 us  [by_field(): pl.pallas_call(functools.partial(sweep_kernel, window, len(late), len_y,...]
    pallas_call x1, Pallas kernels: 0.53 us -> 2.07 us  [by_field(): pl.pallas_call(functools.partial(ready_kernel, window, len(from_x), len_y...]
  transfers between devices with their start and end apart: 10 -> 10, of which waited for: 6 -> 6; matrix products, arithmetic and copies ran while one was open for 0% -> 0% of each run, Pallas kernels for 4% -> 8%
where the time goes in v5:
time: 44.3 us; the launch traced here: 44.1 us
  Pallas kernels  13.3 us (30%)
  starting transfers between devices  10.6 us (24%)
  blocking collectives  10.6 us (24%)
  waiting for transfers between devices  8.88 us (20%)
  between operations  0.72 us (2%)
    ppermute x10, starting transfers between devices, shifted(): lax.ppermute(array, axis, [((i + offset) % peers, i) for i in range(peers)])  10.6 us
    all_to_all x1, blocking collectives, by_field(): message = lax.all_to_all(message, ('gx', 'gy', 'gz'), 0, 0, tiled=True)  10.6 us
    ppermute x10, waiting for transfers between devices, shifted(): lax.ppermute(array, axis, [((i + offset) % peers, i) for i in range(peers)])  8.88 us
    pallas_call x1, Pallas kernels, by_field(): pl.pallas_call(functools.partial(sweep_kernel, window, len(late), len_y,...  7.39 us
    pallas_call x1, Pallas kernels, by_field(): pl.pallas_call(functools.partial(ready_kernel, window, len(from_x), len_y...  2.07 us
    pallas_call x1, Pallas kernels, by_field(): pl.pallas_call(tables_kernel, out_shape=(jax.ShapeDtypeStruct((kinds_n, L...  1.64 us
    pallas_call x1, Pallas kernels, by_field(): pl.pallas_call(finish_kernel, out_shape=(jax.ShapeDtypeStruct((cols, half...  1.05 us
  transfers between devices with their start and end apart: 10, of which 6 were waited for; matrix products, arithmetic and copies ran while one was open for 0% of the time, Pallas kernels for 8%

profile of v5, /device:TPU:0, one launch (start us, length us, event | category | flops | bytes accessed | tf_op | source)
XLA Modules:
  0.0 44.1 jit_solution(12472520550505395590)
XLA Ops:
  0.6 0.5 %collective-permute-start = (f32[2,4,8,192]{3,2,1,0:T(8,128)}, f32[2,4,8,192]{3,2,1,0:T(8,128)S(1)}, u32[]{:S(2)}, u32[]{:S(2)}) collective-permute-start(f32[2,4,8,192]{3,2,1,0:T(8,128)} %refs_2_.1), channel_id=1, source_target_pairs={{1,0},{0,1},{3,2},{2,3},{5,4},{4,5},{7,6},{6,7},{9,8},{8,9},{11,10... | collective-permute-start | bytes 147464 | tf_op jit(solution)/shard_map/ppermute | solution.py:628
  1.2 0.1 collective-permute-start.1
  1.2 0.4 collective-permute-start.3
  1.7 0.1 collective-permute-start.2
  1.7 1.6 %tables.1 = (f32[4,256]{1,0:T(4,128)S(1)}, bf16[256,768]{1,0:T(8,128)(2,1)S(1)}, bf16[1536,256]{1,0:T(8,128)(2,1)S(1)}, f32[2,4,8,192]{3,2,1,0:T(8,128)S(1)}, f3...) custom-call(bf16[4,192,192]{2,1,0:T(8,128)(2,1)} %refs_0_.1, ...), custom_call_target="tpu_custom_call" | custom-call | flops 1000000 | bytes 8000000 | tf_op jit(solution)/shard_map/tables/pallas_call | solution.py:648
  3.4 0.0 collective-permute-done.2.refs_6_
  3.4 0.4 pack.1
  3.8 3.0 %collective-permute-start.6 = (bf16[13,16,128]{2,1,0:T(8,128)(2,1)S(1)}, bf16[13,16,128]{2,1,0:T(8,128)(2,1)S(1)}, u32[]{:S(2)}, u32[]{:S(2)}) collective-permute-start(bf16[13,16,128]{2,1,0:T(8,128)(2,1)S(1)} %get-tuple-element.38.refs_0_.rest_0_), channel_id=1, source_target_pairs={{24,0},{0,8},{8,16},{16,24},{25,1},{1,9},{9,17},{17,25},{26,2},{2,... | collective-permute-start | bytes 159752 | tf_op jit(solution)/shard_map/ppermute | solution.py:628
  6.8 2.6 %collective-permute-start.5 = (bf16[13,16,128]{2,1,0:T(8,128)(2,1)S(1)}, bf16[13,16,128]{2,1,0:T(8,128)(2,1)S(1)}, u32[]{:S(2)}, u32[]{:S(2)}) collective-permute-start(bf16[13,16,128]{2,1,0:T(8,128)(2,1)S(1)} %get-tuple-element.38.refs_0_.rest_0_), channel_id=1, source_target_pairs={{16,0},{24,8},{0,16},{8,24},{17,1},{25,9},{1,17},{9,25},{18,2},{26... | collective-permute-start | bytes 159752 | tf_op jit(solution)/shard_map/ppermute | solution.py:628
  9.4 1.3 %collective-permute-start.4 = (bf16[13,16,128]{2,1,0:T(8,128)(2,1)S(1)}, bf16[13,16,128]{2,1,0:T(8,128)(2,1)S(1)}, u32[]{:S(2)}, u32[]{:S(2)}) collective-permute-start(bf16[13,16,128]{2,1,0:T(8,128)(2,1)S(1)} %get-tuple-element.38.refs_0_.rest_0_), channel_id=1, source_target_pairs={{8,0},{16,8},{24,16},{0,24},{9,1},{17,9},{25,17},{1,25},{10,2},{18... | collective-permute-start | bytes 159752 | tf_op jit(solution)/shard_map/ppermute | solution.py:628
  10.8 0.3 collective-permute-done.6.refs_3_.rest_3_
  11.0 2.4 %collective-permute-done.5.refs_2_.rest_2_ = bf16[13,16,128]{2,1,0:T(8,128)(2,1)S(1)} collective-permute-done((bf16[13,16,128]{2,1,0:T(8,128)(2,1)S(1)}, bf16[13,16,128]{2,1,0:T(8,128)(2,1)S(1)}, u32[]{:S(2)}, u32[]{:S(2)}) %collective-permute-start.5) | collective-permute-done | bytes 53280 | tf_op jit(solution)/shard_map/ppermute | solution.py:628
  13.4 0.4 collective-permute-done.4.refs_1_.rest_1_
  13.8 0.1 assemble.1
  13.9 2.5 %collective-permute-start.7 = (bf16[33,16,128]{2,1,0:T(8,128)(2,1)S(1)}, bf16[33,16,128]{2,1,0:T(8,128)(2,1)S(1)}, u32[]{:S(2)}, u32[]{:S(2)}) collective-permute-start(bf16[33,16,128]{2,1,0:T(8,128)(2,1)S(1)} %get-tuple-element.39), channel_id=1, source_target_pairs={{2,0},{4,2},{6,4},{0,6},{3,1},{5,3},{7,5},{1,7},{10,8},{12,10},{14... | collective-permute-start | bytes 405512 | tf_op jit(solution)/shard_map/ppermute | solution.py:628
  16.4 2.1 %ready.1 = (bf16[32,16,256]{2,1,0:T(8,128)(2,1)S(1)}, f32[8,16,256]{2,1,0:T(8,128)S(1)}, f32[8,7,16,128]{3,2,1,0:T(8,128)S(1)}, bf16[24,42,16,128]{3,2,1,0:T(8,1...) custom-call(bf16[13,16,128]{2,1,0:T(8,128)(2,1)S(1)} %get-tuple-elem, ...), custom_call_target="tpu_custom_call" | custom-call | flops 100000000 | bytes 4000000 | tf_op jit(solution)/shard_map/ready/pallas_call | solution.py:708
  18.5 1.7 %collective-permute-done.7.rest_0_ = bf16[33,16,128]{2,1,0:T(8,128)(2,1)S(1)} collective-permute-done((bf16[33,16,128]{2,1,0:T(8,128)(2,1)S(1)}, bf16[33,16,128]{2,1,0:T(8,128)(2,1)S(1)}, u32[]{:S(2)}, u32[]{:S(2)}) %collective-permute-start.7) | collective-permute-done | bytes 135200 | tf_op jit(solution)/shard_map/ppermute | solution.py:628
  20.2 2.6 %collective-permute-done.8.rest_1_ = bf16[33,16,128]{2,1,0:T(8,128)(2,1)S(1)} collective-permute-done((bf16[33,16,128]{2,1,0:T(8,128)(2,1)S(1)}, bf16[33,16,128]{2,1,0:T(8,128)(2,1)S(1)}, u32[]{:S(2)}, u32[]{:S(2)}) %collective-permute-start.8) | collective-permute-done | bytes 135200 | tf_op jit(solution)/shard_map/ppermute | solution.py:628
  22.8 7.4 %sweeps.1 = (f32[4,8,8,256]{3,2,1,0:T(8,128)S(1)}, f32[4,8,8,256]{3,2,1,0:T(8,128)S(1)}) custom-call(bf16[33,16,128]{2,1,0:T(8,128)(2,1)S(1)} %collective-permute-done.7.rest_0_, bf16[33,16,128]{2,1,0:T(8,128)(2,1)S(1)} %collective-permute-done.8.rest_1_, bf16[32,16,256]{2,1,0:T(8,128)(2,1)S(1)} %get-tuple-element.44.rest_2_, ...), custom_call_target="tpu_custom_call" | custom-call | tf_op jit(solution)/shard_map/sweeps/pallas_call | solution.py:729
  30.2 0.1 collective-permute-start.9
  30.3 1.5 %collective-permute-done.9.got = f32[4,8,8,256]{3,2,1,0:T(8,128)S(1)} collective-permute-done((f32[4,8,8,256]{3,2,1,0:T(8,128)S(1)}, f32[4,8,8,256]{3,2,1,0:T(8,128)S(1)}, u32[]{:S(2)}, u32[]{:S(2)}) %collective-permute-start.9) | collective-permute-done | bytes 262176 | tf_op jit(solution)/shard_map/ppermute | solution.py:628
  31.8 0.6 %moments.1 = (f32[32,2,128]{2,1,0:T(2,128)S(1)}, f32[4,8,8,256]{3,2,1,0:T(8,128)S(1)}, f32[4,8,8,256]{3,2,1,0:T(8,128)S(1)}) custom-call(s32[1]{0:T(128)} %bitcast.core_ref, f32[2,4,8,192]{3,2,1,0:T(8,128)S(1)} %get-tuple-element.32.refs_0_.body_ref, f32[2,4,8,192]{3,2,1,0:T(8,128)S(1)} %get-tuple-element.33.refs_1_.probe_ref, ...), custom_call_target="tpu_custom_call" | custom-call | tf_op jit(solution)/shard_map/moments/pallas_call | solution.py:749
  32.4 10.6 %all_to_all.5.message_ref = f32[32,2,128]{2,1,0:T(2,128)S(1)} all-to-all(f32[32,2,128]{2,1,0:T(2,128)S(1)} %get-tuple-element.55), channel_id=1, replica_groups=mesh['gx'=4,'gy'=4,'gz'=2] {'gx','gy','gz'}, dimensions={0} | all-to-all | bytes 65536 | tf_op jit(solution)/shard_map/all_to_all | solution.py:762
  43.0 1.1 %finish.1 = (f32[8,8,192]{2,1,0:T(8,128)}, f32[8,8,192]{2,1,0:T(8,128)}, f32[1,8]{1,0:T(1,128)}) custom-call(f32[32,2,128]{2,1,0:T(2,128)S(1)} %all_to_all.5.message_ref, f32[4,8,8,256]{3,2,1,0:T(8,128)S(1)} %get-tuple-element.56.pre_state_ref, f32[4,8,8,256]{3,2,1,0:T(8,128)S(1)} %get-tuple-element.57.pre_adjoint_ref), custom_call_target="tpu_custom_call" | custom-call | tf_op jit(solution)/shard_map/finish/pallas_call | solution.py:763
  (4 shorter events, 0.0 us)
Async XLA Ops:
  0.6 2.8 %collective-permute-start = (f32[2,4,8,192]{3,2,1,0:T(8,128)}, f32[2,4,8,192]{3,2,1,0:T(8,128)S(1)}, u32[]{:S(2)}, u32[]{:S(2)}) collective-permute-start(f32[2,4,8,192]{3,2,1,0:T(8,128)} %refs_2_.1), channel_id=1, source_target_pairs={{1,0},{0,1},{3,2},{2,3},{5,4},{4,5},{7,6},{6,7},{9,8},{8,9},{11,10... | collective-permute-start | bytes 147464 | tf_op jit(solution)/shard_map/ppermute | solution.py:628
  1.2 2.3 %collective-permute-start.1 = (f32[2,4,8,192]{3,2,1,0:T(8,128)}, f32[2,4,8,192]{3,2,1,0:T(8,128)S(1)}, u32[]{:S(2)}, u32[]{:S(2)}) collective-permute-start(f32[2,4,8,192]{3,2,1,0:T(8,128)} %refs_3_.1), channel_id=1, source_target_pairs={{1,0},{0,1},{3,2},{2,3},{5,4},{4,5},{7,6},{6,7},{9,8},{8,9},{11,10... | collective-permute-start | bytes 147464 | tf_op jit(solution)/shard_map/ppermute | solution.py:628
  1.2 2.2 %collective-permute-start.3 = (s32[2,7,4,8]{3,2,1,0:T(4,128)}, s32[2,7,4,8]{3,2,1,0:T(4,128)S(1)}, u32[]{:S(2)}, u32[]{:S(2)}) collective-permute-start(s32[2,7,4,8]{3,2,1,0:T(4,128)} %bitcast.5), channel_id=1, source_target_pairs={{1,0},{0,1},{3,2},{2,3},{5,4},{4,5},{7,6},{6,7},{9,8},{8,9},{11,10... | collective-permute-start | bytes 5384 | tf_op jit(solution)/shard_map/ppermute | solution.py:628
  1.7 1.7 %collective-permute-start.2 = (f32[2,4,8]{2,1,0:T(4,128)}, f32[2,4,8]{2,1,0:T(4,128)S(1)}, u32[]{:S(2)}, u32[]{:S(2)}) collective-permute-start(f32[2,4,8]{2,1,0:T(4,128)} %refs_4_.1), channel_id=1, source_target_pairs={{1,0},{0,1},{3,2},{2,3},{5,4},{4,5},{7,6},{6,7},{9,8},{8,9},{11,10... | collective-permute-start | bytes 776 | tf_op jit(solution)/shard_map/ppermute | solution.py:628
  3.8 7.2 %collective-permute-start.6 = (bf16[13,16,128]{2,1,0:T(8,128)(2,1)S(1)}, bf16[13,16,128]{2,1,0:T(8,128)(2,1)S(1)}, u32[]{:S(2)}, u32[]{:S(2)}) collective-permute-start(bf16[13,16,128]{2,1,0:T(8,128)(2,1)S(1)} %get-tuple-element.38.refs_0_.rest_0_), channel_id=1, source_target_pairs={{24,0},{0,8},{8,16},{16,24},{25,1},{1,9},{9,17},{17,25},{26,2},{2,... | collective-permute-start | bytes 159752 | tf_op jit(solution)/shard_map/ppermute | solution.py:628
  6.8 6.6 %collective-permute-start.5 = (bf16[13,16,128]{2,1,0:T(8,128)(2,1)S(1)}, bf16[13,16,128]{2,1,0:T(8,128)(2,1)S(1)}, u32[]{:S(2)}, u32[]{:S(2)}) collective-permute-start(bf16[13,16,128]{2,1,0:T(8,128)(2,1)S(1)} %get-tuple-element.38.refs_0_.rest_0_), channel_id=1, source_target_pairs={{16,0},{24,8},{0,16},{8,24},{17,1},{25,9},{1,17},{9,25},{18,2},{26... | collective-permute-start | bytes 159752 | tf_op jit(solution)/shard_map/ppermute | solution.py:628
  9.4 4.4 %collective-permute-start.4 = (bf16[13,16,128]{2,1,0:T(8,128)(2,1)S(1)}, bf16[13,16,128]{2,1,0:T(8,128)(2,1)S(1)}, u32[]{:S(2)}, u32[]{:S(2)}) collective-permute-start(bf16[13,16,128]{2,1,0:T(8,128)(2,1)S(1)} %get-tuple-element.38.refs_0_.rest_0_), channel_id=1, source_target_pairs={{8,0},{16,8},{24,16},{0,24},{9,1},{17,9},{25,17},{1,25},{10,2},{18... | collective-permute-start | bytes 159752 | tf_op jit(solution)/shard_map/ppermute | solution.py:628
  13.9 6.3 %collective-permute-start.7 = (bf16[33,16,128]{2,1,0:T(8,128)(2,1)S(1)}, bf16[33,16,128]{2,1,0:T(8,128)(2,1)S(1)}, u32[]{:S(2)}, u32[]{:S(2)}) collective-permute-start(bf16[33,16,128]{2,1,0:T(8,128)(2,1)S(1)} %get-tuple-element.39), channel_id=1, source_target_pairs={{2,0},{4,2},{6,4},{0,6},{3,1},{5,3},{7,5},{1,7},{10,8},{12,10},{14... | collective-permute-start | bytes 405512 | tf_op jit(solution)/shard_map/ppermute | solution.py:628
  16.4 6.4 %collective-permute-start.8 = (bf16[33,16,128]{2,1,0:T(8,128)(2,1)S(1)}, bf16[33,16,128]{2,1,0:T(8,128)(2,1)S(1)}, u32[]{:S(2)}, u32[]{:S(2)}) collective-permute-start(bf16[33,16,128]{2,1,0:T(8,128)(2,1)S(1)} %get-tuple-element.40), channel_id=1, source_target_pairs={{6,0},{0,2},{2,4},{4,6},{7,1},{1,3},{3,5},{5,7},{14,8},{8,10},{10,... | collective-permute-start | bytes 405512 | tf_op jit(solution)/shard_map/ppermute | solution.py:628
  30.2 1.6 %collective-permute-start.9 = (f32[4,8,8,256]{3,2,1,0:T(8,128)S(1)}, f32[4,8,8,256]{3,2,1,0:T(8,128)S(1)}, u32[]{:S(2)}, u32[]{:S(2)}) collective-permute-start(f32[4,8,8,256]{3,2,1,0:T(8,128)S(1)} %get-tuple-element.54), channel_id=1, source_target_pairs={{1,0},{0,1},{3,2},{2,3},{5,4},{4,5},{7,6},{6,7},{9,8},{8,9},{11,10... | collective-permute-start | bytes 786440 | tf_op jit(solution)/shard_map/ppermute | solution.py:628

commit v6 on v5

--- a/solution.py
+++ b/solution.py
@@ -16,7 +16,6 @@
 VMEM = pl.BlockSpec(memory_space=pltpu.VMEM)
 SMEM = pl.BlockSpec(memory_space=pltpu.SMEM)
 ANY = pl.BlockSpec(memory_space=pl.ANY)
-HBM = pl.BlockSpec(memory_space=pltpu.HBM)
 
 
 def axis_slots(peers, length, depth):
@@ -83,6 +82,13 @@
             self.notes.append((at, j, x[1], y[1]))
         self.early = [i for i, (at, _) in enumerate(self.sources) if at < self.first_late]
         self.late = [i for i, (at, _) in enumerate(self.sources) if at >= self.first_late]
+        early = set(self.early)
+        self.edges = [
+            i for i, table in enumerate(self.neighbours) if i in early and not all(int(n) in early for n in table)
+        ]
+        self.missing = {
+            k: [i for i in self.edges if int(self.neighbours[i][n]) not in early] for n, k in ((1, 1), (3, 4))
+        }
         self.ready = [i for i in self.early if self.count[0] <= i < self.count[ITERS - 1]]
         self.inside = [
             i for i, table in enumerate(self.neighbours) if i in self.early and all(n in self.early for n in table)
@@ -117,46 +123,47 @@
     return block[:, :128], (rest + pltpu.roll(rest, body, 1)).astype(BF16)
 
 
-def tables_kernel(*refs):
-    count = (len(refs) - 9) // 2
-    blocks, plain, (off_out, self_out) = refs[:2], refs[2 : 2 + count], refs[-2:]
-    (diag_ref, up_w, low_w), copies_out = refs[2 + count : 5 + count], refs[5 + count : 5 + 2 * count]
-    wide, sem = refs[5 + 2 * count : 7 + 2 * count]
-    copies = [
-        pltpu.make_async_copy(a, b, sem.at[n])
-        for n, (a, b) in enumerate(zip(blocks + plain, (off_out, self_out) + copies_out))
-    ]
+def bring_kernel(*refs):
+    count = (len(refs) - 2) // 2
+    given, (diag_ref, *taken), sem = refs[:count], refs[count:-1], refs[-1]
+    copies = [pltpu.make_async_copy(a, b, sem.at[n]) for n, (a, b) in enumerate(zip(given, taken))]
     for copy in copies:
         copy.start()
     copies[0].wait()
-    copies[1].wait()
-    kinds_n, dof, _ = off_out.shape
+    self_ref = taken[0]
+    kinds_n, dof, _ = self_ref.shape
+    body = dof - 128
+    diag_ref[...] = jnp.ones(diag_ref.shape, F32)
+    square = (lax.broadcasted_iota(jnp.int32, (128, 128), 0) == lane_iota((128, 128))).astype(F32)
+    for t in range(kinds_n):
+        diag_ref[t : t + 1, :128] = jnp.sum(self_ref[t, :128, :128].astype(F32) * square, axis=0, keepdims=True)
+        corner = self_ref[t, 128:, 128:].astype(F32) * square[:body, :body]
+        diag_ref[t : t + 1, 128:dof] = jnp.sum(corner, axis=0, keepdims=True)
+    rest = diag_ref[:, 128:]
+    first = lane_iota(rest.shape) < body
+    diag_ref[:, 128:] = jnp.where(first, rest, pltpu.roll(rest, body, 1))
+    for copy in copies[1:]:
+        copy.wait()
+
+
+def tables_kernel(off_ref, self_ref, up_w, low_w, wide):
+    kinds_n, dof, _ = off_ref.shape
     body = dof - 128
     span = 2 * dof
-    diag_ref[...] = jnp.ones(diag_ref.shape, F32)
-    rows = lax.broadcasted_iota(jnp.int32, (dof, 128), 0)
-    lane = lane_iota((dof, 128))
-    eyes = (rows == lane).astype(F32), (rows == 128 + lane % body).astype(F32)
-    first = lane < body
+    first = lane_iota((dof, 128)) < body
     for p in range(kinds_n // 2):
-        pair = [doubled(off_out[2 * p + u], wide) for u in range(2)]
+        pair = [doubled(off_ref[2 * p + u], wide) for u in range(2)]
         at = p * span
         mixed = jnp.where(first, pair[0][1].astype(F32), pair[1][1].astype(F32)).astype(BF16)
         for q, tile in enumerate((pair[0][0], mixed, pair[1][0])):
             up_w[:dof, at + q * 128 : at + q * 128 + 128] = tile
             up_w[dof:, at + q * 128 : at + q * 128 + 128] = tile[128:]
-        owns = [doubled(self_out[2 * p + u], wide) for u in range(2)]
+        owns = [doubled(self_ref[2 * p + u], wide) for u in range(2)]
         for base, halves in ((0, pair), (kinds_n // 2 * span, owns)):
             for side, lanes in enumerate(SIDES):
                 low_w[base + at : base + at + dof, lanes] = halves[0][side]
                 low_w[base + at + dof : base + at + dof + body, lanes] = halves[1][side][128:]
                 low_w[base + at + dof + body : base + at + span, lanes] = halves[1][side][:128]
-        for u in range(2):
-            for side, lanes in enumerate(SIDES):
-                found = jnp.sum(owns[u][side].astype(F32) * eyes[side], axis=0, keepdims=True)
-                diag_ref[2 * p + u : 2 * p + u + 1, lanes] = found
-    for copy in copies[2:]:
-        copy.wait()
 
 
 def pack_kernel(core_ref, diag_ref, *refs):
@@ -288,17 +295,22 @@
         yield from ((t, t), (t, t + 1), (t + 1, t + 1))
 
 
-def build(near, kind, mask, lhs, row, low_row, first, kinds_n):
-    depth = near[0][0].shape[0]
-    dtype = near[0][0].dtype
+DIRECTIONS = ((0, 1, 2), (3, 4, 5), (6,))
+
+
+def build(near, kind, mask, lhs, row, low_row, first, kinds_n, directions=DIRECTIONS):
+    depth = near[0][6].shape[0]
+    dtype = near[0][6].dtype
     zero = jnp.zeros((), dtype)
     at = 0
-    for ks in ((0, 1, 2), (3, 4, 5), (6,)):
+    for ks in directions:
         for t in range(0, kinds_n, 2):
             mixed = jnp.where(first, float(t), float(t + 1)).astype(dtype)
             for side, wanted in ((0, jnp.asarray(t, dtype)), (1, mixed), (0, jnp.asarray(t + 1, dtype))):
                 total = None
                 for k in ks:
+                    if near[side][k] is None:
+                        continue
                     if mask is None:
                         term = jnp.where(kind(k) == wanted, near[side][k], zero)
                     else:
@@ -311,21 +323,20 @@
                 at += 128
 
 
-def advance(window, own, halo, get_own, get, kinds, kinds_16, masks, up_w, low_w, lhs, first):
+def around(window, fetch, i, depth, has):
+    sides = []
+    for lanes in SIDES:
+        mine = fetch(i, lanes)
+        wide = mine.astype(F32)
+        above, below = (pltpu.roll(wide, by, 0).astype(mine.dtype) for by in (depth - 1, 1))
+        x0, y0, x1, y1 = (fetch(int(n), lanes) if has(int(n)) else None for n in window.neighbours[i])
+        sides.append([x0, y0, above, x1, y1, below, mine])
+    return sides
+
+
+def advance(window, own, halo, get_own, get, kinds, kinds_16, masks, up_w, low_w, lhs, first, has=lambda i: True):
     kinds_n = up_w.shape[1] // 192
     depth = first.shape[0]
-
-    def around(fetch, i):
-        table = window.neighbours[i]
-        sides = []
-        for lanes in SIDES:
-            mine = fetch(i, lanes)
-            wide = mine.astype(F32)
-            above, below = (pltpu.roll(wide, by, 0).astype(mine.dtype) for by in (depth - 1, 1))
-            x0, y0, x1, y1 = (fetch(int(n), lanes) for n in table)
-            sides.append([x0, y0, above, x1, y1, below, mine])
-        return sides
-
     n = up_w.shape[1]
 
     def product(start, stop):
@@ -336,14 +347,16 @@
 
     base = 2 * len(own) * depth
     for u, i in enumerate(own):
-        build(around(get_own, i), lambda k: kinds(i, k), None, lhs, u * depth, (len(own) + u) * depth, first, kinds_n)
+        near = around(window, get_own, i, depth, has)
+        build(near, lambda k: kinds(i, k), None, lhs, u * depth, (len(own) + u) * depth, first, kinds_n)
     accs = []
     if own:
         accs.append((own, True, product(0, base)))
     for group in batches(halo, 14):
         for u, i in enumerate(group):
             mask = (lambda n: masks(i, n)) if i in masks.at else None
-            build(around(get, i), lambda k: kinds_16(i, k), mask, lhs, base + u * depth, None, first, kinds_n)
+            near = around(window, get, i, depth, has)
+            build(near, lambda k: kinds_16(i, k), mask, lhs, base + u * depth, None, first, kinds_n)
         accs.append((group, False, product(base, base + len(group) * depth)))
         base += len(group) * depth
     for group, paired, acc in accs:
@@ -355,6 +368,33 @@
                 yield i, acc[u * depth : (u + 1) * depth]
 
 
+def remain(window, get_own, get, kinds, masks, up_w, low_w, lhs, first, part_ref):
+    n = up_w.shape[1]
+    kinds_n = n // 192
+    depth = first.shape[0]
+    own = window.count[0]
+    images = {i: part_ref[m] for m, i in enumerate(window.edges)}
+    base = 0
+    for k, columns in window.missing.items():
+        for u, i in enumerate(columns):
+            fetch = get_own if i < own else get
+            near = []
+            for lanes in SIDES:
+                near.append([None] * 6 + [fetch(i, lanes)])
+                near[-1][k] = fetch(int(window.neighbours[i][1 if k == 1 else 3]), lanes)
+            mask = None if i < own else lambda m, i=i: masks(i, m)
+            build(near, lambda k, i=i: kinds(i, k), mask, lhs, base + u * depth, None, first, kinds_n, ((k,),))
+        rows = lhs[base : base + len(columns) * depth, :n]
+        if k == 1:
+            acc = lax.dot_general(rows, up_w[...], (((1,), (1,)), ((), ())), preferred_element_type=F32)
+        else:
+            acc = jnp.dot(rows, low_w[:n], preferred_element_type=F32)
+        for u, i in enumerate(columns):
+            images[i] = images[i] + acc[u * depth : (u + 1) * depth]
+        base += len(columns) * depth
+    return images.items()
+
+
 def deliver(image, scale, first, keep_ref, send_ref, step, u):
     half = keep_ref.shape[2]
     for side, lanes in enumerate(SIDES):
@@ -368,7 +408,7 @@
 def ready_kernel(window, refs_in, len_y, body, *rest):
     pieces = rest[:refs_in]
     lo_ref, diag_ref, up_w, low_w = rest[refs_in : refs_in + 4]
-    ship, ship_own, kinds, masks, gain, scale, done, done_own, image, lhs = rest[refs_in + 4 :]
+    ship, ship_own, kinds, masks, gain, scale, done, done_own, image, part, lhs = rest[refs_in + 4 :]
     own = window.count[0]
     depth = ship.shape[1]
     first = lane_iota((depth, 128)) < body
@@ -399,10 +439,14 @@
         return get(i, slice(None), lanes).astype(F32)
 
     for i, value in advance(
-        window, [i for i in window.inside if i < own], [i for i in window.inside if i >= own], get_own,
+        window, [i for i in window.inside + window.edges if i < own],
+        [i for i in window.inside + window.edges if i >= own], get_own,
         lambda i, lanes: get(i, slice(None), lanes), lambda i, k: kinds[i, k], None,
-        Columns((masks, window.ready)), up_w, low_w, lhs, first,
+        Columns((masks, window.ready)), up_w, low_w, lhs, first, lambda i: i in window.early,
     ):
+        if i in window.edges:
+            part[window.edges.index(i)] = value
+            continue
         n = window.inside.index(i)
         moved = value * gain[window.early.index(i)]
         done[n] = moved.astype(BF16)
@@ -413,10 +457,12 @@
 
 def sweep_kernel(window, refs_in, len_y, body, *rest):
     pieces = rest[:refs_in]
-    (ship_in, own_a, kinds, masks_in, gain_in, scale, done, done_own, image, diag_ref, up_w, low_w) = rest[
-        refs_in : refs_in + 12
+    (ship_in, own_a, kinds, masks_in, gain_in, scale, done, done_own, image, part, diag_ref, up_w, low_w) = rest[
+        refs_in : refs_in + 13
     ]
-    (keep_ref, send_ref, ship_late, ship_a, ship_b, own_b, own_c, kinds_late, gain_late, lhs) = rest[refs_in + 12 :]
+    (keep_ref, send_ref, ship_late, ship_a, ship_b, own_b, own_c, kinds_late, gain_late, lhs, lhs_edge) = rest[
+        refs_in + 13 :
+    ]
     depth = ship_a.shape[1]
     own = window.count[0]
     targets = window.count[ITERS - 1]
@@ -449,7 +495,7 @@
     ]
     into = ((ship_a, own_b), (ship_b, own_c), (ship_a, own_b), None)
     for step in range(ITERS):
-        wanted = [i for i in range(window.count[ITERS - 1 - step]) if step or i not in window.inside]
+        wanted = [i for i in range(window.count[ITERS - 1 - step]) if step or i in window.late]
 
         def get(i, lanes):
             return ships[step](i, slice(None), lanes)
@@ -463,10 +509,14 @@
             for n, i in enumerate(window.inside):
                 if i < own:
                     deliver(image[n], scale[i], first, keep_ref, send_ref, step, i)
-        for i, value in advance(
+        images = advance(
             window, [i for i in wanted if i < own], [i for i in wanted if i >= own], get_own, get,
             lambda i, k: kinds[i, k], kinds_16, masks, up_w, low_w, lhs, first,
-        ):
+        )
+        if step == 0:
+            edges = remain(window, get_own, get, lambda i, k: kinds[i, k], masks, up_w, low_w, lhs_edge, first, part)
+            images = list(edges) + list(images)
+        for i, value in images:
             if i < own:
                 deliver(value, scale[i], first, keep_ref, send_ref, step, i)
             if into[step] is not None:
@@ -645,26 +695,33 @@
     theirs = tuple(shifted(a, "gz", 1) for a in given)
     plain = given + (block_owner,)
     span = kinds_n * dof
-    diag, up_w, low_w, *plain = pl.pallas_call(
+    given = (self_blocks, off_blocks, *plain)
+    diag, self_blocks, off_blocks, *plain = pl.pallas_call(
+        bring_kernel,
+        out_shape=(
+            jax.ShapeDtypeStruct((kinds_n, LANES), F32),
+            *(jax.ShapeDtypeStruct(a.shape, a.dtype) for a in given),
+        ),
+        in_specs=[ANY] * len(given),
+        out_specs=(VMEM,) * (1 + len(given)),
+        scratch_shapes=[pltpu.SemaphoreType.DMA((len(given),))],
+        compiler_params=small(8),
+        cost_estimate=pl.CostEstimate(flops=10**6, bytes_accessed=8 * 10**6, transcendentals=0),
+        name="bring",
+    )(*(pltpu.with_memory_space_constraint(a, pltpu.HBM) for a in given))
+    up_w, low_w = pl.pallas_call(
         tables_kernel,
         out_shape=(
-            jax.ShapeDtypeStruct((kinds_n, LANES), F32),
             jax.ShapeDtypeStruct((LANES, span), BF16),
             jax.ShapeDtypeStruct((2 * span, LANES), BF16),
-            *(jax.ShapeDtypeStruct(a.shape, a.dtype) for a in plain),
         ),
-        in_specs=[HBM] * (2 + len(plain)),
-        out_specs=(VMEM,) * (3 + len(plain)),
-        scratch_shapes=[
-            pltpu.VMEM((dof, 128), F32),
-            pltpu.SemaphoreType.DMA((2 + len(plain),)),
-            pltpu.VMEM(off_blocks.shape, BF16),
-            pltpu.VMEM(self_blocks.shape, BF16),
-        ],
+        in_specs=[VMEM] * 2,
+        out_specs=(VMEM,) * 2,
+        scratch_shapes=[pltpu.VMEM((dof, 128), F32)],
         compiler_params=small(8),
-        cost_estimate=pl.CostEstimate(flops=10**6, bytes_accessed=8 * 10**6, transcendentals=0),
+        cost_estimate=pl.CostEstimate(flops=10**8, bytes_accessed=8 * 10**6, transcendentals=0),
         name="tables",
-    )(*(pltpu.with_memory_space_constraint(a, pltpu.HBM) for a in (off_blocks, self_blocks, *plain)))
+    )(off_blocks, self_blocks)
     body_load, probe_load, density, kinds, block_owner = plain
     hi, lo = pl.pallas_call(
         pack_kernel,
@@ -717,10 +774,11 @@
             jax.ShapeDtypeStruct((inside, depth, LANES), BF16),
             jax.ShapeDtypeStruct((inside_own, depth, LANES), F32),
             jax.ShapeDtypeStruct((inside_own, depth, LANES), F32),
+            jax.ShapeDtypeStruct((len(window.edges), depth, LANES), F32),
         ),
         in_specs=[VMEM] * (len(from_x) + 4),
-        out_specs=(VMEM,) * 9,
-        scratch_shapes=[pltpu.VMEM((depth * (inside + inside_own), 3 * span), BF16)],
+        out_specs=(VMEM,) * 10,
+        scratch_shapes=[pltpu.VMEM((depth * (inside + len(window.edges) + own), 3 * span), BF16)],
         compiler_params=small(16),
         cost_estimate=pl.CostEstimate(flops=10**8, bytes_accessed=4 * 10**6, transcendentals=0),
         name="ready",
@@ -729,7 +787,7 @@
     keep, send = pl.pallas_call(
         functools.partial(sweep_kernel, window, len(late), len_y, dof - 128),
         out_shape=(jax.ShapeDtypeStruct((ITERS, cols, half, LANES), F32),) * 2,
-        in_specs=[VMEM] * (len(late) + 12),
+        in_specs=[VMEM] * (len(late) + 13),
         out_specs=(VMEM,) * 2,
         scratch_shapes=[
             pltpu.VMEM((len(window.late), depth, LANES), BF16),
@@ -740,6 +798,7 @@
             pltpu.VMEM((len(window.late), 7, depth, 128), BF16),
             pltpu.VMEM((len(window.late), depth, LANES), F32),
             pltpu.VMEM((rows, 3 * span), BF16),
+            pltpu.VMEM((depth * sum(len(c) for c in window.missing.values()), span), BF16),
         ],
         compiler_params=small(24),
         name="sweeps",

time: 44.3 us -> 43.3 us (0.977)
  waiting for transfers between devices: 8.88 us -> 7.81 us
    ppermute x10, waiting for transfers between devices: 8.88 us -> 7.81 us  [shifted(): lax.ppermute(array, axis, [((i + offset) % peers, i) for i in range(peers)])]
    pallas_call x1, Pallas kernels: 2.07 us -> 2.81 us  [by_field(): pl.pallas_call(functools.partial(ready_kernel, window, len(from_x), len_y...]
    pallas_call x1, Pallas kernels: 7.39 us -> 6.7 us  [by_field(): pl.pallas_call(functools.partial(sweep_kernel, window, len(late), len_y,...]
    pallas_call x1 -> x2, Pallas kernels: 1.64 us -> 1.65 us  [the longest x1 1.2 us: by_field(): pl.pallas_call(bring_kernel, out_shape=(jax.ShapeDtypeStruct((kinds_n, LA...]
  transfers between devices with their start and end apart: 10 -> 10, of which waited for: 6 -> 7; matrix products, arithmetic and copies ran while one was open for 0% -> 0% of each run, Pallas kernels for 8% -> 10%
where the time goes in v6:
time: 43.3 us; the launch traced here: 43.1 us
  Pallas kernels  13.3 us (31%)
  blocking collectives  10.7 us (25%)
  starting transfers between devices  10.6 us (24%)
  waiting for transfers between devices  7.81 us (18%)
  between operations  0.7 us (2%)
    all_to_all x1, blocking collectives, by_field(): message = lax.all_to_all(message, ('gx', 'gy', 'gz'), 0, 0, tiled=True)  10.7 us
    ppermute x10, starting transfers between devices, shifted(): lax.ppermute(array, axis, [((i + offset) % peers, i) for i in range(peers)])  10.6 us
    ppermute x10, waiting for transfers between devices, shifted(): lax.ppermute(array, axis, [((i + offset) % peers, i) for i in range(peers)])  7.81 us
    pallas_call x1, Pallas kernels, by_field(): pl.pallas_call(functools.partial(sweep_kernel, window, len(late), len_y,...  6.7 us
    pallas_call x1, Pallas kernels, by_field(): pl.pallas_call(functools.partial(ready_kernel, window, len(from_x), len_y...  2.81 us
    pallas_call x1, Pallas kernels, by_field(): pl.pallas_call(bring_kernel, out_shape=(jax.ShapeDtypeStruct((kinds_n, LA...  1.2 us
    pallas_call x1, Pallas kernels, by_field(): pl.pallas_call(finish_kernel, out_shape=(jax.ShapeDtypeStruct((cols, half...  1.05 us
  transfers between devices with their start and end apart: 10, of which 7 were waited for; matrix products, arithmetic and copies ran while one was open for 0% of the time, Pallas kernels for 10%

profile of v6, /device:TPU:0, one launch (start us, length us, event | category | flops | bytes accessed | tf_op | source)
XLA Modules:
  0.0 43.1 jit_solution(16775183100081428324)
XLA Ops:
  0.6 0.5 %collective-permute-start = (f32[2,4,8,192]{3,2,1,0:T(8,128)}, f32[2,4,8,192]{3,2,1,0:T(8,128)S(1)}, u32[]{:S(2)}, u32[]{:S(2)}) collective-permute-start(f32[2,4,8,192]{3,2,1,0:T(8,128)} %refs_2_.1), channel_id=1, source_target_pairs={{1,0},{0,1},{3,2},{2,3},{5,4},{4,5},{7,6},{6,7},{9,8},{8,9},{11,10... | collective-permute-start | bytes 147464 | tf_op jit(solution)/shard_map/ppermute | solution.py:678
  1.2 0.1 collective-permute-start.1
  1.2 0.4 %collective-permute-start.3 = (s32[2,7,4,8]{3,2,1,0:T(4,128)}, s32[2,7,4,8]{3,2,1,0:T(4,128)S(1)}, u32[]{:S(2)}, u32[]{:S(2)}) collective-permute-start(s32[2,7,4,8]{3,2,1,0:T(4,128)} %bitcast.5), channel_id=1, source_target_pairs={{1,0},{0,1},{3,2},{2,3},{5,4},{4,5},{7,6},{6,7},{9,8},{8,9},{11,10... | collective-permute-start | bytes 5384 | tf_op jit(solution)/shard_map/ppermute | solution.py:678
  1.7 0.1 collective-permute-start.2
  1.7 1.2 %bring.1 = (f32[4,256]{1,0:T(4,128)S(1)}, bf16[4,192,192]{2,1,0:T(8,128)(2,1)S(1)}, bf16[4,192,192]{2,1,0:T(8,128)(2,1)S(1)}, f32[2,4,8,192]{3,2,1,0:T(8,128)S(1...) custom-call(bf16[4,192,192]{2,1,0:T(8,128)(2,1)} %refs_0_.1, ...), custom_call_target="tpu_custom_call" | custom-call | flops 1000000 | bytes 8000000 | tf_op jit(solution)/shard_map/bring/pallas_call | solution.py:699
  2.9 0.1 collective-permute-done.2.refs_6_
  3.1 0.4 pack.1
  3.4 3.0 %collective-permute-start.6 = (bf16[13,16,128]{2,1,0:T(8,128)(2,1)S(1)}, bf16[13,16,128]{2,1,0:T(8,128)(2,1)S(1)}, u32[]{:S(2)}, u32[]{:S(2)}) collective-permute-start(bf16[13,16,128]{2,1,0:T(8,128)(2,1)S(1)} %get-tuple-element.41.refs_0_.rest_0_), channel_id=1, source_target_pairs={{24,0},{0,8},{8,16},{16,24},{25,1},{1,9},{9,17},{17,25},{26,2},{2,... | collective-permute-start | bytes 159752 | tf_op jit(solution)/shard_map/ppermute | solution.py:678
  6.4 2.6 %collective-permute-start.5 = (bf16[13,16,128]{2,1,0:T(8,128)(2,1)S(1)}, bf16[13,16,128]{2,1,0:T(8,128)(2,1)S(1)}, u32[]{:S(2)}, u32[]{:S(2)}) collective-permute-start(bf16[13,16,128]{2,1,0:T(8,128)(2,1)S(1)} %get-tuple-element.41.refs_0_.rest_0_), channel_id=1, source_target_pairs={{16,0},{24,8},{0,16},{8,24},{17,1},{25,9},{1,17},{9,25},{18,2},{26... | collective-permute-start | bytes 159752 | tf_op jit(solution)/shard_map/ppermute | solution.py:678
  9.0 1.3 %collective-permute-start.4 = (bf16[13,16,128]{2,1,0:T(8,128)(2,1)S(1)}, bf16[13,16,128]{2,1,0:T(8,128)(2,1)S(1)}, u32[]{:S(2)}, u32[]{:S(2)}) collective-permute-start(bf16[13,16,128]{2,1,0:T(8,128)(2,1)S(1)} %get-tuple-element.41.refs_0_.rest_0_), channel_id=1, source_target_pairs={{8,0},{16,8},{24,16},{0,24},{9,1},{17,9},{25,17},{1,25},{10,2},{18... | collective-permute-start | bytes 159752 | tf_op jit(solution)/shard_map/ppermute | solution.py:678
  10.3 0.3 collective-permute-done.6.refs_3_.rest_3_
  10.7 2.4 %collective-permute-done.5.refs_2_.rest_2_ = bf16[13,16,128]{2,1,0:T(8,128)(2,1)S(1)} collective-permute-done((bf16[13,16,128]{2,1,0:T(8,128)(2,1)S(1)}, bf16[13,16,128]{2,1,0:T(8,128)(2,1)S(1)}, u32[]{:S(2)}, u32[]{:S(2)}) %collective-permute-start.5) | collective-permute-done | bytes 53280 | tf_op jit(solution)/shard_map/ppermute | solution.py:678
  13.1 0.3 collective-permute-done.4.refs_1_.rest_1_
  13.4 0.1 assemble.1
  13.5 2.5 %collective-permute-start.7 = (bf16[33,16,128]{2,1,0:T(8,128)(2,1)S(1)}, bf16[33,16,128]{2,1,0:T(8,128)(2,1)S(1)}, u32[]{:S(2)}, u32[]{:S(2)}) collective-permute-start(bf16[33,16,128]{2,1,0:T(8,128)(2,1)S(1)} %get-tuple-element.42), channel_id=1, source_target_pairs={{2,0},{4,2},{6,4},{0,6},{3,1},{5,3},{7,5},{1,7},{10,8},{12,10},{14... | collective-permute-start | bytes 405512 | tf_op jit(solution)/shard_map/ppermute | solution.py:678
  16.0 0.4 %tables.1 = (bf16[256,768]{1,0:T(8,128)(2,1)S(1)}, bf16[1536,256]{1,0:T(8,128)(2,1)S(1)}) custom-call(bf16[4,192,192]{2,1,0:T(8,128)(2,1)S(1)} %get-tuple-element.45.off_ref, bf16[4,192,192]{2,1,0:T(8,128)(2,1)S(1)} %get-tuple-element.46.self_ref), custom_call_target="tpu_custom_call" | custom-call | flops 100000000 | bytes 8000000 | tf_op jit(solution)/shard_map/tables/pallas_call | solution.py:712
  16.5 2.8 %ready.1 = (bf16[32,16,256]{2,1,0:T(8,128)(2,1)S(1)}, f32[8,16,256]{2,1,0:T(8,128)S(1)}, f32[8,7,16,128]{3,2,1,0:T(8,128)S(1)}, bf16[24,42,16,128]{3,2,1,0:T(8,1...) custom-call(bf16[13,16,128]{2,1,0:T(8,128)(2,1)S(1)} %get-tuple-elem, ...), custom_call_target="tpu_custom_call" | custom-call | flops 100000000 | bytes 4000000 | tf_op jit(solution)/shard_map/ready/pallas_call | solution.py:765
  19.3 0.5 %collective-permute-done.7.rest_0_ = bf16[33,16,128]{2,1,0:T(8,128)(2,1)S(1)} collective-permute-done((bf16[33,16,128]{2,1,0:T(8,128)(2,1)S(1)}, bf16[33,16,128]{2,1,0:T(8,128)(2,1)S(1)}, u32[]{:S(2)}, u32[]{:S(2)}) %collective-permute-start.7) | collective-permute-done | bytes 135200 | tf_op jit(solution)/shard_map/ppermute | solution.py:678
  19.8 2.6 %collective-permute-done.8.rest_1_ = bf16[33,16,128]{2,1,0:T(8,128)(2,1)S(1)} collective-permute-done((bf16[33,16,128]{2,1,0:T(8,128)(2,1)S(1)}, bf16[33,16,128]{2,1,0:T(8,128)(2,1)S(1)}, u32[]{:S(2)}, u32[]{:S(2)}) %collective-permute-start.8) | collective-permute-done | bytes 135200 | tf_op jit(solution)/shard_map/ppermute | solution.py:678
  22.4 6.7 %sweeps.1 = (f32[4,8,8,256]{3,2,1,0:T(8,128)S(1)}, f32[4,8,8,256]{3,2,1,0:T(8,128)S(1)}) custom-call(bf16[33,16,128]{2,1,0:T(8,128)(2,1)S(1)} %collective-permute-done.7.rest_0_, bf16[33,16,128]{2,1,0:T(8,128)(2,1)S(1)} %collective-permute-done.8.rest_1_, bf16[32,16,256]{2,1,0:T(8,128)(2,1)S(1)} %get-tuple-element.49.rest_2_, ...), custom_call_target="tpu_custom_call" | custom-call | tf_op jit(solution)/shard_map/sweeps/pallas_call | solution.py:787
  29.2 1.5 %collective-permute-done.9.got = f32[4,8,8,256]{3,2,1,0:T(8,128)S(1)} collective-permute-done((f32[4,8,8,256]{3,2,1,0:T(8,128)S(1)}, f32[4,8,8,256]{3,2,1,0:T(8,128)S(1)}, u32[]{:S(2)}, u32[]{:S(2)}) %collective-permute-start.9) | collective-permute-done | bytes 262176 | tf_op jit(solution)/shard_map/ppermute | solution.py:678
  30.7 0.6 %moments.1 = (f32[32,2,128]{2,1,0:T(2,128)S(1)}, f32[4,8,8,256]{3,2,1,0:T(8,128)S(1)}, f32[4,8,8,256]{3,2,1,0:T(8,128)S(1)}) custom-call(s32[1]{0:T(128)} %bitcast.core_ref, f32[2,4,8,192]{3,2,1,0:T(8,128)S(1)} %get-tuple-element.35.refs_0_.body_ref, f32[2,4,8,192]{3,2,1,0:T(8,128)S(1)} %get-tuple-element.36.refs_1_.probe_ref, ...), custom_call_target="tpu_custom_call" | custom-call | tf_op jit(solution)/shard_map/moments/pallas_call | solution.py:808
  31.3 10.7 %all_to_all.5.message_ref = f32[32,2,128]{2,1,0:T(2,128)S(1)} all-to-all(f32[32,2,128]{2,1,0:T(2,128)S(1)} %get-tuple-element.61), channel_id=1, replica_groups=mesh['gx'=4,'gy'=4,'gz'=2] {'gx','gy','gz'}, dimensions={0} | all-to-all | bytes 65536 | tf_op jit(solution)/shard_map/all_to_all | solution.py:821
  42.0 1.1 %finish.1 = (f32[8,8,192]{2,1,0:T(8,128)}, f32[8,8,192]{2,1,0:T(8,128)}, f32[1,8]{1,0:T(1,128)}) custom-call(f32[32,2,128]{2,1,0:T(2,128)S(1)} %all_to_all.5.message_ref, f32[4,8,8,256]{3,2,1,0:T(8,128)S(1)} %get-tuple-element.62.pre_state_ref, f32[4,8,8,256]{3,2,1,0:T(8,128)S(1)} %get-tuple-element.63.pre_adjoint_ref), custom_call_target="tpu_custom_call" | custom-call | tf_op jit(solution)/shard_map/finish/pallas_call | solution.py:822
  (5 shorter events, 0.1 us)
Async XLA Ops:
  0.6 2.4 %collective-permute-start = (f32[2,4,8,192]{3,2,1,0:T(8,128)}, f32[2,4,8,192]{3,2,1,0:T(8,128)S(1)}, u32[]{:S(2)}, u32[]{:S(2)}) collective-permute-start(f32[2,4,8,192]{3,2,1,0:T(8,128)} %refs_2_.1), channel_id=1, source_target_pairs={{1,0},{0,1},{3,2},{2,3},{5,4},{4,5},{7,6},{6,7},{9,8},{8,9},{11,10... | collective-permute-start | bytes 147464 | tf_op jit(solution)/shard_map/ppermute | solution.py:678
  1.2 1.9 %collective-permute-start.1 = (f32[2,4,8,192]{3,2,1,0:T(8,128)}, f32[2,4,8,192]{3,2,1,0:T(8,128)S(1)}, u32[]{:S(2)}, u32[]{:S(2)}) collective-permute-start(f32[2,4,8,192]{3,2,1,0:T(8,128)} %refs_3_.1), channel_id=1, source_target_pairs={{1,0},{0,1},{3,2},{2,3},{5,4},{4,5},{7,6},{6,7},{9,8},{8,9},{11,10... | collective-permute-start | bytes 147464 | tf_op jit(solution)/shard_map/ppermute | solution.py:678
  1.2 1.8 %collective-permute-start.3 = (s32[2,7,4,8]{3,2,1,0:T(4,128)}, s32[2,7,4,8]{3,2,1,0:T(4,128)S(1)}, u32[]{:S(2)}, u32[]{:S(2)}) collective-permute-start(s32[2,7,4,8]{3,2,1,0:T(4,128)} %bitcast.5), channel_id=1, source_target_pairs={{1,0},{0,1},{3,2},{2,3},{5,4},{4,5},{7,6},{6,7},{9,8},{8,9},{11,10... | collective-permute-start | bytes 5384 | tf_op jit(solution)/shard_map/ppermute | solution.py:678
  1.7 1.4 %collective-permute-start.2 = (f32[2,4,8]{2,1,0:T(4,128)}, f32[2,4,8]{2,1,0:T(4,128)S(1)}, u32[]{:S(2)}, u32[]{:S(2)}) collective-permute-start(f32[2,4,8]{2,1,0:T(4,128)} %refs_4_.1), channel_id=1, source_target_pairs={{1,0},{0,1},{3,2},{2,3},{5,4},{4,5},{7,6},{6,7},{9,8},{8,9},{11,10... | collective-permute-start | bytes 776 | tf_op jit(solution)/shard_map/ppermute | solution.py:678
  3.4 7.2 %collective-permute-start.6 = (bf16[13,16,128]{2,1,0:T(8,128)(2,1)S(1)}, bf16[13,16,128]{2,1,0:T(8,128)(2,1)S(1)}, u32[]{:S(2)}, u32[]{:S(2)}) collective-permute-start(bf16[13,16,128]{2,1,0:T(8,128)(2,1)S(1)} %get-tuple-element.41.refs_0_.rest_0_), channel_id=1, source_target_pairs={{24,0},{0,8},{8,16},{16,24},{25,1},{1,9},{9,17},{17,25},{26,2},{2,... | collective-permute-start | bytes 159752 | tf_op jit(solution)/shard_map/ppermute | solution.py:678
  6.4 6.6 %collective-permute-start.5 = (bf16[13,16,128]{2,1,0:T(8,128)(2,1)S(1)}, bf16[13,16,128]{2,1,0:T(8,128)(2,1)S(1)}, u32[]{:S(2)}, u32[]{:S(2)}) collective-permute-start(bf16[13,16,128]{2,1,0:T(8,128)(2,1)S(1)} %get-tuple-element.41.refs_0_.rest_0_), channel_id=1, source_target_pairs={{16,0},{24,8},{0,16},{8,24},{17,1},{25,9},{1,17},{9,25},{18,2},{26... | collective-permute-start | bytes 159752 | tf_op jit(solution)/shard_map/ppermute | solution.py:678
  9.0 4.4 %collective-permute-start.4 = (bf16[13,16,128]{2,1,0:T(8,128)(2,1)S(1)}, bf16[13,16,128]{2,1,0:T(8,128)(2,1)S(1)}, u32[]{:S(2)}, u32[]{:S(2)}) collective-permute-start(bf16[13,16,128]{2,1,0:T(8,128)(2,1)S(1)} %get-tuple-element.41.refs_0_.rest_0_), channel_id=1, source_target_pairs={{8,0},{16,8},{24,16},{0,24},{9,1},{17,9},{25,17},{1,25},{10,2},{18... | collective-permute-start | bytes 159752 | tf_op jit(solution)/shard_map/ppermute | solution.py:678
  13.5 6.3 %collective-permute-start.7 = (bf16[33,16,128]{2,1,0:T(8,128)(2,1)S(1)}, bf16[33,16,128]{2,1,0:T(8,128)(2,1)S(1)}, u32[]{:S(2)}, u32[]{:S(2)}) collective-permute-start(bf16[33,16,128]{2,1,0:T(8,128)(2,1)S(1)} %get-tuple-element.42), channel_id=1, source_target_pairs={{2,0},{4,2},{6,4},{0,6},{3,1},{5,3},{7,5},{1,7},{10,8},{12,10},{14... | collective-permute-start | bytes 405512 | tf_op jit(solution)/shard_map/ppermute | solution.py:678
  16.0 6.4 %collective-permute-start.8 = (bf16[33,16,128]{2,1,0:T(8,128)(2,1)S(1)}, bf16[33,16,128]{2,1,0:T(8,128)(2,1)S(1)}, u32[]{:S(2)}, u32[]{:S(2)}) collective-permute-start(bf16[33,16,128]{2,1,0:T(8,128)(2,1)S(1)} %get-tuple-element.43), channel_id=1, source_target_pairs={{6,0},{0,2},{2,4},{4,6},{7,1},{1,3},{3,5},{5,7},{14,8},{8,10},{10,... | collective-permute-start | bytes 405512 | tf_op jit(solution)/shard_map/ppermute | solution.py:678
  29.1 1.6 %collective-permute-start.9 = (f32[4,8,8,256]{3,2,1,0:T(8,128)S(1)}, f32[4,8,8,256]{3,2,1,0:T(8,128)S(1)}, u32[]{:S(2)}, u32[]{:S(2)}) collective-permute-start(f32[4,8,8,256]{3,2,1,0:T(8,128)S(1)} %get-tuple-element.60), channel_id=1, source_target_pairs={{1,0},{0,1},{3,2},{2,3},{5,4},{4,5},{7,6},{6,7},{9,8},{8,9},{11,10... | collective-permute-start | bytes 786440 | tf_op jit(solution)/shard_map/ppermute | solution.py:678

commit v7 on v6

--- a/solution.py
+++ b/solution.py
@@ -86,13 +86,17 @@
         self.edges = [
             i for i, table in enumerate(self.neighbours) if i in early and not all(int(n) in early for n in table)
         ]
-        self.missing = {
-            k: [i for i in self.edges if int(self.neighbours[i][n]) not in early] for n, k in ((1, 1), (3, 4))
-        }
         self.ready = [i for i in self.early if self.count[0] <= i < self.count[ITERS - 1]]
         self.inside = [
             i for i, table in enumerate(self.neighbours) if i in self.early and all(n in self.early for n in table)
         ]
+        self.inner = [i for i in self.inside if i < self.count[ITERS - 2]]
+
+    def missing(self, columns, present):
+        ways = ((0, 0), (1, 1), (2, 3), (3, 4))
+        found = {k: [(i, int(self.neighbours[i][n])) for i in columns] for n, k in ways}
+        found = {k: [(i, n) for i, n in pairs if n not in present] for k, pairs in found.items()}
+        return {k: pairs for k, pairs in found.items() if pairs}
 
 
 def lane_iota(shape):
@@ -156,14 +160,14 @@
         at = p * span
         mixed = jnp.where(first, pair[0][1].astype(F32), pair[1][1].astype(F32)).astype(BF16)
         for q, tile in enumerate((pair[0][0], mixed, pair[1][0])):
-            up_w[:dof, at + q * 128 : at + q * 128 + 128] = tile
-            up_w[dof:, at + q * 128 : at + q * 128 + 128] = tile[128:]
+            up_w[3 * p + q, :dof] = tile
+            up_w[3 * p + q, dof:] = tile[128:]
         owns = [doubled(self_ref[2 * p + u], wide) for u in range(2)]
         for base, halves in ((0, pair), (kinds_n // 2 * span, owns)):
-            for side, lanes in enumerate(SIDES):
-                low_w[base + at : base + at + dof, lanes] = halves[0][side]
-                low_w[base + at + dof : base + at + dof + body, lanes] = halves[1][side][128:]
-                low_w[base + at + dof + body : base + at + span, lanes] = halves[1][side][:128]
+            for side in range(2):
+                low_w[side, base + at : base + at + dof] = halves[0][side]
+                low_w[side, base + at + dof : base + at + dof + body] = halves[1][side][128:]
+                low_w[side, base + at + dof + body : base + at + span] = halves[1][side][:128]
 
 
 def pack_kernel(core_ref, diag_ref, *refs):
@@ -263,7 +267,7 @@
     rest = jnp.where(first, turned, rest) if j % 2 else jnp.where(first, rest, turned)
     for side, lanes in enumerate(SIDES):
         x = rest if side else main
-        ship[n, :, lanes] = x.astype(BF16)
+        ship[n, side] = x.astype(BF16)
         if low is not None:
             y = low[:, lanes].astype(F32)
             if side:
@@ -317,82 +321,105 @@
                         term = near[side][k] * mask(k * 3 * kinds_n // 2 + at // 128 % (3 * kinds_n // 2))
                     total = term if total is None else total + term
                 hi = total.astype(BF16)
-                lhs[row : row + depth, at : at + 128] = hi
+                lhs[at // 128, row : row + depth] = hi
                 if low_row is not None:
-                    lhs[low_row : low_row + depth, at : at + 128] = (total - hi.astype(F32)).astype(BF16)
+                    lhs[at // 128, low_row : low_row + depth] = (total - hi.astype(F32)).astype(BF16)
                 at += 128
 
 
 def around(window, fetch, i, depth, has):
     sides = []
-    for lanes in SIDES:
-        mine = fetch(i, lanes)
+    for side in range(2):
+        mine = fetch(i, side)
         wide = mine.astype(F32)
         above, below = (pltpu.roll(wide, by, 0).astype(mine.dtype) for by in (depth - 1, 1))
-        x0, y0, x1, y1 = (fetch(int(n), lanes) if has(int(n)) else None for n in window.neighbours[i])
+        x0, y0, x1, y1 = (fetch(int(n), side) if has(int(n)) else None for n in window.neighbours[i])
         sides.append([x0, y0, above, x1, y1, below, mine])
     return sides
 
 
+def tiles(lhs, low, high, start, stop):
+    return jnp.concatenate([lhs[c, start:stop] for c in range(low, high)], axis=1)
+
+
+def by_up(rows, up_w):
+    table = jnp.concatenate([up_w[c] for c in range(up_w.shape[0])], axis=1)
+    return lax.dot_general(rows, table, (((1,), (1,)), ((), ())), preferred_element_type=F32)
+
+
 def advance(window, own, halo, get_own, get, kinds, kinds_16, masks, up_w, low_w, lhs, first, has=lambda i: True):
-    kinds_n = up_w.shape[1] // 192
+    kinds_n = up_w.shape[0] * 128 // 192
     depth = first.shape[0]
-    n = up_w.shape[1]
+    n = up_w.shape[0]
 
     def product(start, stop):
-        acc = lax.dot_general(
-            lhs[start:stop, :n], up_w[...], (((1,), (1,)), ((), ())), preferred_element_type=F32
-        )
-        return acc + jnp.dot(lhs[start:stop, n:], low_w[...], preferred_element_type=F32)
-
-    base = 2 * len(own) * depth
-    for u, i in enumerate(own):
-        near = around(window, get_own, i, depth, has)
-        build(near, lambda k: kinds(i, k), None, lhs, u * depth, (len(own) + u) * depth, first, kinds_n)
-    accs = []
-    if own:
-        accs.append((own, True, product(0, base)))
-    for group in batches(halo, 14):
-        for u, i in enumerate(group):
-            mask = (lambda n: masks(i, n)) if i in masks.at else None
-            near = around(window, get, i, depth, has)
-            build(near, lambda k: kinds_16(i, k), mask, lhs, base + u * depth, None, first, kinds_n)
-        accs.append((group, False, product(base, base + len(group) * depth)))
-        base += len(group) * depth
-    for group, paired, acc in accs:
+        acc = by_up(tiles(lhs, 0, n, start, stop), up_w)
+        low = jnp.concatenate([low_w[0], low_w[1]], axis=1)
+        return acc + jnp.dot(tiles(lhs, n, 3 * n, start, stop), low, preferred_element_type=F32)
+
+    def images(group, paired, acc):
         for u, i in enumerate(group):
             if paired:
-                n = len(group)
-                yield i, acc[u * depth : (u + 1) * depth] + acc[(n + u) * depth : (n + u + 1) * depth]
+                m = len(group)
+                yield i, acc[u * depth : (u + 1) * depth] + acc[(m + u) * depth : (m + u + 1) * depth]
             else:
                 yield i, acc[u * depth : (u + 1) * depth]
 
-
-def remain(window, get_own, get, kinds, masks, up_w, low_w, lhs, first, part_ref):
-    n = up_w.shape[1]
-    kinds_n = n // 192
+    base = 0
+    before = None
+    for paired, group in [(True, own)] * bool(own) + [(False, g) for g in batches(halo, 14)]:
+        stop = base + (1 + paired) * len(group) * depth
+        for u, i in enumerate(group):
+            at = base + u * depth
+            if paired:
+                near = around(window, get_own, i, depth, has)
+                build(near, lambda k: kinds(i, k), None, lhs, at, at + len(group) * depth, first, kinds_n)
+            else:
+                mask = (lambda n: masks(i, n)) if i in masks.at else None
+                near = around(window, get, i, depth, has)
+                build(near, lambda k: kinds_16(i, k), mask, lhs, at, None, first, kinds_n)
+        if before is not None:
+            yield from images(*before)
+        before = group, paired, product(base, stop)
+        base = stop
+    if before is not None:
+        yield from images(*before)
+
+
+def remain(window, columns, present, get_own, get, kinds, masks, up_w, low_w, lhs, first, part_ref, paired):
+    n = up_w.shape[0]
+    kinds_n = n * 128 // 192
     depth = first.shape[0]
     own = window.count[0]
-    images = {i: part_ref[m] for m, i in enumerate(window.edges)}
+    images = {i: part_ref[m] for m, i in enumerate(columns)}
     base = 0
-    for k, columns in window.missing.items():
-        for u, i in enumerate(columns):
+    for k, pairs in window.missing(columns, present).items():
+        rows = base
+        where = []
+        for i, there in pairs:
             fetch = get_own if i < own else get
             near = []
-            for lanes in SIDES:
-                near.append([None] * 6 + [fetch(i, lanes)])
-                near[-1][k] = fetch(int(window.neighbours[i][1 if k == 1 else 3]), lanes)
+            for side in range(2):
+                near.append([None] * 6 + [fetch(i, side)])
+                near[-1][k] = fetch(there, side)
+            low = rows + depth if i < own and paired else None
             mask = None if i < own else lambda m, i=i: masks(i, m)
-            build(near, lambda k, i=i: kinds(i, k), mask, lhs, base + u * depth, None, first, kinds_n, ((k,),))
-        rows = lhs[base : base + len(columns) * depth, :n]
-        if k == 1:
-            acc = lax.dot_general(rows, up_w[...], (((1,), (1,)), ((), ())), preferred_element_type=F32)
+            build(near, lambda k, i=i: kinds(i, k), mask, lhs, rows, low, first, kinds_n, ((k,),))
+            where.append((i, rows))
+            rows += depth
+            if low is not None:
+                where.append((i, low))
+                rows += depth
+        left = tiles(lhs, 0, n, base, rows)
+        if k < 3:
+            acc = by_up(left, up_w)
         else:
-            acc = jnp.dot(rows, low_w[:n], preferred_element_type=F32)
-        for u, i in enumerate(columns):
-            images[i] = images[i] + acc[u * depth : (u + 1) * depth]
-        base += len(columns) * depth
-    return images.items()
+            low = jnp.concatenate([low_w[0, : n * 128], low_w[1, : n * 128]], axis=1)
+            acc = jnp.dot(left, low, preferred_element_type=F32)
+        for i, row in where:
+            images[i] = images[i] + acc[row - base : row - base + depth]
+        base = rows
+    return list(images.items())
 
 
 def deliver(image, scale, first, keep_ref, send_ref, step, u):
@@ -408,9 +435,9 @@
 def ready_kernel(window, refs_in, len_y, body, *rest):
     pieces = rest[:refs_in]
     lo_ref, diag_ref, up_w, low_w = rest[refs_in : refs_in + 4]
-    ship, ship_own, kinds, masks, gain, scale, done, done_own, image, part, lhs = rest[refs_in + 4 :]
+    ship, ship_own, kinds, masks, gain, scale, done, done_own, image, part, part_2, lhs = rest[refs_in + 4 :]
     own = window.count[0]
-    depth = ship.shape[1]
+    depth = ship.shape[2]
     first = lane_iota((depth, 128)) < body
     kinds_n = diag_ref.shape[0]
     for n, i in enumerate(window.early):
@@ -433,15 +460,15 @@
                 gain[n, :, lanes] = g
     get = Columns((ship, window.early))
 
-    def get_own(i, lanes):
+    def get_own(i, side):
         if i < own:
-            return ship_own[i, :, lanes]
-        return get(i, slice(None), lanes).astype(F32)
+            return ship_own[i, :, SIDES[side]]
+        return get(i, side).astype(F32)
 
     for i, value in advance(
         window, [i for i in window.inside + window.edges if i < own],
         [i for i in window.inside + window.edges if i >= own], get_own,
-        lambda i, lanes: get(i, slice(None), lanes), lambda i, k: kinds[i, k], None,
+        get, lambda i, k: kinds[i, k], None,
         Columns((masks, window.ready)), up_w, low_w, lhs, first, lambda i: i in window.early,
     ):
         if i in window.edges:
@@ -449,21 +476,36 @@
             continue
         n = window.inside.index(i)
         moved = value * gain[window.early.index(i)]
-        done[n] = moved.astype(BF16)
+        for side, lanes in enumerate(SIDES):
+            done[n, side] = moved[:, lanes].astype(BF16)
         if i < own:
             done_own[n] = moved
             image[n] = value
+    get_2 = Columns((done, window.inside))
+    inside_own = [i for i in window.inside if i < own]
+
+    def get_own_2(i, side):
+        if i < own:
+            return done_own[inside_own.index(i), :, SIDES[side]]
+        return get_2(i, side).astype(F32)
+
+    for i, value in advance(
+        window, [i for i in window.inner if i < own], [i for i in window.inner if i >= own], get_own_2,
+        get_2, lambda i, k: kinds[i, k], None,
+        Columns((masks, window.ready)), up_w, low_w, lhs, first, lambda i: i in window.inside,
+    ):
+        part_2[window.inner.index(i)] = value
 
 
 def sweep_kernel(window, refs_in, len_y, body, *rest):
     pieces = rest[:refs_in]
-    (ship_in, own_a, kinds, masks_in, gain_in, scale, done, done_own, image, part, diag_ref, up_w, low_w) = rest[
-        refs_in : refs_in + 13
+    (ship_in, own_a, kinds, masks_in, gain_in, scale, done, done_own, image, part, part_2, diag_ref, up_w, low_w) = rest[
+        refs_in : refs_in + 14
     ]
     (keep_ref, send_ref, ship_late, ship_a, ship_b, own_b, own_c, kinds_late, gain_late, lhs, lhs_edge) = rest[
-        refs_in + 13 :
+        refs_in + 14 :
     ]
-    depth = ship_a.shape[1]
+    depth = ship_a.shape[2]
     own = window.count[0]
     targets = window.count[ITERS - 1]
     first = lane_iota((depth, 128)) < body
@@ -495,15 +537,18 @@
     ]
     into = ((ship_a, own_b), (ship_b, own_c), (ship_a, own_b), None)
     for step in range(ITERS):
-        wanted = [i for i in range(window.count[ITERS - 1 - step]) if step or i in window.late]
-
-        def get(i, lanes):
-            return ships[step](i, slice(None), lanes)
-
-        def get_own(i, lanes):
+        wanted = list(range(window.count[ITERS - 1 - step]))
+        if step == 0:
+            wanted = [i for i in wanted if i in window.late]
+        elif step == 1:
+            wanted = [i for i in wanted if i not in window.inner]
+
+        get = ships[step]
+
+        def get_own(i, side):
             if i < own:
-                return owns[step](i, slice(None), lanes)
-            return get(i, lanes).astype(F32)
+                return owns[step](i, slice(None), SIDES[side])
+            return get(i, side).astype(F32)
 
         if step == 0:
             for n, i in enumerate(window.inside):
@@ -513,15 +558,20 @@
             window, [i for i in wanted if i < own], [i for i in wanted if i >= own], get_own, get,
             lambda i, k: kinds[i, k], kinds_16, masks, up_w, low_w, lhs, first,
         )
-        if step == 0:
-            edges = remain(window, get_own, get, lambda i, k: kinds[i, k], masks, up_w, low_w, lhs_edge, first, part)
-            images = list(edges) + list(images)
+        if step < 2:
+            columns, present, known = ((window.edges, window.early, part), (window.inner, window.inside, part_2))[step]
+            parts = remain(
+                window, columns, present, get_own, get, lambda i, k: kinds[i, k], masks, up_w, low_w, lhs_edge, first,
+                known, step > 0,
+            )
+            images = parts + list(images)
         for i, value in images:
             if i < own:
                 deliver(value, scale[i], first, keep_ref, send_ref, step, i)
             if into[step] is not None:
                 moved = value * gain(i)
-                into[step][0][i] = moved.astype(BF16)
+                for side, lanes in enumerate(SIDES):
+                    into[step][0][i, side] = moved[:, lanes].astype(BF16)
                 if i < own:
                     into[step][1][i] = moved
 
@@ -712,8 +762,8 @@
     up_w, low_w = pl.pallas_call(
         tables_kernel,
         out_shape=(
-            jax.ShapeDtypeStruct((LANES, span), BF16),
-            jax.ShapeDtypeStruct((2 * span, LANES), BF16),
+            jax.ShapeDtypeStruct((span // 128, LANES, 128), BF16),
+            jax.ShapeDtypeStruct((2, 2 * span, 128), BF16),
         ),
         in_specs=[VMEM] * 2,
         out_specs=(VMEM,) * 2,
@@ -761,24 +811,28 @@
     targets = window.count[ITERS - 1]
     early = len(window.early)
     inside = len(window.inside)
+    edge_rows = sum(len(pairs) for pairs in window.missing(window.edges, window.early).values())
+    inner_rows = sum((1 + (i < own)) for pairs in window.missing(window.inner, window.inside).values() for i, _ in pairs)
+    edge_rows = max(edge_rows, inner_rows)
     inside_own = sum(i < own for i in window.inside)
     ready = pl.pallas_call(
         functools.partial(ready_kernel, window, len(from_x), len_y, dof - 128),
         out_shape=(
-            jax.ShapeDtypeStruct((early, depth, LANES), BF16),
+            jax.ShapeDtypeStruct((early, 2, depth, 128), BF16),
             jax.ShapeDtypeStruct((own, depth, LANES), F32),
             jax.ShapeDtypeStruct((own, 7, depth, 128), F32),
             jax.ShapeDtypeStruct((len(window.ready), 21 * kinds_n // 2, depth, 128), BF16),
             jax.ShapeDtypeStruct((early, depth, LANES), F32),
             jax.ShapeDtypeStruct((own, depth, 128), F32),
-            jax.ShapeDtypeStruct((inside, depth, LANES), BF16),
+            jax.ShapeDtypeStruct((inside, 2, depth, 128), BF16),
             jax.ShapeDtypeStruct((inside_own, depth, LANES), F32),
             jax.ShapeDtypeStruct((inside_own, depth, LANES), F32),
             jax.ShapeDtypeStruct((len(window.edges), depth, LANES), F32),
+            jax.ShapeDtypeStruct((len(window.inner), depth, LANES), F32),
         ),
         in_specs=[VMEM] * (len(from_x) + 4),
-        out_specs=(VMEM,) * 10,
-        scratch_shapes=[pltpu.VMEM((depth * (inside + len(window.edges) + own), 3 * span), BF16)],
+        out_specs=(VMEM,) * 11,
+        scratch_shapes=[pltpu.VMEM((3 * span // 128, depth * (inside + len(window.edges) + own), 128), BF16)],
         compiler_params=small(16),
         cost_estimate=pl.CostEstimate(flops=10**8, bytes_accessed=4 * 10**6, transcendentals=0),
         name="ready",
@@ -787,18 +841,18 @@
     keep, send = pl.pallas_call(
         functools.partial(sweep_kernel, window, len(late), len_y, dof - 128),
         out_shape=(jax.ShapeDtypeStruct((ITERS, cols, half, LANES), F32),) * 2,
-        in_specs=[VMEM] * (len(late) + 13),
+        in_specs=[VMEM] * (len(late) + 14),
         out_specs=(VMEM,) * 2,
         scratch_shapes=[
-            pltpu.VMEM((len(window.late), depth, LANES), BF16),
-            pltpu.VMEM((targets, depth, LANES), BF16),
-            pltpu.VMEM((targets, depth, LANES), BF16),
+            pltpu.VMEM((len(window.late), 2, depth, 128), BF16),
+            pltpu.VMEM((targets, 2, depth, 128), BF16),
+            pltpu.VMEM((targets, 2, depth, 128), BF16),
             pltpu.VMEM((own, depth, LANES), F32),
             pltpu.VMEM((own, depth, LANES), F32),
             pltpu.VMEM((len(window.late), 7, depth, 128), BF16),
             pltpu.VMEM((len(window.late), depth, LANES), F32),
-            pltpu.VMEM((rows, 3 * span), BF16),
-            pltpu.VMEM((depth * sum(len(c) for c in window.missing.values()), span), BF16),
+            pltpu.VMEM((3 * span // 128, rows, 128), BF16),
+            pltpu.VMEM((span // 128, depth * edge_rows, 128), BF16),
         ],
         compiler_params=small(24),
         name="sweeps",

time: 43.3 us -> 42.8 us (0.988)
  waiting for transfers between devices: 7.81 us -> 6.72 us
  Pallas kernels: 13.3 us -> 14 us
    pallas_call x1, Pallas kernels: 2.81 us -> 3.9 us  [by_field(): pl.pallas_call(functools.partial(ready_kernel, window, len(from_x), len_y...]
    ppermute x10, waiting for transfers between devices: 7.81 us -> 6.72 us  [shifted(): lax.ppermute(array, axis, [((i + offset) % peers, i) for i in range(peers)])]
  transfers between devices with their start and end apart: 10 -> 10, of which waited for: 7 -> 6; matrix products, arithmetic and copies ran while one was open for 0% -> 0% of each run, Pallas kernels for 10% -> 13%
where the time goes in v7:
time: 42.8 us; the launch traced here: 42.7 us
  Pallas kernels  14 us (33%)
  blocking collectives  10.7 us (25%)
  starting transfers between devices  10.6 us (25%)
  waiting for transfers between devices  6.72 us (16%)
  between operations  0.7 us (2%)
    all_to_all x1, blocking collectives, by_field(): message = lax.all_to_all(message, ('gx', 'gy', 'gz'), 0, 0, tiled=True)  10.7 us
    ppermute x10, starting transfers between devices, shifted(): lax.ppermute(array, axis, [((i + offset) % peers, i) for i in range(peers)])  10.6 us
    ppermute x10, waiting for transfers between devices, shifted(): lax.ppermute(array, axis, [((i + offset) % peers, i) for i in range(peers)])  6.72 us
    pallas_call x1, Pallas kernels, by_field(): pl.pallas_call(functools.partial(sweep_kernel, window, len(late), len_y,...  6.3 us
    pallas_call x1, Pallas kernels, by_field(): pl.pallas_call(functools.partial(ready_kernel, window, len(from_x), len_y...  3.9 us
    pallas_call x1, Pallas kernels, by_field(): pl.pallas_call(bring_kernel, out_shape=(jax.ShapeDtypeStruct((kinds_n, LA...  1.2 us
    pallas_call x1, Pallas kernels, by_field(): pl.pallas_call(finish_kernel, out_shape=(jax.ShapeDtypeStruct((cols, half...  1.05 us
  transfers between devices with their start and end apart: 10, of which 6 were waited for; matrix products, arithmetic and copies ran while one was open for 0% of the time, Pallas kernels for 13%

profile of v7, /device:TPU:0, one launch (start us, length us, event | category | flops | bytes accessed | tf_op | source)
XLA Modules:
  0.0 42.7 jit_solution(15384878042891909445)
XLA Ops:
  0.6 0.5 %collective-permute-start = (f32[2,4,8,192]{3,2,1,0:T(8,128)}, f32[2,4,8,192]{3,2,1,0:T(8,128)S(1)}, u32[]{:S(2)}, u32[]{:S(2)}) collective-permute-start(f32[2,4,8,192]{3,2,1,0:T(8,128)} %refs_2_.1), channel_id=1, source_target_pairs={{1,0},{0,1},{3,2},{2,3},{5,4},{4,5},{7,6},{6,7},{9,8},{8,9},{11,10... | collective-permute-start | bytes 147464 | tf_op jit(solution)/shard_map/ppermute | solution.py:728
  1.2 0.1 collective-permute-start.1
  1.2 0.4 %collective-permute-start.3 = (s32[2,7,4,8]{3,2,1,0:T(4,128)}, s32[2,7,4,8]{3,2,1,0:T(4,128)S(1)}, u32[]{:S(2)}, u32[]{:S(2)}) collective-permute-start(s32[2,7,4,8]{3,2,1,0:T(4,128)} %bitcast.5), channel_id=1, source_target_pairs={{1,0},{0,1},{3,2},{2,3},{5,4},{4,5},{7,6},{6,7},{9,8},{8,9},{11,10... | collective-permute-start | bytes 5384 | tf_op jit(solution)/shard_map/ppermute | solution.py:728
  1.7 0.1 collective-permute-start.2
  1.7 1.2 %bring.1 = (f32[4,256]{1,0:T(4,128)S(1)}, bf16[4,192,192]{2,1,0:T(8,128)(2,1)S(1)}, bf16[4,192,192]{2,1,0:T(8,128)(2,1)S(1)}, f32[2,4,8,192]{3,2,1,0:T(8,128)S(1...) custom-call(bf16[4,192,192]{2,1,0:T(8,128)(2,1)} %refs_0_.1, ...), custom_call_target="tpu_custom_call" | custom-call | flops 1000000 | bytes 8000000 | tf_op jit(solution)/shard_map/bring/pallas_call | solution.py:749
  2.9 0.1 collective-permute-done.2.refs_6_
  3.1 0.4 pack.1
  3.4 3.0 %collective-permute-start.6 = (bf16[13,16,128]{2,1,0:T(8,128)(2,1)S(1)}, bf16[13,16,128]{2,1,0:T(8,128)(2,1)S(1)}, u32[]{:S(2)}, u32[]{:S(2)}) collective-permute-start(bf16[13,16,128]{2,1,0:T(8,128)(2,1)S(1)} %get-tuple-element.42.refs_0_.rest_0_), channel_id=1, source_target_pairs={{24,0},{0,8},{8,16},{16,24},{25,1},{1,9},{9,17},{17,25},{26,2},{2,... | collective-permute-start | bytes 159752 | tf_op jit(solution)/shard_map/ppermute | solution.py:728
  6.4 2.6 %collective-permute-start.5 = (bf16[13,16,128]{2,1,0:T(8,128)(2,1)S(1)}, bf16[13,16,128]{2,1,0:T(8,128)(2,1)S(1)}, u32[]{:S(2)}, u32[]{:S(2)}) collective-permute-start(bf16[13,16,128]{2,1,0:T(8,128)(2,1)S(1)} %get-tuple-element.42.refs_0_.rest_0_), channel_id=1, source_target_pairs={{16,0},{24,8},{0,16},{8,24},{17,1},{25,9},{1,17},{9,25},{18,2},{26... | collective-permute-start | bytes 159752 | tf_op jit(solution)/shard_map/ppermute | solution.py:728
  9.0 1.3 %collective-permute-start.4 = (bf16[13,16,128]{2,1,0:T(8,128)(2,1)S(1)}, bf16[13,16,128]{2,1,0:T(8,128)(2,1)S(1)}, u32[]{:S(2)}, u32[]{:S(2)}) collective-permute-start(bf16[13,16,128]{2,1,0:T(8,128)(2,1)S(1)} %get-tuple-element.42.refs_0_.rest_0_), channel_id=1, source_target_pairs={{8,0},{16,8},{24,16},{0,24},{9,1},{17,9},{25,17},{1,25},{10,2},{18... | collective-permute-start | bytes 159752 | tf_op jit(solution)/shard_map/ppermute | solution.py:728
  10.3 0.3 collective-permute-done.6.refs_3_.rest_3_
  10.7 2.4 %collective-permute-done.5.refs_2_.rest_2_ = bf16[13,16,128]{2,1,0:T(8,128)(2,1)S(1)} collective-permute-done((bf16[13,16,128]{2,1,0:T(8,128)(2,1)S(1)}, bf16[13,16,128]{2,1,0:T(8,128)(2,1)S(1)}, u32[]{:S(2)}, u32[]{:S(2)}) %collective-permute-start.5) | collective-permute-done | bytes 53280 | tf_op jit(solution)/shard_map/ppermute | solution.py:728
  13.1 0.3 collective-permute-done.4.refs_1_.rest_1_
  13.4 0.1 assemble.1
  13.5 2.5 %collective-permute-start.7 = (bf16[33,16,128]{2,1,0:T(8,128)(2,1)S(1)}, bf16[33,16,128]{2,1,0:T(8,128)(2,1)S(1)}, u32[]{:S(2)}, u32[]{:S(2)}) collective-permute-start(bf16[33,16,128]{2,1,0:T(8,128)(2,1)S(1)} %get-tuple-element.43), channel_id=1, source_target_pairs={{2,0},{4,2},{6,4},{0,6},{3,1},{5,3},{7,5},{1,7},{10,8},{12,10},{14... | collective-permute-start | bytes 405512 | tf_op jit(solution)/shard_map/ppermute | solution.py:728
  16.0 0.4 %tables.1 = (bf16[6,256,128]{2,1,0:T(8,128)(2,1)S(1)}, bf16[2,1536,128]{2,1,0:T(8,128)(2,1)S(1)}) custom-call(bf16[4,192,192]{2,1,0:T(8,128)(2,1)S(1)} %get-tuple-element.46.off_ref, bf16[4,192,192]{2,1,0:T(8,128)(2,1)S(1)} %get-tuple-element.47.self_ref), custom_call_target="tpu_custom_call" | custom-call | flops 100000000 | bytes 8000000 | tf_op jit(solution)/shard_map/tables/pallas_call | solution.py:762
  16.5 3.9 %ready.1 = (bf16[32,2,16,128]{3,2,1,0:T(8,128)(2,1)S(1)}, f32[8,16,256]{2,1,0:T(8,128)S(1)}, f32[8,7,16,128]{3,2,1,0:T(8,128)S(1)}, bf16[24,42,16,128]{3,2,1,0:T...) custom-call(bf16[13,16,128]{2,1,0:T(8,128)(2,1)S(1)} %get-tuple-elem, ...), custom_call_target="tpu_custom_call" | custom-call | flops 100000000 | bytes 4000000 | tf_op jit(solution)/shard_map/ready/pallas_call | solution.py:818
  20.4 2.0 %collective-permute-done.8.rest_1_ = bf16[33,16,128]{2,1,0:T(8,128)(2,1)S(1)} collective-permute-done((bf16[33,16,128]{2,1,0:T(8,128)(2,1)S(1)}, bf16[33,16,128]{2,1,0:T(8,128)(2,1)S(1)}, u32[]{:S(2)}, u32[]{:S(2)}) %collective-permute-start.8) | collective-permute-done | bytes 135200 | tf_op jit(solution)/shard_map/ppermute | solution.py:728
  22.4 6.3 %sweeps.1 = (f32[4,8,8,256]{3,2,1,0:T(8,128)S(1)}, f32[4,8,8,256]{3,2,1,0:T(8,128)S(1)}) custom-call(bf16[33,16,128]{2,1,0:T(8,128)(2,1)S(1)} %collective-permute-done.7.rest_0_, bf16[33,16,128]{2,1,0:T(8,128)(2,1)S(1)} %collective-permute-done.8.rest_1_, bf16[32,2,16,128]{3,2,1,0:T(8,128)(2,1)S(1)} %get-tuple-element.50.rest_2_, ...), custom_call_target="tpu_custom_call" | custom-call | tf_op jit(solution)/shard_map/sweeps/pallas_call | solution.py:841
  28.7 0.1 collective-permute-start.9
  28.8 1.5 %collective-permute-done.9.got = f32[4,8,8,256]{3,2,1,0:T(8,128)S(1)} collective-permute-done((f32[4,8,8,256]{3,2,1,0:T(8,128)S(1)}, f32[4,8,8,256]{3,2,1,0:T(8,128)S(1)}, u32[]{:S(2)}, u32[]{:S(2)}) %collective-permute-start.9) | collective-permute-done | bytes 262176 | tf_op jit(solution)/shard_map/ppermute | solution.py:728
  30.3 0.6 %moments.1 = (f32[32,2,128]{2,1,0:T(2,128)S(1)}, f32[4,8,8,256]{3,2,1,0:T(8,128)S(1)}, f32[4,8,8,256]{3,2,1,0:T(8,128)S(1)}) custom-call(s32[1]{0:T(128)} %bitcast.core_ref, f32[2,4,8,192]{3,2,1,0:T(8,128)S(1)} %get-tuple-element.36.refs_0_.body_ref, f32[2,4,8,192]{3,2,1,0:T(8,128)S(1)} %get-tuple-element.37.refs_1_.probe_ref, ...), custom_call_target="tpu_custom_call" | custom-call | tf_op jit(solution)/shard_map/moments/pallas_call | solution.py:862
  30.9 10.7 %all_to_all.5.message_ref = f32[32,2,128]{2,1,0:T(2,128)S(1)} all-to-all(f32[32,2,128]{2,1,0:T(2,128)S(1)} %get-tuple-element.63), channel_id=1, replica_groups=mesh['gx'=4,'gy'=4,'gz'=2] {'gx','gy','gz'}, dimensions={0} | all-to-all | bytes 65536 | tf_op jit(solution)/shard_map/all_to_all | solution.py:875
  41.6 1.1 %finish.1 = (f32[8,8,192]{2,1,0:T(8,128)}, f32[8,8,192]{2,1,0:T(8,128)}, f32[1,8]{1,0:T(1,128)}) custom-call(f32[32,2,128]{2,1,0:T(2,128)S(1)} %all_to_all.5.message_ref, f32[4,8,8,256]{3,2,1,0:T(8,128)S(1)} %get-tuple-element.64.pre_state_ref, f32[4,8,8,256]{3,2,1,0:T(8,128)S(1)} %get-tuple-element.65.pre_adjoint_ref), custom_call_target="tpu_custom_call" | custom-call | tf_op jit(solution)/shard_map/finish/pallas_call | solution.py:876
  (5 shorter events, 0.0 us)
Async XLA Ops:
  0.6 2.4 %collective-permute-start = (f32[2,4,8,192]{3,2,1,0:T(8,128)}, f32[2,4,8,192]{3,2,1,0:T(8,128)S(1)}, u32[]{:S(2)}, u32[]{:S(2)}) collective-permute-start(f32[2,4,8,192]{3,2,1,0:T(8,128)} %refs_2_.1), channel_id=1, source_target_pairs={{1,0},{0,1},{3,2},{2,3},{5,4},{4,5},{7,6},{6,7},{9,8},{8,9},{11,10... | collective-permute-start | bytes 147464 | tf_op jit(solution)/shard_map/ppermute | solution.py:728
  1.2 1.9 %collective-permute-start.1 = (f32[2,4,8,192]{3,2,1,0:T(8,128)}, f32[2,4,8,192]{3,2,1,0:T(8,128)S(1)}, u32[]{:S(2)}, u32[]{:S(2)}) collective-permute-start(f32[2,4,8,192]{3,2,1,0:T(8,128)} %refs_3_.1), channel_id=1, source_target_pairs={{1,0},{0,1},{3,2},{2,3},{5,4},{4,5},{7,6},{6,7},{9,8},{8,9},{11,10... | collective-permute-start | bytes 147464 | tf_op jit(solution)/shard_map/ppermute | solution.py:728
  1.2 1.8 %collective-permute-start.3 = (s32[2,7,4,8]{3,2,1,0:T(4,128)}, s32[2,7,4,8]{3,2,1,0:T(4,128)S(1)}, u32[]{:S(2)}, u32[]{:S(2)}) collective-permute-start(s32[2,7,4,8]{3,2,1,0:T(4,128)} %bitcast.5), channel_id=1, source_target_pairs={{1,0},{0,1},{3,2},{2,3},{5,4},{4,5},{7,6},{6,7},{9,8},{8,9},{11,10... | collective-permute-start | bytes 5384 | tf_op jit(solution)/shard_map/ppermute | solution.py:728
  1.7 1.4 %collective-permute-start.2 = (f32[2,4,8]{2,1,0:T(4,128)}, f32[2,4,8]{2,1,0:T(4,128)S(1)}, u32[]{:S(2)}, u32[]{:S(2)}) collective-permute-start(f32[2,4,8]{2,1,0:T(4,128)} %refs_4_.1), channel_id=1, source_target_pairs={{1,0},{0,1},{3,2},{2,3},{5,4},{4,5},{7,6},{6,7},{9,8},{8,9},{11,10... | collective-permute-start | bytes 776 | tf_op jit(solution)/shard_map/ppermute | solution.py:728
  3.4 7.2 %collective-permute-start.6 = (bf16[13,16,128]{2,1,0:T(8,128)(2,1)S(1)}, bf16[13,16,128]{2,1,0:T(8,128)(2,1)S(1)}, u32[]{:S(2)}, u32[]{:S(2)}) collective-permute-start(bf16[13,16,128]{2,1,0:T(8,128)(2,1)S(1)} %get-tuple-element.42.refs_0_.rest_0_), channel_id=1, source_target_pairs={{24,0},{0,8},{8,16},{16,24},{25,1},{1,9},{9,17},{17,25},{26,2},{2,... | collective-permute-start | bytes 159752 | tf_op jit(solution)/shard_map/ppermute | solution.py:728
  6.4 6.6 %collective-permute-start.5 = (bf16[13,16,128]{2,1,0:T(8,128)(2,1)S(1)}, bf16[13,16,128]{2,1,0:T(8,128)(2,1)S(1)}, u32[]{:S(2)}, u32[]{:S(2)}) collective-permute-start(bf16[13,16,128]{2,1,0:T(8,128)(2,1)S(1)} %get-tuple-element.42.refs_0_.rest_0_), channel_id=1, source_target_pairs={{16,0},{24,8},{0,16},{8,24},{17,1},{25,9},{1,17},{9,25},{18,2},{26... | collective-permute-start | bytes 159752 | tf_op jit(solution)/shard_map/ppermute | solution.py:728
  9.0 4.4 %collective-permute-start.4 = (bf16[13,16,128]{2,1,0:T(8,128)(2,1)S(1)}, bf16[13,16,128]{2,1,0:T(8,128)(2,1)S(1)}, u32[]{:S(2)}, u32[]{:S(2)}) collective-permute-start(bf16[13,16,128]{2,1,0:T(8,128)(2,1)S(1)} %get-tuple-element.42.refs_0_.rest_0_), channel_id=1, source_target_pairs={{8,0},{16,8},{24,16},{0,24},{9,1},{17,9},{25,17},{1,25},{10,2},{18... | collective-permute-start | bytes 159752 | tf_op jit(solution)/shard_map/ppermute | solution.py:728
  13.5 6.9 %collective-permute-start.7 = (bf16[33,16,128]{2,1,0:T(8,128)(2,1)S(1)}, bf16[33,16,128]{2,1,0:T(8,128)(2,1)S(1)}, u32[]{:S(2)}, u32[]{:S(2)}) collective-permute-start(bf16[33,16,128]{2,1,0:T(8,128)(2,1)S(1)} %get-tuple-element.43), channel_id=1, source_target_pairs={{2,0},{4,2},{6,4},{0,6},{3,1},{5,3},{7,5},{1,7},{10,8},{12,10},{14... | collective-permute-start | bytes 405512 | tf_op jit(solution)/shard_map/ppermute | solution.py:728
  16.0 6.4 %collective-permute-start.8 = (bf16[33,16,128]{2,1,0:T(8,128)(2,1)S(1)}, bf16[33,16,128]{2,1,0:T(8,128)(2,1)S(1)}, u32[]{:S(2)}, u32[]{:S(2)}) collective-permute-start(bf16[33,16,128]{2,1,0:T(8,128)(2,1)S(1)} %get-tuple-element.44), channel_id=1, source_target_pairs={{6,0},{0,2},{2,4},{4,6},{7,1},{1,3},{3,5},{5,7},{14,8},{8,10},{10,... | collective-permute-start | bytes 405512 | tf_op jit(solution)/shard_map/ppermute | solution.py:728
  28.7 1.6 %collective-permute-start.9 = (f32[4,8,8,256]{3,2,1,0:T(8,128)S(1)}, f32[4,8,8,256]{3,2,1,0:T(8,128)S(1)}, u32[]{:S(2)}, u32[]{:S(2)}) collective-permute-start(f32[4,8,8,256]{3,2,1,0:T(8,128)S(1)} %get-tuple-element.62), channel_id=1, source_target_pairs={{1,0},{0,1},{3,2},{2,3},{5,4},{4,5},{7,6},{6,7},{9,8},{8,9},{11,10... | collective-permute-start | bytes 786440 | tf_op jit(solution)/shard_map/ppermute | solution.py:728

commit v8 on v7

--- a/solution.py
+++ b/solution.py
@@ -150,7 +150,7 @@
         copy.wait()
 
 
-def tables_kernel(off_ref, self_ref, up_w, low_w, wide):
+def tables_kernel(off_ref, self_ref, _, up_w, low_w, wide):
     kinds_n, dof, _ = off_ref.shape
     body = dof - 128
     span = 2 * dof
@@ -222,7 +222,7 @@
 
 
 def assemble_kernel(lines, count_in, body, *refs):
-    ins, outs = refs[:count_in], refs[count_in:]
+    ins, outs = refs[:count_in], refs[count_in + 1 :]
     for out, (columns, notes) in zip(outs, lines):
         for to in range(0, len(columns), 2):
             pair = None
@@ -759,19 +759,6 @@
         cost_estimate=pl.CostEstimate(flops=10**6, bytes_accessed=8 * 10**6, transcendentals=0),
         name="bring",
     )(*(pltpu.with_memory_space_constraint(a, pltpu.HBM) for a in given))
-    up_w, low_w = pl.pallas_call(
-        tables_kernel,
-        out_shape=(
-            jax.ShapeDtypeStruct((span // 128, LANES, 128), BF16),
-            jax.ShapeDtypeStruct((2, 2 * span, 128), BF16),
-        ),
-        in_specs=[VMEM] * 2,
-        out_specs=(VMEM,) * 2,
-        scratch_shapes=[pltpu.VMEM((dof, 128), F32)],
-        compiler_params=small(8),
-        cost_estimate=pl.CostEstimate(flops=10**8, bytes_accessed=8 * 10**6, transcendentals=0),
-        name="tables",
-    )(off_blocks, self_blocks)
     body_load, probe_load, density, kinds, block_owner = plain
     hi, lo = pl.pallas_call(
         pack_kernel,
@@ -785,6 +772,19 @@
         compiler_params=small(8),
         name="pack",
     )(core, diag, *plain[:4], *theirs)
+    up_w, low_w = pl.pallas_call(
+        tables_kernel,
+        out_shape=(
+            jax.ShapeDtypeStruct((span // 128, LANES, 128), BF16),
+            jax.ShapeDtypeStruct((2, 2 * span, 128), BF16),
+        ),
+        in_specs=[VMEM] * 2 + [ANY],
+        out_specs=(VMEM,) * 2,
+        scratch_shapes=[pltpu.VMEM((dof, 128), F32)],
+        compiler_params=small(8),
+        cost_estimate=pl.CostEstimate(flops=10**8, bytes_accessed=8 * 10**6, transcendentals=0),
+        name="tables",
+    )(off_blocks, self_blocks, lo)
     from_x = [hi] + [shifted(hi, "gx", o) for o in window.x_offsets]
     copies = []
     for o in window.y_offsets:
@@ -801,11 +801,11 @@
             jax.ShapeDtypeStruct((3 * ((len(columns) + 1) // 2) + len(notes), depth, 128), BF16)
             for columns, notes in copies
         ),
-        in_specs=[VMEM] * len(from_x),
+        in_specs=[VMEM] * len(from_x) + [ANY],
         out_specs=(VMEM,) * len(copies),
         compiler_params=small(8),
         name="assemble",
-    )(*from_x)
+    )(*from_x, up_w)
     late = [shifted(m, "gy", o) for m, o in zip(messages, window.y_offsets)]
     own = window.count[0]
     targets = window.count[ITERS - 1]

time: 42.8 us -> 42.9 us (level)
  transfers between devices with their start and end apart: 10 -> 10, of which waited for: 6 -> 5; matrix products, arithmetic and copies ran while one was open for 0% -> 0% of each run, Pallas kernels for 13% -> 13%
where the time goes in v8:
time: 42.9 us; the launch traced here: 42.7 us
  Pallas kernels  14 us (33%)
  blocking collectives  10.7 us (25%)
  starting transfers between devices  10.6 us (25%)
  waiting for transfers between devices  6.69 us (16%)
  between operations  0.71 us (2%)
    all_to_all x1, blocking collectives, by_field(): message = lax.all_to_all(message, ('gx', 'gy', 'gz'), 0, 0, tiled=True)  10.7 us
    ppermute x10, starting transfers between devices, shifted(): lax.ppermute(array, axis, [((i + offset) % peers, i) for i in range(peers)])  10.6 us
    ppermute x10, waiting for transfers between devices, shifted(): lax.ppermute(array, axis, [((i + offset) % peers, i) for i in range(peers)])  6.69 us
    pallas_call x1, Pallas kernels, by_field(): pl.pallas_call(functools.partial(sweep_kernel, window, len(late), len_y,...  6.33 us
    pallas_call x1, Pallas kernels, by_field(): pl.pallas_call(functools.partial(ready_kernel, window, len(from_x), len_y...  3.93 us
    pallas_call x1, Pallas kernels, by_field(): pl.pallas_call(bring_kernel, out_shape=(jax.ShapeDtypeStruct((kinds_n, LA...  1.2 us
    pallas_call x1, Pallas kernels, by_field(): pl.pallas_call(finish_kernel, out_shape=(jax.ShapeDtypeStruct((cols, half...  1.05 us
  transfers between devices with their start and end apart: 10, of which 5 were waited for; matrix products, arithmetic and copies ran while one was open for 0% of the time, Pallas kernels for 13%

profile of v8, /device:TPU:0, one launch (start us, length us, event | category | flops | bytes accessed | tf_op | source)
XLA Modules:
  0.0 42.7 jit_solution(11025292315157183216)
XLA Ops:
  0.6 0.5 %collective-permute-start = (f32[2,4,8,192]{3,2,1,0:T(8,128)}, f32[2,4,8,192]{3,2,1,0:T(8,128)S(1)}, u32[]{:S(2)}, u32[]{:S(2)}) collective-permute-start(f32[2,4,8,192]{3,2,1,0:T(8,128)} %refs_2_.1), channel_id=1, source_target_pairs={{1,0},{0,1},{3,2},{2,3},{5,4},{4,5},{7,6},{6,7},{9,8},{8,9},{11,10... | collective-permute-start | bytes 147464 | tf_op jit(solution)/shard_map/ppermute | solution.py:728
  1.2 0.1 collective-permute-start.1
  1.2 0.4 %collective-permute-start.3 = (s32[2,7,4,8]{3,2,1,0:T(4,128)}, s32[2,7,4,8]{3,2,1,0:T(4,128)S(1)}, u32[]{:S(2)}, u32[]{:S(2)}) collective-permute-start(s32[2,7,4,8]{3,2,1,0:T(4,128)} %bitcast.5), channel_id=1, source_target_pairs={{1,0},{0,1},{3,2},{2,3},{5,4},{4,5},{7,6},{6,7},{9,8},{8,9},{11,10... | collective-permute-start | bytes 5384 | tf_op jit(solution)/shard_map/ppermute | solution.py:728
  1.7 0.1 collective-permute-start.2
  1.7 1.2 %bring.1 = (f32[4,256]{1,0:T(4,128)S(1)}, bf16[4,192,192]{2,1,0:T(8,128)(2,1)S(1)}, bf16[4,192,192]{2,1,0:T(8,128)(2,1)S(1)}, f32[2,4,8,192]{3,2,1,0:T(8,128)S(1...) custom-call(bf16[4,192,192]{2,1,0:T(8,128)(2,1)} %refs_0_.1, ...), custom_call_target="tpu_custom_call" | custom-call | flops 1000000 | bytes 8000000 | tf_op jit(solution)/shard_map/bring/pallas_call | solution.py:749
  2.9 0.1 collective-permute-done.2.refs_6_
  3.0 0.0 collective-permute-done.3.refs_7_
  3.1 0.4 pack.1
  3.4 3.0 %collective-permute-start.6 = (bf16[13,16,128]{2,1,0:T(8,128)(2,1)S(1)}, bf16[13,16,128]{2,1,0:T(8,128)(2,1)S(1)}, u32[]{:S(2)}, u32[]{:S(2)}) collective-permute-start(bf16[13,16,128]{2,1,0:T(8,128)(2,1)S(1)} %get-tuple-element.42.refs_0_.rest_0_), channel_id=1, source_target_pairs={{24,0},{0,8},{8,16},{16,24},{25,1},{1,9},{9,17},{17,25},{26,2},{2,... | collective-permute-start | bytes 159752 | tf_op jit(solution)/shard_map/ppermute | solution.py:728
  6.4 2.6 %collective-permute-start.5 = (bf16[13,16,128]{2,1,0:T(8,128)(2,1)S(1)}, bf16[13,16,128]{2,1,0:T(8,128)(2,1)S(1)}, u32[]{:S(2)}, u32[]{:S(2)}) collective-permute-start(bf16[13,16,128]{2,1,0:T(8,128)(2,1)S(1)} %get-tuple-element.42.refs_0_.rest_0_), channel_id=1, source_target_pairs={{16,0},{24,8},{0,16},{8,24},{17,1},{25,9},{1,17},{9,25},{18,2},{26... | collective-permute-start | bytes 159752 | tf_op jit(solution)/shard_map/ppermute | solution.py:728
  9.0 1.3 %collective-permute-start.4 = (bf16[13,16,128]{2,1,0:T(8,128)(2,1)S(1)}, bf16[13,16,128]{2,1,0:T(8,128)(2,1)S(1)}, u32[]{:S(2)}, u32[]{:S(2)}) collective-permute-start(bf16[13,16,128]{2,1,0:T(8,128)(2,1)S(1)} %get-tuple-element.42.refs_0_.rest_0_), channel_id=1, source_target_pairs={{8,0},{16,8},{24,16},{0,24},{9,1},{17,9},{25,17},{1,25},{10,2},{18... | collective-permute-start | bytes 159752 | tf_op jit(solution)/shard_map/ppermute | solution.py:728
  10.3 0.4 %tables.1 = (bf16[6,256,128]{2,1,0:T(8,128)(2,1)S(1)}, bf16[2,1536,128]{2,1,0:T(8,128)(2,1)S(1)}) custom-call(bf16[4,192,192]{2,1,0:T(8,128)(2,1)S(1)} %get-tuple-element.43.off_ref, bf16[4,192,192]{2,1,0:T(8,128)(2,1)S(1)} %get-tuple-element.44.self_ref, bf16[8,16,256]{2,1,0:T(8,128)(2,1)S(1)} %get-tuple-element.45._.rest_4_), custom_call_target="tpu_custom_call" | custom-call | flops 100000000 | bytes 8000000 | tf_op jit(solution)/shard_map/tables/pallas_call | solution.py:775
  10.8 2.3 %collective-permute-done.5.refs_2_.rest_2_ = bf16[13,16,128]{2,1,0:T(8,128)(2,1)S(1)} collective-permute-done((bf16[13,16,128]{2,1,0:T(8,128)(2,1)S(1)}, bf16[13,16,128]{2,1,0:T(8,128)(2,1)S(1)}, u32[]{:S(2)}, u32[]{:S(2)}) %collective-permute-start.5) | collective-permute-done | bytes 53280 | tf_op jit(solution)/shard_map/ppermute | solution.py:728
  13.1 0.3 collective-permute-done.4.refs_1_.rest_1_
  13.4 0.1 assemble.1
  13.5 2.5 %collective-permute-start.7 = (bf16[33,16,128]{2,1,0:T(8,128)(2,1)S(1)}, bf16[33,16,128]{2,1,0:T(8,128)(2,1)S(1)}, u32[]{:S(2)}, u32[]{:S(2)}) collective-permute-start(bf16[33,16,128]{2,1,0:T(8,128)(2,1)S(1)} %get-tuple-element.47), channel_id=1, source_target_pairs={{2,0},{4,2},{6,4},{0,6},{3,1},{5,3},{7,5},{1,7},{10,8},{12,10},{14... | collective-permute-start | bytes 405512 | tf_op jit(solution)/shard_map/ppermute | solution.py:728
  16.0 3.9 %ready.1 = (bf16[32,2,16,128]{3,2,1,0:T(8,128)(2,1)S(1)}, f32[8,16,256]{2,1,0:T(8,128)S(1)}, f32[8,7,16,128]{3,2,1,0:T(8,128)S(1)}, bf16[24,42,16,128]{3,2,1,0:T...) custom-call(bf16[13,16,128]{2,1,0:T(8,128)(2,1)S(1)} %get-tuple-elem, ...), custom_call_target="tpu_custom_call" | custom-call | flops 100000000 | bytes 4000000 | tf_op jit(solution)/shard_map/ready/pallas_call | solution.py:818
  20.0 2.5 %collective-permute-done.8.rest_1_ = bf16[33,16,128]{2,1,0:T(8,128)(2,1)S(1)} collective-permute-done((bf16[33,16,128]{2,1,0:T(8,128)(2,1)S(1)}, bf16[33,16,128]{2,1,0:T(8,128)(2,1)S(1)}, u32[]{:S(2)}, u32[]{:S(2)}) %collective-permute-start.8) | collective-permute-done | bytes 135200 | tf_op jit(solution)/shard_map/ppermute | solution.py:728
  22.4 6.3 %sweeps.1 = (f32[4,8,8,256]{3,2,1,0:T(8,128)S(1)}, f32[4,8,8,256]{3,2,1,0:T(8,128)S(1)}) custom-call(bf16[33,16,128]{2,1,0:T(8,128)(2,1)S(1)} %collective-permute-done.7.rest_0_, bf16[33,16,128]{2,1,0:T(8,128)(2,1)S(1)} %collective-permute-done.8.rest_1_, bf16[32,2,16,128]{3,2,1,0:T(8,128)(2,1)S(1)} %get-tuple-element.50.rest_2_, ...), custom_call_target="tpu_custom_call" | custom-call | tf_op jit(solution)/shard_map/sweeps/pallas_call | solution.py:841
  28.8 0.1 collective-permute-start.9
  28.8 1.5 %collective-permute-done.9.got = f32[4,8,8,256]{3,2,1,0:T(8,128)S(1)} collective-permute-done((f32[4,8,8,256]{3,2,1,0:T(8,128)S(1)}, f32[4,8,8,256]{3,2,1,0:T(8,128)S(1)}, u32[]{:S(2)}, u32[]{:S(2)}) %collective-permute-start.9) | collective-permute-done | bytes 262176 | tf_op jit(solution)/shard_map/ppermute | solution.py:728
  30.4 0.6 %moments.1 = (f32[32,2,128]{2,1,0:T(2,128)S(1)}, f32[4,8,8,256]{3,2,1,0:T(8,128)S(1)}, f32[4,8,8,256]{3,2,1,0:T(8,128)S(1)}) custom-call(s32[1]{0:T(128)} %bitcast.core_ref, f32[2,4,8,192]{3,2,1,0:T(8,128)S(1)} %get-tuple-element.36.refs_0_.body_ref, f32[2,4,8,192]{3,2,1,0:T(8,128)S(1)} %get-tuple-element.37.refs_1_.probe_ref, ...), custom_call_target="tpu_custom_call" | custom-call | tf_op jit(solution)/shard_map/moments/pallas_call | solution.py:862
  31.0 10.7 %all_to_all.5.message_ref = f32[32,2,128]{2,1,0:T(2,128)S(1)} all-to-all(f32[32,2,128]{2,1,0:T(2,128)S(1)} %get-tuple-element.63), channel_id=1, replica_groups=mesh['gx'=4,'gy'=4,'gz'=2] {'gx','gy','gz'}, dimensions={0} | all-to-all | bytes 65536 | tf_op jit(solution)/shard_map/all_to_all | solution.py:875
  41.6 1.1 %finish.1 = (f32[8,8,192]{2,1,0:T(8,128)}, f32[8,8,192]{2,1,0:T(8,128)}, f32[1,8]{1,0:T(1,128)}) custom-call(f32[32,2,128]{2,1,0:T(2,128)S(1)} %all_to_all.5.message_ref, f32[4,8,8,256]{3,2,1,0:T(8,128)S(1)} %get-tuple-element.64.pre_state_ref, f32[4,8,8,256]{3,2,1,0:T(8,128)S(1)} %get-tuple-element.65.pre_adjoint_ref), custom_call_target="tpu_custom_call" | custom-call | tf_op jit(solution)/shard_map/finish/pallas_call | solution.py:876
  (5 shorter events, 0.0 us)
Async XLA Ops:
  0.6 2.4 %collective-permute-start = (f32[2,4,8,192]{3,2,1,0:T(8,128)}, f32[2,4,8,192]{3,2,1,0:T(8,128)S(1)}, u32[]{:S(2)}, u32[]{:S(2)}) collective-permute-start(f32[2,4,8,192]{3,2,1,0:T(8,128)} %refs_2_.1), channel_id=1, source_target_pairs={{1,0},{0,1},{3,2},{2,3},{5,4},{4,5},{7,6},{6,7},{9,8},{8,9},{11,10... | collective-permute-start | bytes 147464 | tf_op jit(solution)/shard_map/ppermute | solution.py:728
  1.2 1.9 %collective-permute-start.1 = (f32[2,4,8,192]{3,2,1,0:T(8,128)}, f32[2,4,8,192]{3,2,1,0:T(8,128)S(1)}, u32[]{:S(2)}, u32[]{:S(2)}) collective-permute-start(f32[2,4,8,192]{3,2,1,0:T(8,128)} %refs_3_.1), channel_id=1, source_target_pairs={{1,0},{0,1},{3,2},{2,3},{5,4},{4,5},{7,6},{6,7},{9,8},{8,9},{11,10... | collective-permute-start | bytes 147464 | tf_op jit(solution)/shard_map/ppermute | solution.py:728
  1.2 1.8 %collective-permute-start.3 = (s32[2,7,4,8]{3,2,1,0:T(4,128)}, s32[2,7,4,8]{3,2,1,0:T(4,128)S(1)}, u32[]{:S(2)}, u32[]{:S(2)}) collective-permute-start(s32[2,7,4,8]{3,2,1,0:T(4,128)} %bitcast.5), channel_id=1, source_target_pairs={{1,0},{0,1},{3,2},{2,3},{5,4},{4,5},{7,6},{6,7},{9,8},{8,9},{11,10... | collective-permute-start | bytes 5384 | tf_op jit(solution)/shard_map/ppermute | solution.py:728
  1.7 1.4 %collective-permute-start.2 = (f32[2,4,8]{2,1,0:T(4,128)}, f32[2,4,8]{2,1,0:T(4,128)S(1)}, u32[]{:S(2)}, u32[]{:S(2)}) collective-permute-start(f32[2,4,8]{2,1,0:T(4,128)} %refs_4_.1), channel_id=1, source_target_pairs={{1,0},{0,1},{3,2},{2,3},{5,4},{4,5},{7,6},{6,7},{9,8},{8,9},{11,10... | collective-permute-start | bytes 776 | tf_op jit(solution)/shard_map/ppermute | solution.py:728
  3.4 7.4 %collective-permute-start.6 = (bf16[13,16,128]{2,1,0:T(8,128)(2,1)S(1)}, bf16[13,16,128]{2,1,0:T(8,128)(2,1)S(1)}, u32[]{:S(2)}, u32[]{:S(2)}) collective-permute-start(bf16[13,16,128]{2,1,0:T(8,128)(2,1)S(1)} %get-tuple-element.42.refs_0_.rest_0_), channel_id=1, source_target_pairs={{24,0},{0,8},{8,16},{16,24},{25,1},{1,9},{9,17},{17,25},{26,2},{2,... | collective-permute-start | bytes 159752 | tf_op jit(solution)/shard_map/ppermute | solution.py:728
  6.4 6.6 %collective-permute-start.5 = (bf16[13,16,128]{2,1,0:T(8,128)(2,1)S(1)}, bf16[13,16,128]{2,1,0:T(8,128)(2,1)S(1)}, u32[]{:S(2)}, u32[]{:S(2)}) collective-permute-start(bf16[13,16,128]{2,1,0:T(8,128)(2,1)S(1)} %get-tuple-element.42.refs_0_.rest_0_), channel_id=1, source_target_pairs={{16,0},{24,8},{0,16},{8,24},{17,1},{25,9},{1,17},{9,25},{18,2},{26... | collective-permute-start | bytes 159752 | tf_op jit(solution)/shard_map/ppermute | solution.py:728
  9.0 4.4 %collective-permute-start.4 = (bf16[13,16,128]{2,1,0:T(8,128)(2,1)S(1)}, bf16[13,16,128]{2,1,0:T(8,128)(2,1)S(1)}, u32[]{:S(2)}, u32[]{:S(2)}) collective-permute-start(bf16[13,16,128]{2,1,0:T(8,128)(2,1)S(1)} %get-tuple-element.42.refs_0_.rest_0_), channel_id=1, source_target_pairs={{8,0},{16,8},{24,16},{0,24},{9,1},{17,9},{25,17},{1,25},{10,2},{18... | collective-permute-start | bytes 159752 | tf_op jit(solution)/shard_map/ppermute | solution.py:728
  13.5 6.4 %collective-permute-start.7 = (bf16[33,16,128]{2,1,0:T(8,128)(2,1)S(1)}, bf16[33,16,128]{2,1,0:T(8,128)(2,1)S(1)}, u32[]{:S(2)}, u32[]{:S(2)}) collective-permute-start(bf16[33,16,128]{2,1,0:T(8,128)(2,1)S(1)} %get-tuple-element.47), channel_id=1, source_target_pairs={{2,0},{4,2},{6,4},{0,6},{3,1},{5,3},{7,5},{1,7},{10,8},{12,10},{14... | collective-permute-start | bytes 405512 | tf_op jit(solution)/shard_map/ppermute | solution.py:728
  16.0 6.4 %collective-permute-start.8 = (bf16[33,16,128]{2,1,0:T(8,128)(2,1)S(1)}, bf16[33,16,128]{2,1,0:T(8,128)(2,1)S(1)}, u32[]{:S(2)}, u32[]{:S(2)}) collective-permute-start(bf16[33,16,128]{2,1,0:T(8,128)(2,1)S(1)} %get-tuple-element.48), channel_id=1, source_target_pairs={{6,0},{0,2},{2,4},{4,6},{7,1},{1,3},{3,5},{5,7},{14,8},{8,10},{10,... | collective-permute-start | bytes 405512 | tf_op jit(solution)/shard_map/ppermute | solution.py:728
  28.8 1.6 %collective-permute-start.9 = (f32[4,8,8,256]{3,2,1,0:T(8,128)S(1)}, f32[4,8,8,256]{3,2,1,0:T(8,128)S(1)}, u32[]{:S(2)}, u32[]{:S(2)}) collective-permute-start(f32[4,8,8,256]{3,2,1,0:T(8,128)S(1)} %get-tuple-element.62), channel_id=1, source_target_pairs={{1,0},{0,1},{3,2},{2,3},{5,4},{4,5},{7,6},{6,7},{9,8},{8,9},{11,10... | collective-permute-start | bytes 786440 | tf_op jit(solution)/shard_map/ppermute | solution.py:728

commit v9 on v7

--- a/solution.py
+++ b/solution.py
@@ -261,13 +261,14 @@
 
 
 def unpack(piece, j, low, n, first, body, ship, ship_own):
-    main = piece[3 * (j // 2) + j % 2].astype(F32)
+    main = piece[3 * (j // 2) + j % 2]
     rest = piece[3 * (j // 2) + 2].astype(F32)
     turned = pltpu.roll(rest, body, 1)
     rest = jnp.where(first, turned, rest) if j % 2 else jnp.where(first, rest, turned)
     for side, lanes in enumerate(SIDES):
         x = rest if side else main
         ship[n, side] = x.astype(BF16)
+        x = x.astype(F32)
         if low is not None:
             y = low[:, lanes].astype(F32)
             if side:

time: 42.8 us -> 42.8 us (level)
  no operation moved by 1% of the time
where the time goes in v9:
time: 42.8 us; the launch traced here: 42.6 us
  Pallas kernels  14 us (33%)
  blocking collectives  10.7 us (25%)
  starting transfers between devices  10.6 us (25%)
  waiting for transfers between devices  6.72 us (16%)
  between operations  0.7 us (2%)
    all_to_all x1, blocking collectives, by_field(): message = lax.all_to_all(message, ('gx', 'gy', 'gz'), 0, 0, tiled=True)  10.7 us
    ppermute x10, starting transfers between devices, shifted(): lax.ppermute(array, axis, [((i + offset) % peers, i) for i in range(peers)])  10.6 us
    ppermute x10, waiting for transfers between devices, shifted(): lax.ppermute(array, axis, [((i + offset) % peers, i) for i in range(peers)])  6.72 us
    pallas_call x1, Pallas kernels, by_field(): pl.pallas_call(functools.partial(sweep_kernel, window, len(late), len_y,...  6.27 us
    pallas_call x1, Pallas kernels, by_field(): pl.pallas_call(functools.partial(ready_kernel, window, len(from_x), len_y...  3.9 us
    pallas_call x1, Pallas kernels, by_field(): pl.pallas_call(bring_kernel, out_shape=(jax.ShapeDtypeStruct((kinds_n, LA...  1.2 us
    pallas_call x1, Pallas kernels, by_field(): pl.pallas_call(finish_kernel, out_shape=(jax.ShapeDtypeStruct((cols, half...  1.05 us
  transfers between devices with their start and end apart: 10, of which 6 were waited for; matrix products, arithmetic and copies ran while one was open for 0% of the time, Pallas kernels for 13%

profile of v9, /device:TPU:0, one launch (start us, length us, event | category | flops | bytes accessed | tf_op | source)
XLA Modules:
  0.0 42.6 jit_solution(9712052786959994096)
XLA Ops:
  0.6 0.5 %collective-permute-start = (f32[2,4,8,192]{3,2,1,0:T(8,128)}, f32[2,4,8,192]{3,2,1,0:T(8,128)S(1)}, u32[]{:S(2)}, u32[]{:S(2)}) collective-permute-start(f32[2,4,8,192]{3,2,1,0:T(8,128)} %refs_2_.1), channel_id=1, source_target_pairs={{1,0},{0,1},{3,2},{2,3},{5,4},{4,5},{7,6},{6,7},{9,8},{8,9},{11,10... | collective-permute-start | bytes 147464 | tf_op jit(solution)/shard_map/ppermute | solution.py:729
  1.2 0.1 collective-permute-start.1
  1.2 0.4 %collective-permute-start.3 = (s32[2,7,4,8]{3,2,1,0:T(4,128)}, s32[2,7,4,8]{3,2,1,0:T(4,128)S(1)}, u32[]{:S(2)}, u32[]{:S(2)}) collective-permute-start(s32[2,7,4,8]{3,2,1,0:T(4,128)} %bitcast.5), channel_id=1, source_target_pairs={{1,0},{0,1},{3,2},{2,3},{5,4},{4,5},{7,6},{6,7},{9,8},{8,9},{11,10... | collective-permute-start | bytes 5384 | tf_op jit(solution)/shard_map/ppermute | solution.py:729
  1.7 0.1 collective-permute-start.2
  1.7 1.2 %bring.1 = (f32[4,256]{1,0:T(4,128)S(1)}, bf16[4,192,192]{2,1,0:T(8,128)(2,1)S(1)}, bf16[4,192,192]{2,1,0:T(8,128)(2,1)S(1)}, f32[2,4,8,192]{3,2,1,0:T(8,128)S(1...) custom-call(bf16[4,192,192]{2,1,0:T(8,128)(2,1)} %refs_0_.1, ...), custom_call_target="tpu_custom_call" | custom-call | flops 1000000 | bytes 8000000 | tf_op jit(solution)/shard_map/bring/pallas_call | solution.py:750
  2.9 0.1 collective-permute-done.2.refs_6_
  3.1 0.4 pack.1
  3.4 3.0 %collective-permute-start.6 = (bf16[13,16,128]{2,1,0:T(8,128)(2,1)S(1)}, bf16[13,16,128]{2,1,0:T(8,128)(2,1)S(1)}, u32[]{:S(2)}, u32[]{:S(2)}) collective-permute-start(bf16[13,16,128]{2,1,0:T(8,128)(2,1)S(1)} %get-tuple-element.42.refs_0_.rest_0_), channel_id=1, source_target_pairs={{24,0},{0,8},{8,16},{16,24},{25,1},{1,9},{9,17},{17,25},{26,2},{2,... | collective-permute-start | bytes 159752 | tf_op jit(solution)/shard_map/ppermute | solution.py:729
  6.4 2.6 %collective-permute-start.5 = (bf16[13,16,128]{2,1,0:T(8,128)(2,1)S(1)}, bf16[13,16,128]{2,1,0:T(8,128)(2,1)S(1)}, u32[]{:S(2)}, u32[]{:S(2)}) collective-permute-start(bf16[13,16,128]{2,1,0:T(8,128)(2,1)S(1)} %get-tuple-element.42.refs_0_.rest_0_), channel_id=1, source_target_pairs={{16,0},{24,8},{0,16},{8,24},{17,1},{25,9},{1,17},{9,25},{18,2},{26... | collective-permute-start | bytes 159752 | tf_op jit(solution)/shard_map/ppermute | solution.py:729
  9.0 1.3 %collective-permute-start.4 = (bf16[13,16,128]{2,1,0:T(8,128)(2,1)S(1)}, bf16[13,16,128]{2,1,0:T(8,128)(2,1)S(1)}, u32[]{:S(2)}, u32[]{:S(2)}) collective-permute-start(bf16[13,16,128]{2,1,0:T(8,128)(2,1)S(1)} %get-tuple-element.42.refs_0_.rest_0_), channel_id=1, source_target_pairs={{8,0},{16,8},{24,16},{0,24},{9,1},{17,9},{25,17},{1,25},{10,2},{18... | collective-permute-start | bytes 159752 | tf_op jit(solution)/shard_map/ppermute | solution.py:729
  10.3 0.3 collective-permute-done.6.refs_3_.rest_3_
  10.7 2.4 %collective-permute-done.5.refs_2_.rest_2_ = bf16[13,16,128]{2,1,0:T(8,128)(2,1)S(1)} collective-permute-done((bf16[13,16,128]{2,1,0:T(8,128)(2,1)S(1)}, bf16[13,16,128]{2,1,0:T(8,128)(2,1)S(1)}, u32[]{:S(2)}, u32[]{:S(2)}) %collective-permute-start.5) | collective-permute-done | bytes 53280 | tf_op jit(solution)/shard_map/ppermute | solution.py:729
  13.1 0.3 collective-permute-done.4.refs_1_.rest_1_
  13.4 0.1 assemble.1
  13.5 2.5 %collective-permute-start.7 = (bf16[33,16,128]{2,1,0:T(8,128)(2,1)S(1)}, bf16[33,16,128]{2,1,0:T(8,128)(2,1)S(1)}, u32[]{:S(2)}, u32[]{:S(2)}) collective-permute-start(bf16[33,16,128]{2,1,0:T(8,128)(2,1)S(1)} %get-tuple-element.43), channel_id=1, source_target_pairs={{2,0},{4,2},{6,4},{0,6},{3,1},{5,3},{7,5},{1,7},{10,8},{12,10},{14... | collective-permute-start | bytes 405512 | tf_op jit(solution)/shard_map/ppermute | solution.py:729
  16.0 0.4 %tables.1 = (bf16[6,256,128]{2,1,0:T(8,128)(2,1)S(1)}, bf16[2,1536,128]{2,1,0:T(8,128)(2,1)S(1)}) custom-call(bf16[4,192,192]{2,1,0:T(8,128)(2,1)S(1)} %get-tuple-element.46.off_ref, bf16[4,192,192]{2,1,0:T(8,128)(2,1)S(1)} %get-tuple-element.47.self_ref), custom_call_target="tpu_custom_call" | custom-call | flops 100000000 | bytes 8000000 | tf_op jit(solution)/shard_map/tables/pallas_call | solution.py:763
  16.5 3.9 %ready.1 = (bf16[32,2,16,128]{3,2,1,0:T(8,128)(2,1)S(1)}, f32[8,16,256]{2,1,0:T(8,128)S(1)}, f32[8,7,16,128]{3,2,1,0:T(8,128)S(1)}, bf16[24,42,16,128]{3,2,1,0:T...) custom-call(bf16[13,16,128]{2,1,0:T(8,128)(2,1)S(1)} %get-tuple-elem, ...), custom_call_target="tpu_custom_call" | custom-call | flops 100000000 | bytes 4000000 | tf_op jit(solution)/shard_map/ready/pallas_call | solution.py:819
  20.4 2.1 %collective-permute-done.8.rest_1_ = bf16[33,16,128]{2,1,0:T(8,128)(2,1)S(1)} collective-permute-done((bf16[33,16,128]{2,1,0:T(8,128)(2,1)S(1)}, bf16[33,16,128]{2,1,0:T(8,128)(2,1)S(1)}, u32[]{:S(2)}, u32[]{:S(2)}) %collective-permute-start.8) | collective-permute-done | bytes 135200 | tf_op jit(solution)/shard_map/ppermute | solution.py:729
  22.4 6.3 %sweeps.1 = (f32[4,8,8,256]{3,2,1,0:T(8,128)S(1)}, f32[4,8,8,256]{3,2,1,0:T(8,128)S(1)}) custom-call(bf16[33,16,128]{2,1,0:T(8,128)(2,1)S(1)} %collective-permute-done.7.rest_0_, bf16[33,16,128]{2,1,0:T(8,128)(2,1)S(1)} %collective-permute-done.8.rest_1_, bf16[32,2,16,128]{3,2,1,0:T(8,128)(2,1)S(1)} %get-tuple-element.50.rest_2_, ...), custom_call_target="tpu_custom_call" | custom-call | tf_op jit(solution)/shard_map/sweeps/pallas_call | solution.py:842
  28.7 0.1 collective-permute-start.9
  28.8 1.5 %collective-permute-done.9.got = f32[4,8,8,256]{3,2,1,0:T(8,128)S(1)} collective-permute-done((f32[4,8,8,256]{3,2,1,0:T(8,128)S(1)}, f32[4,8,8,256]{3,2,1,0:T(8,128)S(1)}, u32[]{:S(2)}, u32[]{:S(2)}) %collective-permute-start.9) | collective-permute-done | bytes 262176 | tf_op jit(solution)/shard_map/ppermute | solution.py:729
  30.3 0.6 %moments.1 = (f32[32,2,128]{2,1,0:T(2,128)S(1)}, f32[4,8,8,256]{3,2,1,0:T(8,128)S(1)}, f32[4,8,8,256]{3,2,1,0:T(8,128)S(1)}) custom-call(s32[1]{0:T(128)} %bitcast.core_ref, f32[2,4,8,192]{3,2,1,0:T(8,128)S(1)} %get-tuple-element.36.refs_0_.body_ref, f32[2,4,8,192]{3,2,1,0:T(8,128)S(1)} %get-tuple-element.37.refs_1_.probe_ref, ...), custom_call_target="tpu_custom_call" | custom-call | tf_op jit(solution)/shard_map/moments/pallas_call | solution.py:863
  30.9 10.7 %all_to_all.5.message_ref = f32[32,2,128]{2,1,0:T(2,128)S(1)} all-to-all(f32[32,2,128]{2,1,0:T(2,128)S(1)} %get-tuple-element.63), channel_id=1, replica_groups=mesh['gx'=4,'gy'=4,'gz'=2] {'gx','gy','gz'}, dimensions={0} | all-to-all | bytes 65536 | tf_op jit(solution)/shard_map/all_to_all | solution.py:876
  41.6 1.1 %finish.1 = (f32[8,8,192]{2,1,0:T(8,128)}, f32[8,8,192]{2,1,0:T(8,128)}, f32[1,8]{1,0:T(1,128)}) custom-call(f32[32,2,128]{2,1,0:T(2,128)S(1)} %all_to_all.5.message_ref, f32[4,8,8,256]{3,2,1,0:T(8,128)S(1)} %get-tuple-element.64.pre_state_ref, f32[4,8,8,256]{3,2,1,0:T(8,128)S(1)} %get-tuple-element.65.pre_adjoint_ref), custom_call_target="tpu_custom_call" | custom-call | tf_op jit(solution)/shard_map/finish/pallas_call | solution.py:877
  (5 shorter events, 0.0 us)
Async XLA Ops:
  0.6 2.4 %collective-permute-start = (f32[2,4,8,192]{3,2,1,0:T(8,128)}, f32[2,4,8,192]{3,2,1,0:T(8,128)S(1)}, u32[]{:S(2)}, u32[]{:S(2)}) collective-permute-start(f32[2,4,8,192]{3,2,1,0:T(8,128)} %refs_2_.1), channel_id=1, source_target_pairs={{1,0},{0,1},{3,2},{2,3},{5,4},{4,5},{7,6},{6,7},{9,8},{8,9},{11,10... | collective-permute-start | bytes 147464 | tf_op jit(solution)/shard_map/ppermute | solution.py:729
  1.2 1.9 %collective-permute-start.1 = (f32[2,4,8,192]{3,2,1,0:T(8,128)}, f32[2,4,8,192]{3,2,1,0:T(8,128)S(1)}, u32[]{:S(2)}, u32[]{:S(2)}) collective-permute-start(f32[2,4,8,192]{3,2,1,0:T(8,128)} %refs_3_.1), channel_id=1, source_target_pairs={{1,0},{0,1},{3,2},{2,3},{5,4},{4,5},{7,6},{6,7},{9,8},{8,9},{11,10... | collective-permute-start | bytes 147464 | tf_op jit(solution)/shard_map/ppermute | solution.py:729
  1.2 1.8 %collective-permute-start.3 = (s32[2,7,4,8]{3,2,1,0:T(4,128)}, s32[2,7,4,8]{3,2,1,0:T(4,128)S(1)}, u32[]{:S(2)}, u32[]{:S(2)}) collective-permute-start(s32[2,7,4,8]{3,2,1,0:T(4,128)} %bitcast.5), channel_id=1, source_target_pairs={{1,0},{0,1},{3,2},{2,3},{5,4},{4,5},{7,6},{6,7},{9,8},{8,9},{11,10... | collective-permute-start | bytes 5384 | tf_op jit(solution)/shard_map/ppermute | solution.py:729
  1.7 1.4 %collective-permute-start.2 = (f32[2,4,8]{2,1,0:T(4,128)}, f32[2,4,8]{2,1,0:T(4,128)S(1)}, u32[]{:S(2)}, u32[]{:S(2)}) collective-permute-start(f32[2,4,8]{2,1,0:T(4,128)} %refs_4_.1), channel_id=1, source_target_pairs={{1,0},{0,1},{3,2},{2,3},{5,4},{4,5},{7,6},{6,7},{9,8},{8,9},{11,10... | collective-permute-start | bytes 776 | tf_op jit(solution)/shard_map/ppermute | solution.py:729
  3.4 7.2 %collective-permute-start.6 = (bf16[13,16,128]{2,1,0:T(8,128)(2,1)S(1)}, bf16[13,16,128]{2,1,0:T(8,128)(2,1)S(1)}, u32[]{:S(2)}, u32[]{:S(2)}) collective-permute-start(bf16[13,16,128]{2,1,0:T(8,128)(2,1)S(1)} %get-tuple-element.42.refs_0_.rest_0_), channel_id=1, source_target_pairs={{24,0},{0,8},{8,16},{16,24},{25,1},{1,9},{9,17},{17,25},{26,2},{2,... | collective-permute-start | bytes 159752 | tf_op jit(solution)/shard_map/ppermute | solution.py:729
  6.4 6.6 %collective-permute-start.5 = (bf16[13,16,128]{2,1,0:T(8,128)(2,1)S(1)}, bf16[13,16,128]{2,1,0:T(8,128)(2,1)S(1)}, u32[]{:S(2)}, u32[]{:S(2)}) collective-permute-start(bf16[13,16,128]{2,1,0:T(8,128)(2,1)S(1)} %get-tuple-element.42.refs_0_.rest_0_), channel_id=1, source_target_pairs={{16,0},{24,8},{0,16},{8,24},{17,1},{25,9},{1,17},{9,25},{18,2},{26... | collective-permute-start | bytes 159752 | tf_op jit(solution)/shard_map/ppermute | solution.py:729
  9.0 4.4 %collective-permute-start.4 = (bf16[13,16,128]{2,1,0:T(8,128)(2,1)S(1)}, bf16[13,16,128]{2,1,0:T(8,128)(2,1)S(1)}, u32[]{:S(2)}, u32[]{:S(2)}) collective-permute-start(bf16[13,16,128]{2,1,0:T(8,128)(2,1)S(1)} %get-tuple-element.42.refs_0_.rest_0_), channel_id=1, source_target_pairs={{8,0},{16,8},{24,16},{0,24},{9,1},{17,9},{25,17},{1,25},{10,2},{18... | collective-permute-start | bytes 159752 | tf_op jit(solution)/shard_map/ppermute | solution.py:729
  13.5 6.9 %collective-permute-start.7 = (bf16[33,16,128]{2,1,0:T(8,128)(2,1)S(1)}, bf16[33,16,128]{2,1,0:T(8,128)(2,1)S(1)}, u32[]{:S(2)}, u32[]{:S(2)}) collective-permute-start(bf16[33,16,128]{2,1,0:T(8,128)(2,1)S(1)} %get-tuple-element.43), channel_id=1, source_target_pairs={{2,0},{4,2},{6,4},{0,6},{3,1},{5,3},{7,5},{1,7},{10,8},{12,10},{14... | collective-permute-start | bytes 405512 | tf_op jit(solution)/shard_map/ppermute | solution.py:729
  16.0 6.4 %collective-permute-start.8 = (bf16[33,16,128]{2,1,0:T(8,128)(2,1)S(1)}, bf16[33,16,128]{2,1,0:T(8,128)(2,1)S(1)}, u32[]{:S(2)}, u32[]{:S(2)}) collective-permute-start(bf16[33,16,128]{2,1,0:T(8,128)(2,1)S(1)} %get-tuple-element.44), channel_id=1, source_target_pairs={{6,0},{0,2},{2,4},{4,6},{7,1},{1,3},{3,5},{5,7},{14,8},{8,10},{10,... | collective-permute-start | bytes 405512 | tf_op jit(solution)/shard_map/ppermute | solution.py:729
  28.7 1.6 %collective-permute-start.9 = (f32[4,8,8,256]{3,2,1,0:T(8,128)S(1)}, f32[4,8,8,256]{3,2,1,0:T(8,128)S(1)}, u32[]{:S(2)}, u32[]{:S(2)}) collective-permute-start(f32[4,8,8,256]{3,2,1,0:T(8,128)S(1)} %get-tuple-element.62), channel_id=1, source_target_pairs={{1,0},{0,1},{3,2},{2,3},{5,4},{4,5},{7,6},{6,7},{9,8},{8,9},{11,10... | collective-permute-start | bytes 786440 | tf_op jit(solution)/shard_map/ppermute | solution.py:729
